TPU v7x, 512 devices: a whole 4x4x16 slice. The times are simulated.
512 devices in a mesh: blk: 64 (over z_lo, x, core), uly: 8 (over z_hi, y).
Axes of the slice: x: 4, y: 4, z: 16 (z_hi: 2, z_lo: 8; z = z_hi * 8 + z_lo), core: 2. Of those that a mesh axis runs over, the one named last changes fastest.
Arguments:
- query_in: bfloat16 [64, 1024, 2048], P('blk', 'uly'), may hold values from -54 to 54
- key_in: bfloat16 [64, 1024, 2048], P('blk', 'uly'), may hold values from -54 to 54
- value_in: bfloat16 [64, 1024, 2048], P('blk', 'uly'), may hold values from -12 to 12
- velocity_grad: bfloat16 [64, 1024, 3072], P('blk', 'uly'), may hold values from -108 to 108
- velocity_gap: bfloat16 [64, 1024, 3072], P('blk', 'uly'), may hold values from -6 to 6
- query_gain: float32 [128], replicated, may hold values from 1 to 6.5
- key_gain: float32 [128], replicated, may hold values from 1 to 6.5
- out_proj: bfloat16 [2048, 3072], P('uly', 'blk'), may hold values from -0.125 to 0.125
Outputs:
- grad_query: bfloat16 [64, 1024, 2048], P('blk', 'uly')
- grad_key: bfloat16 [64, 1024, 2048], P('blk', 'uly')
- grad_value: bfloat16 [64, 1024, 2048], P('blk', 'uly')
- gain_grads: float32 [2, 128], replicated
- grad_out_proj: float32 [2048, 3072], P('uly', 'blk')
All inputs are finite; a program needn't handle non-finite values.
Results may differ from a plain program's by a relative error of at most 0.0095.
The roundings to bfloat16 on the way count: a program that leaves them out, or rounds other values in their place, can miss the bound.
Values may be sent and summed in bfloat16 or wider, within the bound.
No kernel may reach another device: no remote copies, remote signals or barrier semaphores. Data moves between devices by JAX's collectives and lax.ppermute only.
A program may use at most 64 MiB of HBM per device.

v0:
```python
import math

import jax
import jax.numpy as jnp
from jax import lax
from jax.sharding import PartitionSpec as P

kl_weight = 0.5
norm_eps = 1e-06


def head_norm(field, gain):
    mean_square = jnp.mean(field * field, axis=-1, keepdims=True)
    return field * lax.rsqrt(mean_square + norm_eps) * gain


def forward_head(inputs):
    queries, keyset, valueset = inputs
    score_scale = 1.0 / math.sqrt(queries.shape[-1])
    scores = jnp.dot(queries, keyset.T, preferred_element_type=jnp.float32) * score_scale
    row_top = jnp.max(scores, axis=1, keepdims=True)
    log_total = row_top + jnp.log(jnp.sum(jnp.exp(scores - row_top), axis=1, keepdims=True))
    weights = jnp.exp(scores - log_total).astype(jnp.bfloat16)
    outcome = jnp.dot(weights, valueset, preferred_element_type=jnp.float32).astype(jnp.bfloat16)
    return (outcome, log_total)


def backward_head(inputs):
    queries, keyset, valueset, outcome, d_outcome, log_total = inputs
    score_scale = 1.0 / math.sqrt(queries.shape[-1])
    scores = jnp.dot(queries, keyset.T, preferred_element_type=jnp.float32) * score_scale
    weights = jnp.exp(scores - log_total)
    delta_rows = jnp.sum(
        d_outcome.astype(jnp.float32) * outcome.astype(jnp.float32), axis=1, keepdims=True
    )
    d_weights = jnp.dot(d_outcome, valueset.T, preferred_element_type=jnp.float32)
    d_scores = (weights * (d_weights - delta_rows)).astype(jnp.bfloat16)
    d_query = jnp.dot(d_scores, keyset, preferred_element_type=jnp.float32) * score_scale
    d_key = jnp.dot(d_scores.T, queries, preferred_element_type=jnp.float32) * score_scale
    d_value = jnp.dot(weights.astype(jnp.bfloat16).T, d_outcome, preferred_element_type=jnp.float32)
    return (d_query, d_key, d_value)


def local(query_in, key_in, value_in, velocity_grad, velocity_gap, query_gain, key_gain, out_proj):
    groups = lax.axis_size("uly")
    tokens_here = query_in.shape[1]
    local_width = out_proj.shape[0]
    head_dim = query_gain.shape[0]
    heads_here = local_width // head_dim
    row_count = tokens_here * groups
    arrived = (
        lax.all_to_all(query_in[0], "uly", split_axis=1, concat_axis=0, tiled=True),
        lax.all_to_all(key_in[0], "uly", split_axis=1, concat_axis=0, tiled=True),
        lax.all_to_all(value_in[0], "uly", split_axis=1, concat_axis=0, tiled=True),
    )

    def heads_first(field):
        return jnp.transpose(field.reshape(row_count, heads_here, head_dim), (1, 0, 2))

    def tokens_first(field):
        return jnp.transpose(field, (1, 0, 2)).reshape(row_count, local_width)

    query_f = heads_first(arrived[0]).astype(jnp.float32)
    key_f = heads_first(arrived[1]).astype(jnp.float32)
    value_h = heads_first(arrived[2])
    query_n = head_norm(query_f, query_gain).astype(jnp.bfloat16)
    key_n = head_norm(key_f, key_gain).astype(jnp.bfloat16)
    outcome_h, log_total = lax.map(forward_head, (query_n, key_n, value_h))
    outcome_rows = tokens_first(outcome_h)
    d_velocity_own = (
        velocity_grad[0].astype(jnp.float32) + kl_weight * velocity_gap[0].astype(jnp.float32)
    ).astype(jnp.bfloat16)
    d_velocity = lax.all_gather(d_velocity_own, "uly", axis=0, tiled=True)
    d_outcome_sum = lax.dot_general(
        d_velocity,
        lax.all_gather(out_proj, "blk", axis=1, tiled=True),
        (((1,), (1,)), ((), ())),
        preferred_element_type=jnp.float32,
    )
    d_outcome_h = heads_first(d_outcome_sum.astype(jnp.bfloat16))
    weight_term = lax.dot_general(
        outcome_rows, d_velocity, (((0,), (0,)), ((), ())), preferred_element_type=jnp.float32
    )
    grad_out_proj = lax.psum_scatter(weight_term, "blk", scatter_dimension=1, tiled=True)
    d_query_n, d_key_n, d_value = lax.map(
        backward_head, (query_n, key_n, value_h, outcome_h, d_outcome_h, log_total)
    )
    unused_q, pull_query = jax.vjp(head_norm, query_f, query_gain)
    grad_query_f, query_gain_part = pull_query(d_query_n)
    unused_k, pull_key = jax.vjp(head_norm, key_f, key_gain)
    grad_key_f, key_gain_part = pull_key(d_key_n)
    gain_grads = lax.psum(jnp.stack([query_gain_part, key_gain_part]), ("blk", "uly"))
    grad_query_h = tokens_first(grad_query_f).astype(jnp.bfloat16)
    grad_key_h = tokens_first(grad_key_f).astype(jnp.bfloat16)
    grad_value_h = tokens_first(d_value).astype(jnp.bfloat16)
    grad_query, grad_key, grad_value = (
        lax.all_to_all(grad_query_h, "uly", split_axis=0, concat_axis=1, tiled=True),
        lax.all_to_all(grad_key_h, "uly", split_axis=0, concat_axis=1, tiled=True),
        lax.all_to_all(grad_value_h, "uly", split_axis=0, concat_axis=1, tiled=True),
    )
    return (grad_query[None], grad_key[None], grad_value[None], gain_grads, grad_out_proj)


def solution(mesh):
    placed = (
        P("blk", "uly", None),
        P("blk", "uly", None),
        P("blk", "uly", None),
        P("blk", "uly", None),
        P("blk", "uly", None),
        P(),
        P(),
        P("uly", "blk"),
    )
    return jax.shard_map(
        local,
        mesh=mesh,
        in_specs=placed,
        out_specs=(
            P("blk", "uly", None),
            P("blk", "uly", None),
            P("blk", "uly", None),
            P(),
            P("uly", "blk"),
        ),
        check_vma=False,
    )
```

profile of v0, /device:TPU:1, one launch (start us, length us, event | category | flops | bytes accessed | tf_op | source)
XLA Modules:
  0.0 909.6 jit_solution(15770008008258215739)
XLA Ops:
  8.0 2.6 add_convert_fusion
  10.6 2.0 copy.52
  12.6 18.3 %all-to-all-start = ((bf16[128,8,256]{0,2,1:T(8,128)(2,1)}), bf16[128,8,256]{0,2,1:T(8,128)(2,1)S(1)}, u32[]{:S(2)}, u32[]{:S(2)}) async-start(bf16[128,8,256]{0,2,1:T(8,128)(2,1)} %bitcast.14), calls=%async_computation | async-start | bytes 1048576 | tf_op jit(solution)/shard_map/all_to_all | solution.py:52
  30.9 1.0 copy.54
  31.9 16.6 %all-to-all-done = bf16[128,8,256]{0,2,1:T(8,128)(2,1)S(1)} async-done(((bf16[128,8,256]{0,2,1:T(8,128)(2,1)}), bf16[128,8,256]{0,2,1:T(8,128)(2,1)S(1)}, u32[]{:S(2)}, u32[]{:S(2)}) %all-to-all-start) | async-done | bytes 524320 | tf_op jit(solution)/shard_map/all_to_all | solution.py:52
  48.5 3.7 all-to-all-start.1
  52.2 1.0 copy.56
  53.2 15.2 %all-to-all-done.1 = bf16[128,8,256]{0,2,1:T(8,128)(2,1)S(1)} async-done(((bf16[128,8,256]{0,2,1:T(8,128)(2,1)}), bf16[128,8,256]{0,2,1:T(8,128)(2,1)S(1)}, u32[]{:S(2)}, u32[]{:S(2)}) %all-to-all-start.1) | async-done | bytes 524320 | tf_op jit(solution)/shard_map/all_to_all | solution.py:53
  68.4 10.6 %all-to-all-start.2 = ((bf16[128,8,256]{0,2,1:T(8,128)(2,1)}), bf16[128,8,256]{0,2,1:T(8,128)(2,1)}, u32[]{:S(2)}, u32[]{:S(2)}) async-start(bf16[128,8,256]{0,2,1:T(8,128)(2,1)} %bitcast.20), calls=%async_computation.2 | async-start | bytes 1048576 | tf_op jit(solution)/shard_map/all_to_all | solution.py:54
  80.6 1.6 copy.55
  82.2 1.4 reshape.143
  85.0 16.7 %all-to-all-done.2 = bf16[128,8,256]{0,2,1:T(8,128)(2,1)} async-done(((bf16[128,8,256]{0,2,1:T(8,128)(2,1)}), bf16[128,8,256]{0,2,1:T(8,128)(2,1)}, u32[]{:S(2)}, u32[]{:S(2)}) %all-to-all-start.2) | async-done | bytes 524320 | tf_op jit(solution)/shard_map/all_to_all | solution.py:54
  101.7 1.4 copy.57
  103.3 1.0 copy.60
  104.3 8.0 while.26
  105.8 2.5 fusion.88
  109.8 2.5 fusion.88
  112.3 1.2 copy.73
  113.6 76.3 %all-gather.4.cloned.1.call-done = bf16[256,3072]{0,1:T(8,128)(2,1)} async-done(((bf16[256,48]{0,1:T(8,128)(2,1)}), bf16[256,3072]{0,1:T(8,128)(2,1)}) %all-gather.4.cloned.1.call-update) | async-done | bytes 1572880 | tf_op jit(solution)/shard_map/all_gather | solution.py:76
  189.9 224.1 %all-gather.6.cloned.1.call-done = bf16[1,1024,3072]{2,1,0:T(8,128)(2,1)} async-done(((bf16[1,128,3072]{2,1,0:T(8,128)(2,1)}), bf16[1,1024,3072]{2,1,0:T(8,128)(2,1)}) %all-gather.6.cloned.1.call-update) | async-done | bytes 6291472 | tf_op jit(solution)/shard_map/all_gather | solution.py:73
  414.0 5.1 fusion.55
  419.3 7.0 fusion.51
  426.4 17.6 %while.27 = (s32[]{:T(128)}, f32[2,1024,128]{1,2,0:T(8,128)}, f32[2,1024,128]{1,2,0:T(8,128)}, bf16[2,1024,128]{2,1,0:T(8,128)(2,1)}, bf16[2,1024,128]{2,1,0:T(8...) while((s32[]{:T(128)}, f32[2,1024,128]{1,2,0:T(8,128)}, ...), condition=%wide.region_8.9_spmd, body=%wide.region_6.8_spmd.sunk | while | flops 1351351296 | bytes 27028616 | solution.py:85
  426.4 1.2 fusion.100
  428.3 1.9 fusion.103
  430.2 2.1 multiply_convert_fusion.4
  434.1 1.1 constant_dynamic-update-slice_fusion.6
  435.2 1.2 fusion.100
  437.1 1.9 fusion.103
  439.0 2.1 multiply_convert_fusion.4
  442.9 1.1 constant_dynamic-update-slice_fusion.6
  444.0 2.2 copy.69
  446.2 1.1 copy.89
  447.3 0.9 copy.70
  448.2 5.1 all-to-all-start.5
  453.3 1.6 multiply_reduce_fusion.2
  455.2 1.4 fusion.58
  456.7 0.9 copy.68
  457.6 11.7 %all-to-all-done.5 = bf16[8,128,256]{1,2,0:T(8,128)(2,1)} async-done(((bf16[8,128,256]{1,2,0:T(8,128)(2,1)}), bf16[8,128,256]{1,2,0:T(8,128)(2,1)}, u32[]{:S(2)}, u32[]{:S(2)}) %all-to-all-start.5) | async-done | bytes 524320 | tf_op jit(solution)/shard_map/all_to_all | solution.py:99
  469.3 3.5 all-to-all-start.4
  472.8 1.1 copy.87
  474.8 20.0 %all-to-all-done.4 = bf16[8,128,256]{1,2,0:T(8,128)(2,1)S(1)} async-done(((bf16[8,128,256]{1,2,0:T(8,128)(2,1)}), bf16[8,128,256]{1,2,0:T(8,128)(2,1)S(1)}, u32[]{:S(2)}, u32[]{:S(2)}) %all-to-all-start.4) | async-done | bytes 524320 | tf_op jit(solution)/shard_map/all_to_all | solution.py:98
  494.8 12.0 %all-to-all-start.3 = ((bf16[8,128,256]{1,2,0:T(8,128)(2,1)}), bf16[8,128,256]{1,2,0:T(8,128)(2,1)S(1)}, u32[]{:S(2)}, u32[]{:S(2)}) async-start(bf16[8,128,256]{1,2,0:T(8,128)(2,1)} %copy.66), calls=%async_computation.3 | async-start | bytes 1048576 | tf_op jit(solution)/shard_map/all_to_all | solution.py:97
  506.8 135.1 %psum.7 = f32[2,128]{1,0:T(2,128)} all-reduce(f32[2,128]{1,0:T(2,128)S(1)} %pad_maximum_fusion), channel_id=1, replica_groups=mesh['blk'=64,'uly'=8] {'blk','uly'}, use_global_device_ids=true, to_apply=%region_13.14 | all-reduce | flops 256 | bytes 2048 | tf_op jit(solution)/shard_map/psum | solution.py:92
  641.9 2.0 copy.76
  644.0 1.0 copy.75
  645.0 1.0 copy.74
  646.0 257.1 %reduce-scatter.2.cloned.1.call-done = f32[256,48]{0,1:T(8,128)} async-done(((f32[256,3072]{0,1:T(8,128)}), f32[256,48]{0,1:T(8,128)}) %reduce-scatter.2.cloned.1.call-update) | async-done | bytes 49168 | tf_op jit(solution)/shard_map/reduce_scatter | solution.py:84
  (72 shorter events, 13.5 us)
Async XLA Ops:
  7.2 23.7 %copy-start.6 = (bf16[1,128,2048]{2,1,0:T(8,128)(2,1)S(1)}, bf16[1,128,2048]{2,1,0:T(8,128)(2,1)}, u32[]{:S(2)}) copy-start(bf16[1,128,2048]{2,1,0:T(8,128)(2,1)} %param.13) | copy-start | bytes 1572868
  7.2 45.0 %copy-start.7 = (bf16[1,128,2048]{2,1,0:T(8,128)(2,1)S(1)}, bf16[1,128,2048]{2,1,0:T(8,128)(2,1)}, u32[]{:S(2)}) copy-start(bf16[1,128,2048]{2,1,0:T(8,128)(2,1)} %param.14) | copy-start | bytes 1572868
  7.2 182.7 %all-gather.4.cloned.1.call-start = ((), (), s32[]{:S(2)}) async-start(), calls=%async_computation.7 | async-start | bytes 1597440 | tf_op jit(solution)/shard_map/all_gather | solution.py:76
  7.9 406.1 %all-gather.6.cloned.1.call-start = ((), (), s32[]{:S(2)}) async-start(), calls=%async_computation.9 | async-start | bytes 7077888 | tf_op jit(solution)/shard_map/all_gather | solution.py:73
  12.6 35.9 %all-to-all-start = ((bf16[128,8,256]{0,2,1:T(8,128)(2,1)}), bf16[128,8,256]{0,2,1:T(8,128)(2,1)S(1)}, u32[]{:S(2)}, u32[]{:S(2)}) async-start(bf16[128,8,256]{0,2,1:T(8,128)(2,1)} %bitcast.14), calls=%async_computation | async-start | bytes 1048576 | tf_op jit(solution)/shard_map/all_to_all | solution.py:52
  48.5 19.9 %all-to-all-start.1 = ((bf16[128,8,256]{0,2,1:T(8,128)(2,1)}), bf16[128,8,256]{0,2,1:T(8,128)(2,1)S(1)}, u32[]{:S(2)}, u32[]{:S(2)}) async-start(bf16[128,8,256]{0,2,1:T(8,128)(2,1)} %bitcast.17), calls=%async_computation.1 | async-start | bytes 1048576 | tf_op jit(solution)/shard_map/all_to_all | solution.py:53
  53.2 26.9 %copy-start.8 = (f32[128]{0:T(128)S(1)}, f32[128]{0:T(128)}, u32[]{:S(2)}) copy-start(f32[128]{0:T(128)} %param.17) | copy-start | bytes 1540
  68.4 33.3 %all-to-all-start.2 = ((bf16[128,8,256]{0,2,1:T(8,128)(2,1)}), bf16[128,8,256]{0,2,1:T(8,128)(2,1)}, u32[]{:S(2)}, u32[]{:S(2)}) async-start(bf16[128,8,256]{0,2,1:T(8,128)(2,1)} %bitcast.20), calls=%async_computation.2 | async-start | bytes 1048576 | tf_op jit(solution)/shard_map/all_to_all | solution.py:54
  79.0 824.1 %reduce-scatter.2.cloned.1.call-start = ((), (), s32[]{:S(2)}) async-start(), calls=%async_computation.8 | async-start | bytes 3194880 | tf_op jit(solution)/shard_map/reduce_scatter | solution.py:84
  80.0 3.6 copy-start
  80.2 4.3 copy-start.9
  83.6 1.0 copy-start.2
  444.0 9.3 %copy-start.1 = (f32[1024,2,128]{0,2,1:T(8,128)S(1)}, f32[1024,2,128]{0,2,1:T(8,128)}, u32[]{:S(2)}) copy-start(f32[1024,2,128]{0,2,1:T(8,128)} %copy-done) | copy-start | bytes 3145732
  444.0 10.9 %copy-start.3 = (f32[1024,2,128]{0,2,1:T(8,128)S(1)}, f32[1024,2,128]{0,2,1:T(8,128)}, u32[]{:S(2)}) copy-start(f32[1024,2,128]{0,2,1:T(8,128)} %copy-done.2) | copy-start | bytes 3145732
  444.0 10.9 %copy-start.4 = (f32[2,1024,128]{1,2,0:T(8,128)S(1)}, f32[2,1024,128]{1,2,0:T(8,128)}, u32[]{:S(2)}) copy-start(f32[2,1024,128]{1,2,0:T(8,128)} %get-tuple-element.95) | copy-start | bytes 3145732
  448.2 21.1 %all-to-all-start.5 = ((bf16[8,128,256]{1,2,0:T(8,128)(2,1)}), bf16[8,128,256]{1,2,0:T(8,128)(2,1)}, u32[]{:S(2)}, u32[]{:S(2)}) async-start(bf16[8,128,256]{1,2,0:T(8,128)(2,1)} %copy.70), calls=%async_computation.5 | async-start | bytes 1048576 | tf_op jit(solution)/shard_map/all_to_all | solution.py:99
  453.3 1.9 copy-start.5
  469.3 25.5 %all-to-all-start.4 = ((bf16[8,128,256]{1,2,0:T(8,128)(2,1)}), bf16[8,128,256]{1,2,0:T(8,128)(2,1)S(1)}, u32[]{:S(2)}, u32[]{:S(2)}) async-start(bf16[8,128,256]{1,2,0:T(8,128)(2,1)} %copy.68), calls=%async_computation.4 | async-start | bytes 1048576 | tf_op jit(solution)/shard_map/all_to_all | solution.py:98
  494.8 150.2 %all-to-all-start.3 = ((bf16[8,128,256]{1,2,0:T(8,128)(2,1)}), bf16[8,128,256]{1,2,0:T(8,128)(2,1)S(1)}, u32[]{:S(2)}, u32[]{:S(2)}) async-start(bf16[8,128,256]{1,2,0:T(8,128)(2,1)} %copy.66), calls=%async_computation.3 | async-start | bytes 1048576 | tf_op jit(solution)/shard_map/all_to_all | solution.py:97
Sparse Core Ops, SparseCore 0:
  10.2 179.6 all-gather.3
  193.1 220.8 all-gather.5
  426.5 476.5 reduce-scatter.1
where the time goes:
time: 921 us; the launch traced here: 910 us
  waiting for transfers between devices  639 us (69%)
  blocking collectives  135 us (15%)
  starting transfers between devices  53.2 us (6%)
  matrix products  30.8 us (3%)
  local copies, waits for them, and re-layouts  27.6 us (3%)
  between operations  14 us (2%)
  other arithmetic  10.3 us (1%)
    reduce_scatter x1, waiting for transfers between devices, local(): lax.psum_scatter(weight_term, 'blk', scatter_dimension=1, tiled=True)  257 us
    all_gather x1, waiting for transfers between devices, local(): d_velocity = lax.all_gather(d_velocity_own, 'uly', axis=0, tiled=True)  224 us
    psum x1, blocking collectives, local(): lax.psum(jnp.stack([query_gain_part, key_gain_part]), ('blk', 'uly'))  135 us
    all_gather x1, waiting for transfers between devices, local(): lax.all_gather(out_proj, 'blk', axis=1, tiled=True)  76.3 us
    all_to_all x1, waiting for transfers between devices, local(): lax.all_to_all(grad_key_h, 'uly', split_axis=0, concat_axis=1, tiled=True)  20 us
  transfers between devices with their start and end apart: 9, of which 8 were waited for; matrix products, arithmetic and copies ran while one was open for 6% of the time, Pallas kernels for 0%

commit v1 on v0

v1 whole, which is shorter than its diff:
```python
import itertools
import math

import jax
import jax.numpy as jnp
import numpy as np
from jax import lax
from jax.experimental import pallas as pl
from jax.experimental.pallas import tpu as pltpu
from jax.sharding import Mesh, PartitionSpec as P

kl_weight = 0.5
norm_eps = 1e-06

AXES = ("zlo", "x", "core", "zhi", "y")
SIZES = (8, 4, 2, 2, 4)
PLACES = list(itertools.product(*map(range, SIZES)))
BF = jnp.bfloat16
F32 = jnp.float32
HEAD = 128
ROWS = 128
GROUPS = 8
SEQ = GROUPS * ROWS
TILE = 256
BLOCK = 96


def moved(field, where):
    number = lambda place: int(np.ravel_multi_index(place, SIZES))
    pairs = [(number(place), number(where(*place))) for place in PLACES]
    return lax.ppermute(field, AXES, pairs)


def clip_swap(l, x, c, h, y):
    return (l, x, h, c, y)


def clip_cross(l, x, c, h, y):
    return (l, x, 1 - h, c, y)


def core_swap(l, x, c, h, y):
    return (l, x, 1 - c, h, y)


def y_step(step):
    return lambda l, x, c, h, y: (l, x, c, h, (y + step) % 4)


def x_step(step):
    return lambda l, x, c, h, y: (l, x ^ step, c, h, y)


def whole():
    return pl.BlockSpec(memory_space=pltpu.VMEM)


def anywhere():
    return pl.BlockSpec(memory_space=pl.ANY)


def after(field, *earlier):
    return pl.pallas_call(
        lambda *refs: None,
        out_shape=jax.ShapeDtypeStruct(field.shape, field.dtype),
        in_specs=[anywhere()] * (1 + len(earlier)),
        out_specs=anywhere(),
        input_output_aliases={0: 0},
    )(field, *earlier)


def prepare_kernel(query_ref, key_ref, value_ref, first_ref, second_ref):
    for part, ref in enumerate((query_ref, key_ref, value_ref)):
        for group in range(GROUPS):
            at = group * 2 * HEAD
            first_ref[group, part] = ref[:, at : at + HEAD]
            second_ref[group, part] = ref[:, at + HEAD : at + 2 * HEAD]


def prepare(query, key, value):
    shape = jax.ShapeDtypeStruct((GROUPS, 3, ROWS, HEAD), BF)
    return pl.pallas_call(
        prepare_kernel,
        out_shape=(shape, shape),
        in_specs=[whole()] * 3,
        out_specs=(whole(), whole()),
    )(query, key, value)


def finish_kernel(first_ref, second_ref, query_ref, key_ref, value_ref):
    for part, ref in enumerate((query_ref, key_ref, value_ref)):
        for group in range(GROUPS):
            at = group * 2 * HEAD
            ref[:, at : at + HEAD] = first_ref[group, part]
            ref[:, at + HEAD : at + 2 * HEAD] = second_ref[group, part]


def finish(first, second):
    shape = jax.ShapeDtypeStruct((ROWS, GROUPS * 2 * HEAD), BF)
    return pl.pallas_call(
        finish_kernel,
        out_shape=(shape,) * 3,
        in_specs=[whole()] * 2,
        out_specs=(whole(),) * 3,
    )(first, second)


def project_kernel(order_ref, *refs):
    blocks, weight_ref, out_ref, rows, sems = refs[:8], refs[8], refs[9], refs[10], refs[11]
    copies = [
        pltpu.make_async_copy(blocks[i], rows.at[order_ref[i]], sems.at[i]) for i in range(8)
    ]
    for copy in copies:
        copy.start()
    for copy in copies:
        copy.wait()
    width = rows.shape[-1]
    out = jnp.dot(
        rows[...].reshape(SEQ, width), weight_ref[...], preferred_element_type=F32
    ).astype(BF)
    for head in range(2):
        out_ref[head] = out[:, head * HEAD : (head + 1) * HEAD]


def project(order, blocks, weight):
    width = weight.shape[0]
    return pl.pallas_call(
        project_kernel,
        out_shape=jax.ShapeDtypeStruct((2, SEQ, HEAD), BF),
        in_specs=[pl.BlockSpec(memory_space=pltpu.SMEM)] + [anywhere()] * 8 + [whole()],
        out_specs=whole(),
        scratch_shapes=[
            pltpu.VMEM((GROUPS, ROWS, width), BF),
            pltpu.SemaphoreType.DMA((8,)),
        ],
        compiler_params=pltpu.CompilerParams(vmem_limit_bytes=40 << 20),
        cost_estimate=pl.CostEstimate(
            flops=2 * SEQ * width * 256, bytes_accessed=10 << 20, transcendentals=0
        ),
    )(order, *blocks, weight)


def attend_kernel(head, in_ref, d_out_ref, gain_ref, out_ref, grad_ref, gain_out_ref, dk_acc, dv_acc, dq_all):
    scale = 1.0 / math.sqrt(HEAD)
    query_f = in_ref[:, 0].reshape(SEQ, HEAD).astype(F32)
    key_f = in_ref[:, 1].reshape(SEQ, HEAD).astype(F32)
    value = in_ref[:, 2].reshape(SEQ, HEAD)
    query_gain = gain_ref[0:1]
    key_gain = gain_ref[1:2]
    query_r = lax.rsqrt(jnp.mean(query_f * query_f, axis=-1, keepdims=True) + norm_eps)
    key_r = lax.rsqrt(jnp.mean(key_f * key_f, axis=-1, keepdims=True) + norm_eps)
    query_n = (query_f * query_r * query_gain).astype(BF)
    key_n = (key_f * key_r * key_gain).astype(BF)
    key_t = key_n.T
    value_t = value.T
    for tile in range(SEQ // TILE):
        at = tile * TILE
        query_tile = query_n[at : at + TILE]
        d_out = d_out_ref[head, at : at + TILE]
        d_out_t = d_out.T
        scores = jnp.dot(key_n, query_tile.T, preferred_element_type=F32) * scale
        top = jnp.max(scores, axis=0, keepdims=True)
        terms = jnp.exp(scores - top)
        weights = terms * (1.0 / jnp.sum(terms, axis=0, keepdims=True))
        weights_b = weights.astype(BF)
        out_t = jnp.dot(value_t, weights_b, preferred_element_type=F32).astype(BF)
        delta = jnp.sum(d_out_t.astype(F32) * out_t.astype(F32), axis=0, keepdims=True)
        d_weights = jnp.dot(value, d_out_t, preferred_element_type=F32)
        d_scores = (weights * (d_weights - delta)).astype(BF)
        d_query_t = jnp.dot(key_t, d_scores, preferred_element_type=F32)
        d_key = jnp.dot(d_scores, query_tile, preferred_element_type=F32)
        d_value = jnp.dot(weights_b, d_out, preferred_element_type=F32)
        out_ref[at : at + TILE] = out_t.T
        dq_all[at : at + TILE] = d_query_t.T
        if tile == 0:
            dk_acc[...] = d_key
            dv_acc[...] = d_value
        else:
            dk_acc[...] += d_key
            dv_acc[...] += d_value

    def pull(field, r, gain, cotangent):
        cotangent = cotangent * scale
        scaled = field * r
        gained = cotangent * gain
        inner = jnp.mean(gained * scaled, axis=-1, keepdims=True)
        grad = (r * (gained - scaled * inner)).astype(BF)
        return grad.reshape(GROUPS, ROWS, HEAD), jnp.sum(cotangent * scaled, axis=0, keepdims=True)

    grad_ref[:, 0], query_part = pull(query_f, query_r, query_gain, dq_all[...])
    grad_ref[:, 1], key_part = pull(key_f, key_r, key_gain, dk_acc[...])
    grad_ref[:, 2] = dv_acc[...].astype(BF).reshape(GROUPS, ROWS, HEAD)
    gain_out_ref[...] = jnp.concatenate([query_part, key_part], axis=0)


def attend(head, fields, d_out, gains):
    return pl.pallas_call(
        lambda *refs: attend_kernel(head, *refs),
        out_shape=(
            jax.ShapeDtypeStruct((SEQ, HEAD), BF),
            jax.ShapeDtypeStruct((GROUPS, 3, ROWS, HEAD), BF),
            jax.ShapeDtypeStruct((2, HEAD), F32),
        ),
        in_specs=[whole()] * 3,
        out_specs=(whole(),) * 3,
        scratch_shapes=[pltpu.VMEM((SEQ, HEAD), F32)] * 3,
        compiler_params=pltpu.CompilerParams(vmem_limit_bytes=40 << 20),
        cost_estimate=pl.CostEstimate(
            flops=12 * SEQ * SEQ * HEAD, bytes_accessed=2 << 20, transcendentals=SEQ * SEQ
        ),
    )(fields, d_out, gains)


def pair_rows(row):
    high = row.astype(BF)
    low = (row - high.astype(F32)).astype(BF)
    return jnp.concatenate([high, low, jnp.zeros((14, row.shape[1]), BF)], axis=0)


def weigh_kernel(order_ref, *refs):
    blocks = refs[:8]
    first_ref, second_ref, gain_first, gain_second, out_ref, rows, sems = refs[8:]
    copies = [
        pltpu.make_async_copy(blocks[i], rows.at[order_ref[i]], sems.at[i]) for i in range(8)
    ]
    for copy in copies:
        copy.start()
    for copy in copies:
        copy.wait()
    step = 8 * BLOCK
    for head, ref in enumerate((first_ref, second_ref)):
        out_t = ref[...].T
        for part in range(rows.shape[-1] // step):
            columns = rows[:, :, part * step : (part + 1) * step].reshape(SEQ, step)
            term = jnp.dot(out_t, columns, preferred_element_type=F32).T.astype(BF)
            for i in range(8):
                out_ref[i % 4, 2 * part + i // 4, 0:BLOCK, head * HEAD : (head + 1) * HEAD] = term[
                    i * BLOCK : (i + 1) * BLOCK
                ]
    gains = gain_first[...] + gain_second[...]
    tail = pair_rows(jnp.concatenate([gains[0:1], gains[1:2]], axis=1))
    for i in range(4):
        for j in range(8):
            out_ref[i, j, BLOCK : BLOCK + 16] = tail


def weigh(order, blocks, outs, gain_parts):
    width = blocks[0].shape[-1]
    return pl.pallas_call(
        weigh_kernel,
        out_shape=jax.ShapeDtypeStruct((4, 8, BLOCK + 16, 2 * HEAD), BF),
        in_specs=[pl.BlockSpec(memory_space=pltpu.SMEM)] + [anywhere()] * 8 + [whole()] * 4,
        out_specs=whole(),
        scratch_shapes=[
            pltpu.VMEM((GROUPS, ROWS, width), BF),
            pltpu.SemaphoreType.DMA((8,)),
        ],
        compiler_params=pltpu.CompilerParams(vmem_limit_bytes=40 << 20),
        cost_estimate=pl.CostEstimate(
            flops=2 * SEQ * width * 256, bytes_accessed=10 << 20, transcendentals=0
        ),
    )(order, *blocks, *outs, *gain_parts)


def first_sum_kernel(in_ref, out_ref):
    for j in range(8):
        total = sum(in_ref[i, j].astype(F32) for i in range(4))
        out_ref[j, 0:BLOCK] = total[0:BLOCK].astype(BF)
        out_ref[j, BLOCK : BLOCK + 16] = pair_rows(
            total[BLOCK : BLOCK + 1] + total[BLOCK + 1 : BLOCK + 2]
        )


def first_sum(field):
    return pl.pallas_call(
        first_sum_kernel,
        out_shape=jax.ShapeDtypeStruct(field.shape[1:], BF),
        in_specs=[whole()],
        out_specs=whole(),
    )(field)


def second_sum_kernel(in_ref, out_ref, gain_ref):
    total = sum(in_ref[j].astype(F32) for j in range(8))
    out_ref[0] = total[0 : BLOCK // 2]
    out_ref[1] = total[BLOCK // 2 : BLOCK]
    gain = total[BLOCK : BLOCK + 1] + total[BLOCK + 1 : BLOCK + 2]
    gain_ref[...] = jnp.broadcast_to(gain[None], gain_ref.shape)


def second_sum(field):
    return pl.pallas_call(
        second_sum_kernel,
        out_shape=(
            jax.ShapeDtypeStruct((2, BLOCK // 2, 2 * HEAD), F32),
            jax.ShapeDtypeStruct((8, 8, 2 * HEAD), F32),
        ),
        in_specs=[whole()],
        out_specs=(whole(), whole()),
    )(field)


def local(query_in, key_in, value_in, velocity_grad, velocity_gap, query_gain, key_gain, out_proj):
    core, zhi, y = lax.axis_index("core"), lax.axis_index("zhi"), lax.axis_index("y")
    d_velocity = (
        velocity_grad[0].astype(F32) + kl_weight * velocity_gap[0].astype(F32)
    ).astype(BF)
    d_velocity = moved(d_velocity, clip_swap)
    first, second = prepare(query_in[0], key_in[0], value_in[0])

    own = out_proj.T
    other = moved(own, core_swap)
    low = jnp.where(core == 0, own, other)
    high = jnp.where(core == 0, other, own)
    columns = moved(jnp.concatenate([low, high], axis=0), clip_swap)
    columns = lax.all_to_all(
        jnp.broadcast_to(columns[None], (8,) + columns.shape), "zlo", 0, 0
    )
    columns = lax.all_gather(columns, "x", axis=1)
    weight = columns.reshape(-1, 2 * HEAD)

    blocks = [d_velocity] + [moved(d_velocity, y_step(step)) for step in (1, 3, 2)]
    blocks = blocks + [moved(block, core_swap) for block in blocks]
    from_y = [y, (y + 3) % 4, (y + 1) % 4, (y + 2) % 4]
    order = jnp.stack([core * 4 + at for at in from_y] + [(1 - core) * 4 + at for at in from_y])
    order = order.astype(jnp.int32)
    gains = jnp.stack([query_gain, key_gain])

    first = moved(after(first, d_velocity), clip_swap)
    first_in = lax.all_to_all(first, ("core", "y"), 0, 0)
    second = moved(after(second, first), clip_swap)
    d_out = project(order, blocks, weight)
    first_out, first_grad, first_gain = attend(0, first_in, d_out, gains)
    first_back = lax.all_to_all(first_grad, ("core", "y"), 0, 0)
    first_back = moved(first_back, clip_swap)
    second_in = lax.all_to_all(second, ("core", "y"), 0, 0)
    second_out, second_grad, second_gain = attend(1, second_in, d_out, gains)
    second_back = lax.all_to_all(second_grad, ("core", "y"), 0, 0)
    second_back = moved(second_back, clip_swap)

    terms = weigh(order, blocks, (first_out, second_out), (first_gain, second_gain))
    terms = first_sum(lax.all_to_all(terms, "x", 0, 0))
    halves, gain_rows = second_sum(lax.all_to_all(terms, "zlo", 0, 0))
    gain_rows = jnp.sum(lax.all_to_all(gain_rows, ("core", "y"), 0, 0), axis=0)
    straight = jnp.where(zhi == 0, halves[0], halves[1])
    across = jnp.where(zhi == 0, halves[1], halves[0])
    straight = moved(jnp.concatenate([straight, gain_rows], axis=0), clip_swap)
    across = moved(jnp.concatenate([across, gain_rows], axis=0), clip_cross)
    total = straight + across
    grad_out_proj = total[: BLOCK // 2].T
    gain_grads = total[BLOCK // 2].reshape(2, HEAD)

    grad_query, grad_key, grad_value = finish(first_back, second_back)
    return (grad_query[None], grad_key[None], grad_value[None], gain_grads, grad_out_proj)


def solution(mesh):
    fine = Mesh(mesh.devices.reshape(SIZES), AXES)
    blk, uly = ("zlo", "x", "core"), ("zhi", "y")
    rows = P(blk, uly, None)
    return jax.shard_map(
        local,
        mesh=fine,
        in_specs=(rows, rows, rows, rows, rows, P(), P(), P(uly, blk)),
        out_specs=(rows, rows, rows, P(), P(uly, blk)),
        check_vma=False,
    )
```

time: 921 us -> 396 us (0.43); the launches traced: 910 us -> 394 us
  waiting for transfers between devices: 639 us -> 118 us
  starting transfers between devices: 53.2 us -> 186 us
  blocking collectives: 135 us -> 27.3 us
  Pallas kernels: 0 us -> 35.1 us
  matrix products: 30.8 us -> 0 us
  local copies, waits for them, and re-layouts: 27.6 us -> 10.2 us
    all_gather x2 -> x1, waiting for transfers between devices: 300 us -> 0.02 us  [local(): columns = lax.all_gather(columns, 'x', axis=1)]
    reduce_scatter x1 -> x0, waiting for transfers between devices: 257 us -> none  [local(): lax.psum_scatter(weight_term, 'blk', scatter_dimension=1, tiled=True)]
    psum x1 -> x0, blocking collectives: 135 us -> none  [local(): lax.psum(jnp.stack([query_gain_part, key_gain_part]), ('blk', 'uly'))]
    ppermute x0 -> x16, starting transfers between devices: none -> 91.6 us  [moved(): return lax.ppermute(field, AXES, pairs)]
    ppermute x0 -> x16, waiting for transfers between devices: none -> 48.5 us  [moved(): return lax.ppermute(field, AXES, pairs)]
    all_to_all x6 -> x7, starting transfers between devices: 53.1 us -> 94.3 us  [the longest x1 34.5 us: local(): gain_rows = jnp.sum(lax.all_to_all(gain_rows, ('core', 'y'), 0, 0), axis=0)]
    pallas_call x0 -> x10, Pallas kernels: none -> 35.1 us  [the longest x2 16.1 us: attend(): pl.pallas_call(lambda *refs: attend_kernel(head, *refs), out_shape=(jax.S...]
    dot_general x16 -> x0, matrix products: 30.8 us -> none  [the longest x1 7.03 us: local(): lax.dot_general(outcome_rows, d_velocity, (((0,), (0,)), ((), ())), prefe...]
  transfers between devices with their start and end apart: 9 -> 24, of which waited for: 8 -> 11; matrix products, arithmetic and copies ran while one was open for 6% -> 1% of each run, Pallas kernels for 0% -> 9%
where the time goes in v1:
time: 396 us; the launch traced here: 394 us
  starting transfers between devices  186 us (47%)
  waiting for transfers between devices  118 us (30%)
  Pallas kernels  35.1 us (9%)
  blocking collectives  27.3 us (7%)
  between operations  14.4 us (4%)
  local copies, waits for them, and re-layouts  10.2 us (3%)
    ppermute x16, starting transfers between devices, moved(): return lax.ppermute(field, AXES, pairs)  91.6 us
    all_to_all x1, waiting for transfers between devices, local(): halves, gain_rows = second_sum(lax.all_to_all(terms, 'zlo', 0, 0))  48.7 us
    ppermute x16, waiting for transfers between devices, moved(): return lax.ppermute(field, AXES, pairs)  48.5 us
    all_to_all x1, starting transfers between devices, local(): gain_rows = jnp.sum(lax.all_to_all(gain_rows, ('core', 'y'), 0, 0), axis=0)  34.5 us
    all_to_all x1, starting transfers between devices, local(): halves, gain_rows = second_sum(lax.all_to_all(terms, 'zlo', 0, 0))  33.1 us
    all_to_all x1, blocking collectives, local(): terms = first_sum(lax.all_to_all(terms, 'x', 0, 0))  27.3 us
    pallas_call x2, Pallas kernels, attend(): pl.pallas_call(lambda *refs: attend_kernel(head, *refs), out_shape=(jax.S...  16.1 us
    all_to_all x1, waiting for transfers between devices, local(): second_back = lax.all_to_all(second_grad, ('core', 'y'), 0, 0)  9.68 us
  transfers between devices with their start and end apart: 24, of which 11 were waited for; matrix products, arithmetic and copies ran while one was open for 1% of the time, Pallas kernels for 9%

profile of v1, /device:TPU:1, one launch (start us, length us, event | category | flops | bytes accessed | tf_op | source)
XLA Modules:
  0.0 393.9 jit_solution(3798327985132088721)
XLA Ops:
  7.2 8.9 %collective-permute-start.9 = (bf16[48,256]{1,0:T(8,128)(2,1)}, bf16[48,256]{1,0:T(8,128)(2,1)S(1)}, u32[]{:S(2)}, u32[]{:S(2)}) collective-permute-start(bf16[48,256]{1,0:T(8,128)(2,1)} %bitcast.33), channel_id=1, source_target_pairs={{0,8},{1,9},{2,10},{3,11},{4,12},{5,13},{6,14},{7,15},{8,0},{9,1},... | collective-permute-start | bytes 73736 | tf_op jit(solution)/shard_map/ppermute | solution.py:31
  16.1 1.0 collective-permute-done.9
  17.9 10.3 %collective-permute-start.10 = (bf16[96,256]{1,0:T(8,128)(2,1)S(1)}, bf16[96,256]{1,0:T(8,128)(2,1)S(1)}, u32[]{:S(2)}, u32[]{:S(2)}) collective-permute-start(bf16[96,256]{1,0:T(8,128)(2,1)S(1)} %pad_maximum_fusion.2), channel_id=1, source_target_pairs={{0,0},{1,1},{2,2},{3,3},{4,8},{5,9},{6,10},{7,11},{8,4},{9,5},{10,... | collective-permute-start | bytes 147464 | tf_op jit(solution)/shard_map/ppermute | solution.py:31
  28.2 3.8 collective-permute-done.10
  32.8 7.0 %all-to-all-start.1 = ((bf16[8,96,256]{2,1,0:T(8,128)(2,1)}), bf16[8,96,256]{2,1,0:T(8,128)(2,1)S(1)}, u32[]{:S(2)}, u32[]{:S(2)}) async-start(bf16[8,96,256]{2,1,0:T(8,128)(2,1)} %broadcast_in_dim.15), calls=%async_computation.1 | async-start | bytes 786432 | tf_op jit(solution)/shard_map/all_to_all | solution.py:316
  39.8 1.4 fusion
  41.2 9.0 %collective-permute-start = (bf16[128,3072]{1,0:T(8,128)(2,1)S(1)}, bf16[128,3072]{1,0:T(8,128)(2,1)S(1)}, u32[]{:S(2)}, u32[]{:S(2)}) collective-permute-start(bf16[128,3072]{1,0:T(8,128)(2,1)S(1)} %fusion), channel_id=1, source_target_pairs={{0,0},{1,1},{2,2},{3,3},{4,8},{5,9},{6,10},{7,11},{8,4},{9,5},{10,... | collective-permute-start | bytes 2359304 | tf_op jit(solution)/shard_map/ppermute | solution.py:31
  50.2 3.5 all-to-all-done.1
  54.4 2.8 shard_map.119
  57.2 6.4 %collective-permute-done.refs_1_.refs_0_ = bf16[128,3072]{1,0:T(8,128)(2,1)S(1)} collective-permute-done((bf16[128,3072]{1,0:T(8,128)(2,1)S(1)}, bf16[128,3072]{1,0:T(8,128)(2,1)S(1)}, u32[]{:S(2)}, u32[]{:S(2)}) %collective-permute-start) | collective-permute-done | bytes 786464 | tf_op jit(solution)/shard_map/ppermute | solution.py:31
  63.6 0.9 copy-done
  64.5 9.0 %collective-permute-start.1 = (bf16[8,3,128,128]{3,2,1,0:T(8,128)(2,1)}, bf16[8,3,128,128]{3,2,1,0:T(8,128)(2,1)}, u32[]{:S(2)}, u32[]{:S(2)}) collective-permute-start(bf16[8,3,128,128]{3,2,1,0:T(8,128)(2,1)} %shard_map.120), channel_id=1, source_target_pairs={{0,0},{1,1},{2,2},{3,3},{4,8},{5,9},{6,10},{7,11},{8,4},{9,5},{10,... | collective-permute-start | bytes 2359304 | tf_op jit(solution)/shard_map/ppermute | solution.py:31
  73.5 4.8 %collective-permute-start.4 = (bf16[128,3072]{1,0:T(8,128)(2,1)}, bf16[128,3072]{1,0:T(8,128)(2,1)S(1)}, u32[]{:S(2)}, u32[]{:S(2)}) collective-permute-start(bf16[128,3072]{1,0:T(8,128)(2,1)} %copy-done), channel_id=1, source_target_pairs={{0,2},{1,3},{2,0},{3,1},{4,6},{5,7},{6,4},{7,5},{8,10},{9,11},{10,... | collective-permute-start | bytes 2359304 | tf_op jit(solution)/shard_map/ppermute | solution.py:31
  78.3 2.7 collective-permute-start.3
  81.0 2.6 collective-permute-start.2
  83.6 19.9 %collective-permute-done.1.refs_1_ = bf16[8,3,128,128]{3,2,1,0:T(8,128)(2,1)} collective-permute-done((bf16[8,3,128,128]{3,2,1,0:T(8,128)(2,1)}, bf16[8,3,128,128]{3,2,1,0:T(8,128)(2,1)}, u32[]{:S(2)}, u32[]{:S(2)}) %collective-permute-start.1) | collective-permute-done | bytes 786464 | tf_op jit(solution)/shard_map/ppermute | solution.py:31
  103.5 6.8 %collective-permute-start.12 = (bf16[8,3,128,128]{3,2,1,0:T(8,128)(2,1)}, bf16[8,3,128,128]{3,2,1,0:T(8,128)(2,1)}, u32[]{:S(2)}, u32[]{:S(2)}) collective-permute-start(bf16[8,3,128,128]{3,2,1,0:T(8,128)(2,1)} %shard_map.123), channel_id=1, source_target_pairs={{0,0},{1,1},{2,2},{3,3},{4,8},{5,9},{6,10},{7,11},{8,4},{9,5},{10,... | collective-permute-start | bytes 2359304 | tf_op jit(solution)/shard_map/ppermute | solution.py:31
  110.4 4.6 %all-to-all-start = ((bf16[8,3,128,128]{3,2,1,0:T(8,128)(2,1)}), bf16[8,3,128,128]{3,2,1,0:T(8,128)(2,1)}, u32[]{:S(2)}, u32[]{:S(2)}) async-start(bf16[8,3,128,128]{3,2,1,0:T(8,128)(2,1)} %collective-permute-done.1.refs_1_), calls=%async_computation | async-start | bytes 1572864 | tf_op jit(solution)/shard_map/all_to_all | solution.py:330
  115.0 1.9 collective-permute-start.5
  116.9 2.4 collective-permute-start.8
  119.3 1.9 collective-permute-start.7
  121.3 2.4 collective-permute-start.6
  123.7 3.6 all-to-all-done.refs_0_
  127.3 14.0 %collective-permute-done.12 = bf16[8,3,128,128]{3,2,1,0:T(8,128)(2,1)} collective-permute-done((bf16[8,3,128,128]{3,2,1,0:T(8,128)(2,1)}, bf16[8,3,128,128]{3,2,1,0:T(8,128)(2,1)}, u32[]{:S(2)}, u32[]{:S(2)}) %collective-permute-start.12) | collective-permute-done | bytes 786464 | tf_op jit(solution)/shard_map/ppermute | solution.py:31
  141.3 4.6 %all-to-all-start.3 = ((bf16[8,3,128,128]{3,2,1,0:T(8,128)(2,1)}), bf16[8,3,128,128]{3,2,1,0:T(8,128)(2,1)}, u32[]{:S(2)}, u32[]{:S(2)}) async-start(bf16[8,3,128,128]{3,2,1,0:T(8,128)(2,1)} %collective-permute-done.12), calls=%async_computation.3 | async-start | bytes 1572864 | tf_op jit(solution)/shard_map/all_to_all | solution.py:336
  146.0 1.4 copy-done.6
  147.4 4.5 %shard_map.121.refs_1_ = bf16[2,1024,128]{2,1,0:T(8,128)(2,1)S(1)} custom-call(s32[8]{0:T(128)S(1)} %stack.44.order_ref, bf16[128,3072]{1,0:T(8,128)(2,1)S(1)} %copy-done.1, bf16[128,3072]{1,0:T(8,128)(2,1)S(1)} %collective-permute-done.2.refs_1_, bf16[128,3072]{1,0:T(8,128)(2,1)S(1)} %collective-permute-done.3.refs_2_, ...), custom_call_target="tpu_custom_call" | custom-call | flops 1610612736 | bytes 10485760 | tf_op jit(solution)/shard_map/pallas_call | solution.py:127
  151.9 7.5 %shard_map.122 = (bf16[1024,128]{1,0:T(8,128)(2,1)S(1)}, bf16[8,3,128,128]{3,2,1,0:T(8,128)(2,1)S(1)}, f32[2,128]{1,0:T(2,128)S(1)}) custom-call(bf16[8,3,128,128]{3,2,1,0:T(8,128)(2,1)} %all-to-all-done.refs_0_, bf16[2,1024,128]{2,1,0:T(8,128)(2,1)S(1)} %shard_map.121.refs_1_, f32[2,128]{1,0:T(2,128)S(1)} %pad_maximum_fusion.3.refs_2_), custom_call_target="tpu_custom_call" | custom-call | flops 1610612736 | bytes 2097152 | tf_op jit(solution)/shard_map/pallas_call | solution.py:197
  159.5 1.0 copy-done.7
  161.9 4.9 %all-to-all-start.2 = ((bf16[8,3,128,128]{3,2,1,0:T(8,128)(2,1)}), bf16[8,3,128,128]{3,2,1,0:T(8,128)(2,1)}, u32[]{:S(2)}, u32[]{:S(2)}) async-start(bf16[8,3,128,128]{3,2,1,0:T(8,128)(2,1)} %copy-done.7), calls=%async_computation.2 | async-start | bytes 1572864 | tf_op jit(solution)/shard_map/all_to_all | solution.py:334
  166.9 8.5 %shard_map.124 = (bf16[1024,128]{1,0:T(8,128)(2,1)S(1)}, bf16[8,3,128,128]{3,2,1,0:T(8,128)(2,1)}, f32[2,128]{1,0:T(2,128)S(1)}) custom-call(bf16[8,3,128,128]{3,2,1,0:T(8,128)(2,1)} %all-to-all-done.3.refs_0_, bf16[2,1024,128]{2,1,0:T(8,128)(2,1)S(1)} %copy-done.9, f32[2,128]{1,0:T(2,128)S(1)} %pad_maximum_fusion.3.refs_2_), custom_call_target="tpu_custom_call" | custom-call | flops 1610612736 | bytes 2097152 | tf_op jit(solution)/shard_map/pallas_call | solution.py:197
  175.5 4.6 %shard_map.126 = bf16[4,8,112,256]{3,2,1,0:T(8,128)(2,1)S(1)} custom-call(s32[8]{0:T(128)S(1)} %stack.44.order_ref, bf16[128,3072]{1,0:T(8,128)(2,1)S(1)} %copy-done.1, bf16[128,3072]{1,0:T(8,128)(2,1)S(1)} %copy-done.5, bf16[128,3072]{1,0:T(8,128)(2,1)S(1)} %copy-done.3, bf16[128,3072]{1,0:T(8,128)(2,1)S(1)} %collective-permute-done.4.refs_3_, ...), custom_call_target="tpu_custom_call" | custom-call | flops 1610612736 | bytes 10485760 | tf_op jit(solution)/shard_map/pallas_call | solution.py:249
  180.1 27.3 %all_to_all.40.in_ref = bf16[4,8,112,256]{3,2,1,0:T(8,128)(2,1)} all-to-all(bf16[4,8,112,256]{3,2,1,0:T(8,128)(2,1)S(1)} %shard_map.126), channel_id=1, replica_groups=mesh['zlo'=8,'x'=4,'core'=2,'zhi'=2,'y'=4] {'x'}, dimensions={0} | all-to-all | bytes 3670016 | tf_op jit(solution)/shard_map/all_to_all | solution.py:342
  207.4 5.6 %all-to-all-start.4 = ((bf16[8,3,128,128]{3,2,1,0:T(8,128)(2,1)}), bf16[8,3,128,128]{3,2,1,0:T(8,128)(2,1)S(1)}, u32[]{:S(2)}, u32[]{:S(2)}) async-start(bf16[8,3,128,128]{3,2,1,0:T(8,128)(2,1)} %get-tuple-element.21), calls=%async_computation.4 | async-start | bytes 1572864 | tf_op jit(solution)/shard_map/all_to_all | solution.py:338
  212.9 2.5 shard_map.127
  215.4 9.7 %all-to-all-done.4 = bf16[8,3,128,128]{3,2,1,0:T(8,128)(2,1)S(1)} async-done(((bf16[8,3,128,128]{3,2,1,0:T(8,128)(2,1)}), bf16[8,3,128,128]{3,2,1,0:T(8,128)(2,1)S(1)}, u32[]{:S(2)}, u32[]{:S(2)}) %all-to-all-start.4) | async-done | bytes 786464 | tf_op jit(solution)/shard_map/all_to_all | solution.py:338
  225.1 33.1 %all-to-all-start.6 = ((bf16[8,112,256]{2,1,0:T(8,128)(2,1)}), bf16[8,112,256]{2,1,0:T(8,128)(2,1)S(1)}, u32[]{:S(2)}, u32[]{:S(2)}) async-start(bf16[8,112,256]{2,1,0:T(8,128)(2,1)} %shard_map.127), calls=%async_computation.6 | async-start | bytes 917504 | tf_op jit(solution)/shard_map/all_to_all | solution.py:343
  258.2 8.9 %collective-permute-start.11 = (bf16[8,3,128,128]{3,2,1,0:T(8,128)(2,1)}, bf16[8,3,128,128]{3,2,1,0:T(8,128)(2,1)S(1)}, u32[]{:S(2)}, u32[]{:S(2)}) collective-permute-start(bf16[8,3,128,128]{3,2,1,0:T(8,128)(2,1)} %all-to-all-done.2), channel_id=1, source_target_pairs={{0,0},{1,1},{2,2},{3,3},{4,8},{5,9},{6,10},{7,11},{8,4},{9,5},{10,... | collective-permute-start | bytes 2359304 | tf_op jit(solution)/shard_map/ppermute | solution.py:31
  267.1 5.3 %collective-permute-start.13 = (bf16[8,3,128,128]{3,2,1,0:T(8,128)(2,1)S(1)}, bf16[8,3,128,128]{3,2,1,0:T(8,128)(2,1)S(1)}, u32[]{:S(2)}, u32[]{:S(2)}) collective-permute-start(bf16[8,3,128,128]{3,2,1,0:T(8,128)(2,1)S(1)} %all-to-all-done.4), channel_id=1, source_target_pairs={{0,0},{1,1},{2,2},{3,3},{4,8},{5,9},{6,10},{7,11},{8,4},{9,5},{10,... | collective-permute-start | bytes 2359304 | tf_op jit(solution)/shard_map/ppermute | solution.py:31
  272.5 48.7 %all-to-all-done.6.in_ref = bf16[8,112,256]{2,1,0:T(8,128)(2,1)S(1)} async-done(((bf16[8,112,256]{2,1,0:T(8,128)(2,1)}), bf16[8,112,256]{2,1,0:T(8,128)(2,1)S(1)}, u32[]{:S(2)}, u32[]{:S(2)}) %all-to-all-start.6) | async-done | bytes 458784 | tf_op jit(solution)/shard_map/all_to_all | solution.py:343
  322.0 1.7 shard_map.128
  323.7 34.5 %all-to-all-start.7 = ((f32[8,8,256]{2,1,0:T(8,128)}), f32[8,8,256]{2,1,0:T(8,128)S(1)}, u32[]{:S(2)}, u32[]{:S(2)}) async-start(f32[8,8,256]{2,1,0:T(8,128)} %get-tuple-element.30), calls=%async_computation.7 | async-start | bytes 131072 | tf_op jit(solution)/shard_map/all_to_all | solution.py:344
  359.1 4.1 %all-to-all-done.7 = f32[8,8,256]{2,1,0:T(8,128)S(1)} async-done(((f32[8,8,256]{2,1,0:T(8,128)}), f32[8,8,256]{2,1,0:T(8,128)S(1)}, u32[]{:S(2)}, u32[]{:S(2)}) %all-to-all-start.7) | async-done | bytes 65568 | tf_op jit(solution)/shard_map/all_to_all | solution.py:344
  363.2 8.4 %collective-permute-start.15 = (f32[56,256]{1,0:T(8,128)S(1)}, f32[56,256]{1,0:T(8,128)S(1)}, u32[]{:S(2)}, u32[]{:S(2)}) collective-permute-start(f32[56,256]{1,0:T(8,128)S(1)} %get-tuple-element.35), channel_id=1, source_target_pairs={{0,8},{1,9},{2,10},{3,11},{4,0},{5,1},{6,2},{7,3},{8,12},{9,13},{1... | collective-permute-start | bytes 172040 | tf_op jit(solution)/shard_map/ppermute | solution.py:31
  371.7 6.1 %collective-permute-start.14 = (f32[56,256]{1,0:T(8,128)S(1)}, f32[56,256]{1,0:T(8,128)S(1)}, u32[]{:S(2)}, u32[]{:S(2)}) collective-permute-start(f32[56,256]{1,0:T(8,128)S(1)} %get-tuple-element.36), channel_id=1, source_target_pairs={{0,0},{1,1},{2,2},{3,3},{4,8},{5,9},{6,10},{7,11},{8,4},{9,5},{10,... | collective-permute-start | bytes 172040 | tf_op jit(solution)/shard_map/ppermute | solution.py:31
  377.8 0.9 copy-done.14
  379.6 2.9 shard_map.125
  382.5 3.4 collective-permute-done.14
  (62 shorter events, 7.7 us)
Async XLA Ops:
  7.2 32.6 %copy-start.16 = (bf16[1,128,3072]{2,1,0:T(8,128)(2,1)S(1)}, bf16[1,128,3072]{2,1,0:T(8,128)(2,1)}, u32[]{:S(2)}) copy-start(bf16[1,128,3072]{2,1,0:T(8,128)(2,1)} %param.12) | copy-start | bytes 2359300
  7.2 10.0 %collective-permute-start.9 = (bf16[48,256]{1,0:T(8,128)(2,1)}, bf16[48,256]{1,0:T(8,128)(2,1)S(1)}, u32[]{:S(2)}, u32[]{:S(2)}) collective-permute-start(bf16[48,256]{1,0:T(8,128)(2,1)} %bitcast.33), channel_id=1, source_target_pairs={{0,8},{1,9},{2,10},{3,11},{4,12},{5,13},{6,14},{7,15},{8,0},{9,1},... | collective-permute-start | bytes 73736 | tf_op jit(solution)/shard_map/ppermute | solution.py:31
  17.9 14.1 %collective-permute-start.10 = (bf16[96,256]{1,0:T(8,128)(2,1)S(1)}, bf16[96,256]{1,0:T(8,128)(2,1)S(1)}, u32[]{:S(2)}, u32[]{:S(2)}) collective-permute-start(bf16[96,256]{1,0:T(8,128)(2,1)S(1)} %pad_maximum_fusion.2), channel_id=1, source_target_pairs={{0,0},{1,1},{2,2},{3,3},{4,8},{5,9},{6,10},{7,11},{8,4},{9,5},{10,... | collective-permute-start | bytes 147464 | tf_op jit(solution)/shard_map/ppermute | solution.py:31
  32.8 20.9 %all-to-all-start.1 = ((bf16[8,96,256]{2,1,0:T(8,128)(2,1)}), bf16[8,96,256]{2,1,0:T(8,128)(2,1)S(1)}, u32[]{:S(2)}, u32[]{:S(2)}) async-start(bf16[8,96,256]{2,1,0:T(8,128)(2,1)} %broadcast_in_dim.15), calls=%async_computation.1 | async-start | bytes 786432 | tf_op jit(solution)/shard_map/all_to_all | solution.py:316
  39.8 106.3 %all-gather.3.cloned.1.call-start = ((), (), s32[]{:S(2)}) async-start(), calls=%async_computation.8 | async-start | bytes 1966080 | tf_op jit(solution)/shard_map/all_gather | solution.py:319
  41.2 22.4 %collective-permute-start = (bf16[128,3072]{1,0:T(8,128)(2,1)S(1)}, bf16[128,3072]{1,0:T(8,128)(2,1)S(1)}, u32[]{:S(2)}, u32[]{:S(2)}) collective-permute-start(bf16[128,3072]{1,0:T(8,128)(2,1)S(1)} %fusion), channel_id=1, source_target_pairs={{0,0},{1,1},{2,2},{3,3},{4,8},{5,9},{6,10},{7,11},{8,4},{9,5},{10,... | collective-permute-start | bytes 2359304 | tf_op jit(solution)/shard_map/ppermute | solution.py:31
  53.6 0.7 copy-start.13
  63.6 0.9 copy-start
  64.5 39.0 %collective-permute-start.1 = (bf16[8,3,128,128]{3,2,1,0:T(8,128)(2,1)}, bf16[8,3,128,128]{3,2,1,0:T(8,128)(2,1)}, u32[]{:S(2)}, u32[]{:S(2)}) collective-permute-start(bf16[8,3,128,128]{3,2,1,0:T(8,128)(2,1)} %shard_map.120), channel_id=1, source_target_pairs={{0,0},{1,1},{2,2},{3,3},{4,8},{5,9},{6,10},{7,11},{8,4},{9,5},{10,... | collective-permute-start | bytes 2359304 | tf_op jit(solution)/shard_map/ppermute | solution.py:31
  73.5 43.5 %collective-permute-start.4 = (bf16[128,3072]{1,0:T(8,128)(2,1)}, bf16[128,3072]{1,0:T(8,128)(2,1)S(1)}, u32[]{:S(2)}, u32[]{:S(2)}) collective-permute-start(bf16[128,3072]{1,0:T(8,128)(2,1)} %copy-done), channel_id=1, source_target_pairs={{0,2},{1,3},{2,0},{3,1},{4,6},{5,7},{6,4},{7,5},{8,10},{9,11},{10,... | collective-permute-start | bytes 2359304 | tf_op jit(solution)/shard_map/ppermute | solution.py:31
  78.3 41.0 %collective-permute-start.3 = (bf16[128,3072]{1,0:T(8,128)(2,1)}, bf16[128,3072]{1,0:T(8,128)(2,1)S(1)}, u32[]{:S(2)}, u32[]{:S(2)}) collective-permute-start(bf16[128,3072]{1,0:T(8,128)(2,1)} %copy-done), channel_id=1, source_target_pairs={{0,3},{1,0},{2,1},{3,2},{4,7},{5,4},{6,5},{7,6},{8,11},{9,8},{10,9... | collective-permute-start | bytes 2359304 | tf_op jit(solution)/shard_map/ppermute | solution.py:31
  81.0 40.3 %collective-permute-start.2 = (bf16[128,3072]{1,0:T(8,128)(2,1)}, bf16[128,3072]{1,0:T(8,128)(2,1)S(1)}, u32[]{:S(2)}, u32[]{:S(2)}) collective-permute-start(bf16[128,3072]{1,0:T(8,128)(2,1)} %copy-done), channel_id=1, source_target_pairs={{0,1},{1,2},{2,3},{3,0},{4,5},{5,6},{6,7},{7,4},{8,9},{9,10},{10,1... | collective-permute-start | bytes 2359304 | tf_op jit(solution)/shard_map/ppermute | solution.py:31
  103.5 11.5 %copy-start.1 = (bf16[128,3072]{1,0:T(8,128)(2,1)S(1)}, bf16[128,3072]{1,0:T(8,128)(2,1)}, u32[]{:S(2)}) copy-start(bf16[128,3072]{1,0:T(8,128)(2,1)} %copy-done) | copy-start | bytes 2359300
  103.5 42.4 %copy-start.17 = (f32[128]{0:T(128)S(1)}, f32[128]{0:T(128)}, u32[]{:S(2)}) copy-start(f32[128]{0:T(128)} %param.14) | copy-start | bytes 1540
  103.5 42.4 %copy-start.18 = (f32[128]{0:T(128)S(1)}, f32[128]{0:T(128)}, u32[]{:S(2)}) copy-start(f32[128]{0:T(128)} %param.13) | copy-start | bytes 1540
  103.5 37.7 %collective-permute-start.12 = (bf16[8,3,128,128]{3,2,1,0:T(8,128)(2,1)}, bf16[8,3,128,128]{3,2,1,0:T(8,128)(2,1)}, u32[]{:S(2)}, u32[]{:S(2)}) collective-permute-start(bf16[8,3,128,128]{3,2,1,0:T(8,128)(2,1)} %shard_map.123), channel_id=1, source_target_pairs={{0,0},{1,1},{2,2},{3,3},{4,8},{5,9},{6,10},{7,11},{8,4},{9,5},{10,... | collective-permute-start | bytes 2359304 | tf_op jit(solution)/shard_map/ppermute | solution.py:31
  110.4 16.9 %all-to-all-start = ((bf16[8,3,128,128]{3,2,1,0:T(8,128)(2,1)}), bf16[8,3,128,128]{3,2,1,0:T(8,128)(2,1)}, u32[]{:S(2)}, u32[]{:S(2)}) async-start(bf16[8,3,128,128]{3,2,1,0:T(8,128)(2,1)} %collective-permute-done.1.refs_1_), calls=%async_computation | async-start | bytes 1572864 | tf_op jit(solution)/shard_map/all_to_all | solution.py:330
  115.0 31.0 %collective-permute-start.5 = (bf16[128,3072]{1,0:T(8,128)(2,1)S(1)}, bf16[128,3072]{1,0:T(8,128)(2,1)}, u32[]{:S(2)}, u32[]{:S(2)}) collective-permute-start(bf16[128,3072]{1,0:T(8,128)(2,1)S(1)} %copy-done.1), channel_id=1, source_target_pairs={{0,8},{1,9},{2,10},{3,11},{4,12},{5,13},{6,14},{7,15},{8,0},{9,1},... | collective-permute-start | bytes 2359304 | tf_op jit(solution)/shard_map/ppermute | solution.py:31
  116.9 29.1 %collective-permute-start.8 = (bf16[128,3072]{1,0:T(8,128)(2,1)S(1)}, bf16[128,3072]{1,0:T(8,128)(2,1)}, u32[]{:S(2)}, u32[]{:S(2)}) collective-permute-start(bf16[128,3072]{1,0:T(8,128)(2,1)S(1)} %collective-permute-done.4.refs_3_), channel_id=1, source_target_pairs={{0,8},{1,9},{2,10},{3,11},{4,12},{5,13},{6,14},{7,15},{8,0},{9,1},... | collective-permute-start | bytes 2359304 | tf_op jit(solution)/shard_map/ppermute | solution.py:31
  119.3 32.6 %copy-start.2 = (bf16[128,3072]{1,0:T(8,128)(2,1)}, bf16[128,3072]{1,0:T(8,128)(2,1)S(1)}, u32[]{:S(2)}) copy-start(bf16[128,3072]{1,0:T(8,128)(2,1)S(1)} %collective-permute-done.3.refs_2_) | copy-start | bytes 2359300
  119.3 26.6 %collective-permute-start.7 = (bf16[128,3072]{1,0:T(8,128)(2,1)S(1)}, bf16[128,3072]{1,0:T(8,128)(2,1)}, u32[]{:S(2)}, u32[]{:S(2)}) collective-permute-start(bf16[128,3072]{1,0:T(8,128)(2,1)S(1)} %collective-permute-done.3.refs_2_), channel_id=1, source_target_pairs={{0,8},{1,9},{2,10},{3,11},{4,12},{5,13},{6,14},{7,15},{8,0},{9,1},... | collective-permute-start | bytes 2359304 | tf_op jit(solution)/shard_map/ppermute | solution.py:31
  121.3 30.6 %copy-start.4 = (bf16[128,3072]{1,0:T(8,128)(2,1)}, bf16[128,3072]{1,0:T(8,128)(2,1)S(1)}, u32[]{:S(2)}) copy-start(bf16[128,3072]{1,0:T(8,128)(2,1)S(1)} %collective-permute-done.2.refs_1_) | copy-start | bytes 2359300
  121.3 24.7 %collective-permute-start.6 = (bf16[128,3072]{1,0:T(8,128)(2,1)S(1)}, bf16[128,3072]{1,0:T(8,128)(2,1)}, u32[]{:S(2)}, u32[]{:S(2)}) collective-permute-start(bf16[128,3072]{1,0:T(8,128)(2,1)S(1)} %collective-permute-done.2.refs_1_), channel_id=1, source_target_pairs={{0,8},{1,9},{2,10},{3,11},{4,12},{5,13},{6,14},{7,15},{8,0},{9,1},... | collective-permute-start | bytes 2359304 | tf_op jit(solution)/shard_map/ppermute | solution.py:31
  141.3 20.7 %all-to-all-start.3 = ((bf16[8,3,128,128]{3,2,1,0:T(8,128)(2,1)}), bf16[8,3,128,128]{3,2,1,0:T(8,128)(2,1)}, u32[]{:S(2)}, u32[]{:S(2)}) async-start(bf16[8,3,128,128]{3,2,1,0:T(8,128)(2,1)} %collective-permute-done.12), calls=%async_computation.3 | async-start | bytes 1572864 | tf_op jit(solution)/shard_map/all_to_all | solution.py:336
  146.0 1.4 copy-start.6
  159.5 1.0 copy-start.7
  160.4 0.8 copy-start.8
  161.2 0.7 copy-start.10
  161.9 4.9 %copy-start.9 = (bf16[2,1024,128]{2,1,0:T(8,128)(2,1)S(1)}, bf16[2,1024,128]{2,1,0:T(8,128)(2,1)}, u32[]{:S(2)}) copy-start(bf16[2,1024,128]{2,1,0:T(8,128)(2,1)} %copy-done.8) | copy-start | bytes 1572868
  161.9 18.2 %all-to-all-start.2 = ((bf16[8,3,128,128]{3,2,1,0:T(8,128)(2,1)}), bf16[8,3,128,128]{3,2,1,0:T(8,128)(2,1)}, u32[]{:S(2)}, u32[]{:S(2)}) async-start(bf16[8,3,128,128]{3,2,1,0:T(8,128)(2,1)} %copy-done.7), calls=%async_computation.2 | async-start | bytes 1572864 | tf_op jit(solution)/shard_map/all_to_all | solution.py:334
  166.9 8.6 %copy-start.3 = (bf16[128,3072]{1,0:T(8,128)(2,1)S(1)}, bf16[128,3072]{1,0:T(8,128)(2,1)}, u32[]{:S(2)}) copy-start(bf16[128,3072]{1,0:T(8,128)(2,1)} %copy-done.2) | copy-start | bytes 2359300
  166.9 8.6 %copy-start.5 = (bf16[128,3072]{1,0:T(8,128)(2,1)S(1)}, bf16[128,3072]{1,0:T(8,128)(2,1)}, u32[]{:S(2)}) copy-start(bf16[128,3072]{1,0:T(8,128)(2,1)} %copy-done.4) | copy-start | bytes 2359300
  166.9 8.6 %copy-start.11 = (bf16[1024,128]{1,0:T(8,128)(2,1)S(1)}, bf16[1024,128]{1,0:T(8,128)(2,1)}, u32[]{:S(2)}) copy-start(bf16[1024,128]{1,0:T(8,128)(2,1)} %copy-done.10) | copy-start | bytes 786436
  207.4 17.7 %all-to-all-start.4 = ((bf16[8,3,128,128]{3,2,1,0:T(8,128)(2,1)}), bf16[8,3,128,128]{3,2,1,0:T(8,128)(2,1)S(1)}, u32[]{:S(2)}, u32[]{:S(2)}) async-start(bf16[8,3,128,128]{3,2,1,0:T(8,128)(2,1)} %get-tuple-element.21), calls=%async_computation.4 | async-start | bytes 1572864 | tf_op jit(solution)/shard_map/all_to_all | solution.py:338
  225.1 96.1 %all-to-all-start.6 = ((bf16[8,112,256]{2,1,0:T(8,128)(2,1)}), bf16[8,112,256]{2,1,0:T(8,128)(2,1)S(1)}, u32[]{:S(2)}, u32[]{:S(2)}) async-start(bf16[8,112,256]{2,1,0:T(8,128)(2,1)} %shard_map.127), calls=%async_computation.6 | async-start | bytes 917504 | tf_op jit(solution)/shard_map/all_to_all | solution.py:343
  258.2 119.6 %collective-permute-start.11 = (bf16[8,3,128,128]{3,2,1,0:T(8,128)(2,1)}, bf16[8,3,128,128]{3,2,1,0:T(8,128)(2,1)S(1)}, u32[]{:S(2)}, u32[]{:S(2)}) collective-permute-start(bf16[8,3,128,128]{3,2,1,0:T(8,128)(2,1)} %all-to-all-done.2), channel_id=1, source_target_pairs={{0,0},{1,1},{2,2},{3,3},{4,8},{5,9},{6,10},{7,11},{8,4},{9,5},{10,... | collective-permute-start | bytes 2359304 | tf_op jit(solution)/shard_map/ppermute | solution.py:31
  267.1 110.7 %collective-permute-start.13 = (bf16[8,3,128,128]{3,2,1,0:T(8,128)(2,1)S(1)}, bf16[8,3,128,128]{3,2,1,0:T(8,128)(2,1)S(1)}, u32[]{:S(2)}, u32[]{:S(2)}) collective-permute-start(bf16[8,3,128,128]{3,2,1,0:T(8,128)(2,1)S(1)} %all-to-all-done.4), channel_id=1, source_target_pairs={{0,0},{1,1},{2,2},{3,3},{4,8},{5,9},{6,10},{7,11},{8,4},{9,5},{10,... | collective-permute-start | bytes 2359304 | tf_op jit(solution)/shard_map/ppermute | solution.py:31
  321.2 0.8 copy-start.12
  323.7 39.5 %all-to-all-start.7 = ((f32[8,8,256]{2,1,0:T(8,128)}), f32[8,8,256]{2,1,0:T(8,128)S(1)}, u32[]{:S(2)}, u32[]{:S(2)}) async-start(f32[8,8,256]{2,1,0:T(8,128)} %get-tuple-element.30), calls=%async_computation.7 | async-start | bytes 131072 | tf_op jit(solution)/shard_map/all_to_all | solution.py:344
  363.2 19.3 %collective-permute-start.15 = (f32[56,256]{1,0:T(8,128)S(1)}, f32[56,256]{1,0:T(8,128)S(1)}, u32[]{:S(2)}, u32[]{:S(2)}) collective-permute-start(f32[56,256]{1,0:T(8,128)S(1)} %get-tuple-element.35), channel_id=1, source_target_pairs={{0,8},{1,9},{2,10},{3,11},{4,0},{5,1},{6,2},{7,3},{8,12},{9,13},{1... | collective-permute-start | bytes 172040 | tf_op jit(solution)/shard_map/ppermute | solution.py:31
  371.7 14.2 %collective-permute-start.14 = (f32[56,256]{1,0:T(8,128)S(1)}, f32[56,256]{1,0:T(8,128)S(1)}, u32[]{:S(2)}, u32[]{:S(2)}) collective-permute-start(f32[56,256]{1,0:T(8,128)S(1)} %get-tuple-element.36), channel_id=1, source_target_pairs={{0,0},{1,1},{2,2},{3,3},{4,8},{5,9},{6,10},{7,11},{8,4},{9,5},{10,... | collective-permute-start | bytes 172040 | tf_op jit(solution)/shard_map/ppermute | solution.py:31
  377.8 0.9 copy-start.14
  378.7 0.9 copy-start.15
Sparse Core Ops, SparseCore 0:
  54.5 47.0 all-gather.2

commit v2 on v1

v2 whole, which is shorter than its diff:
```python
import itertools
import math

import jax
import jax.numpy as jnp
import numpy as np
from jax import lax
from jax.experimental import pallas as pl
from jax.experimental.pallas import tpu as pltpu
from jax.sharding import Mesh, PartitionSpec as P

kl_weight = 0.5
norm_eps = 1e-06

AXES = ("zlo", "x", "core", "zhi", "y")
SIZES = (8, 4, 2, 2, 4)
PLACES = list(itertools.product(*map(range, SIZES)))
BF = jnp.bfloat16
F32 = jnp.float32
HEAD = 128
ROWS = 128
GROUPS = 8
SEQ = GROUPS * ROWS
TILE = 256
BLOCK = 96
PARTS = 12


def moved(field, where):
    number = lambda place: int(np.ravel_multi_index(place, SIZES))
    pairs = [(number(place), number(where(*place))) for place in PLACES]
    return lax.ppermute(field, AXES, pairs)


def clip_swap(l, x, c, h, y):
    return (l, x, h, c, y)


def clip_cross(l, x, c, h, y):
    return (l, x, 1 - h, c, y)


def core_swap(l, x, c, h, y):
    return (l, x, 1 - c, h, y)


def y_step(step):
    return lambda l, x, c, h, y: (l, x, c, h, (y + step) % 4)


def x_step(step):
    return lambda l, x, c, h, y: (l, x ^ step, c, h, y)


def z_pair(step):
    return lambda l, x, c, h, y: (l ^ step, x, c, h, y)


def whole():
    return pl.BlockSpec(memory_space=pltpu.VMEM)


def anywhere():
    return pl.BlockSpec(memory_space=pl.ANY)


def after(field, *earlier):
    return pl.pallas_call(
        lambda *refs: None,
        out_shape=jax.ShapeDtypeStruct(field.shape, field.dtype),
        in_specs=[anywhere()] * (1 + len(earlier)),
        out_specs=anywhere(),
        input_output_aliases={0: 0},
    )(field, *earlier)


def prepare_kernel(query_ref, key_ref, value_ref, first_ref, second_ref):
    for part, ref in enumerate((query_ref, key_ref, value_ref)):
        for group in range(GROUPS):
            at = group * 2 * HEAD
            first_ref[group, part] = ref[:, at : at + HEAD]
            second_ref[group, part] = ref[:, at + HEAD : at + 2 * HEAD]


def prepare(query, key, value):
    shape = jax.ShapeDtypeStruct((GROUPS, 3, ROWS, HEAD), BF)
    return pl.pallas_call(
        prepare_kernel,
        out_shape=(shape, shape),
        in_specs=[whole()] * 3,
        out_specs=(whole(), whole()),
    )(query, key, value)


def finish_kernel(first_ref, second_ref, query_ref, key_ref, value_ref):
    for part, ref in enumerate((query_ref, key_ref, value_ref)):
        rows = slice(part * ROWS, (part + 1) * ROWS)
        for group in range(GROUPS):
            at = group * 2 * HEAD
            ref[:, at : at + HEAD] = first_ref[group, rows]
            ref[:, at + HEAD : at + 2 * HEAD] = second_ref[group, rows]


def finish(first, second):
    shape = jax.ShapeDtypeStruct((ROWS, GROUPS * 2 * HEAD), BF)
    return pl.pallas_call(
        finish_kernel,
        out_shape=(shape,) * 3,
        in_specs=[whole()] * 2,
        out_specs=(whole(),) * 3,
    )(first, second)


def form_kernel(core_ref, grad_ref, gap_ref, own_ref, other_ref, out_ref):
    for j in range(PARTS):
        at = slice(j * 256, (j + 1) * 256)
        out_ref[j * ROWS : (j + 1) * ROWS] = (
            grad_ref[:, at].astype(F32) + kl_weight * gap_ref[:, at].astype(F32)
        ).astype(BF)
    half = BLOCK // 2
    core = core_ref[0]
    own_at = pl.multiple_of(PARTS * ROWS + core * half, 16)
    other_at = pl.multiple_of(PARTS * ROWS + (1 - core) * half, 16)
    out_ref[pl.ds(own_at, half)] = own_ref[...]
    out_ref[pl.ds(other_at, half)] = other_ref[...]


def form(core, grad, gap, own, other):
    return pl.pallas_call(
        form_kernel,
        out_shape=jax.ShapeDtypeStruct((PARTS * ROWS + BLOCK, 256), BF),
        in_specs=[pl.BlockSpec(memory_space=pltpu.SMEM)] + [whole()] * 4,
        out_specs=whole(),
    )(core, grad, gap, own, other)


def gather_blocks(order_ref, blocks, rows, sems):
    copies = [
        pltpu.make_async_copy(blocks[i], rows.at[:, order_ref[i]], sems.at[i]) for i in range(8)
    ]
    for copy in copies:
        copy.start()
    for copy in copies:
        copy.wait()


def block_scratch():
    return [pltpu.VMEM((PARTS, GROUPS, ROWS, 256), BF), pltpu.SemaphoreType.DMA((8,))]


def project_kernel(order_ref, *refs):
    blocks, weight_ref, out_ref, rows, sems = refs[:8], refs[8], refs[9], refs[10], refs[11]
    gather_blocks(order_ref, blocks, rows, sems)
    for pair in range(4):
        total = None
        for j in range(PARTS):
            part = jnp.dot(
                rows[j, 2 * pair : 2 * pair + 2].reshape(2 * ROWS, 256),
                weight_ref[j * 256 : (j + 1) * 256],
                preferred_element_type=F32,
            )
            total = part if total is None else total + part
        out = total.astype(BF)
        at = pair * 2 * ROWS
        for head in range(2):
            out_ref[head, at : at + 2 * ROWS] = out[:, head * HEAD : (head + 1) * HEAD]


def project(order, blocks, weight):
    return pl.pallas_call(
        project_kernel,
        out_shape=jax.ShapeDtypeStruct((2, SEQ, HEAD), BF),
        in_specs=[pl.BlockSpec(memory_space=pltpu.SMEM)] + [anywhere()] * 8 + [whole()],
        out_specs=whole(),
        scratch_shapes=block_scratch(),
        compiler_params=pltpu.CompilerParams(vmem_limit_bytes=40 << 20),
    )(order, *blocks, weight)


def attend_kernel(head, *refs):
    in_ref, d_out_ref, gain_ref = refs[:3]
    earlier_ref = refs[3] if len(refs) == 10 else None
    out_ref, grad_ref, gain_out_ref, dk_acc, dv_acc, dq_all = refs[-6:]
    scale = 1.0 / math.sqrt(HEAD)
    query_f = in_ref[:, 0].reshape(SEQ, HEAD).astype(F32)
    key_f = in_ref[:, 1].reshape(SEQ, HEAD).astype(F32)
    value = in_ref[:, 2].reshape(SEQ, HEAD)
    query_gain = gain_ref[0:1]
    key_gain = gain_ref[1:2]
    query_r = lax.rsqrt(jnp.mean(query_f * query_f, axis=-1, keepdims=True) + norm_eps)
    key_r = lax.rsqrt(jnp.mean(key_f * key_f, axis=-1, keepdims=True) + norm_eps)
    query_n = (query_f * query_r * query_gain).astype(BF)
    key_n = (key_f * key_r * key_gain).astype(BF)
    key_t = key_n.T
    value_t = value.T
    for tile in range(SEQ // TILE):
        at = tile * TILE
        query_tile = query_n[at : at + TILE]
        d_out = d_out_ref[head, at : at + TILE]
        d_out_t = d_out.T
        scores = jnp.dot(key_n, query_tile.T, preferred_element_type=F32) * scale
        top = jnp.max(scores, axis=0, keepdims=True)
        terms = jnp.exp(scores - top)
        weights = terms * (1.0 / jnp.sum(terms, axis=0, keepdims=True))
        weights_b = weights.astype(BF)
        out_t = jnp.dot(value_t, weights_b, preferred_element_type=F32).astype(BF)
        delta = jnp.sum(d_out_t.astype(F32) * out_t.astype(F32), axis=0, keepdims=True)
        d_weights = jnp.dot(value, d_out_t, preferred_element_type=F32)
        d_scores = (weights * (d_weights - delta)).astype(BF)
        d_query_t = jnp.dot(key_t, d_scores, preferred_element_type=F32)
        d_key = jnp.dot(d_scores, query_tile, preferred_element_type=F32)
        d_value = jnp.dot(weights_b, d_out, preferred_element_type=F32)
        out_ref[at : at + TILE] = out_t.T
        dq_all[at : at + TILE] = d_query_t.T
        if tile == 0:
            dk_acc[...] = d_key
            dv_acc[...] = d_value
        else:
            dk_acc[...] += d_key
            dv_acc[...] += d_value

    def pull(field, r, gain, cotangent):
        cotangent = cotangent * scale
        scaled = field * r
        gained = cotangent * gain
        inner = jnp.mean(gained * scaled, axis=-1, keepdims=True)
        grad = (r * (gained - scaled * inner)).astype(BF)
        return grad.reshape(GROUPS, ROWS, HEAD), jnp.sum(cotangent * scaled, axis=0, keepdims=True)

    grad_ref[:, 0:ROWS], query_part = pull(query_f, query_r, query_gain, dq_all[...])
    grad_ref[:, ROWS : 2 * ROWS], key_part = pull(key_f, key_r, key_gain, dk_acc[...])
    grad_ref[:, 2 * ROWS : 3 * ROWS] = dv_acc[...].astype(BF).reshape(GROUPS, ROWS, HEAD)
    gains = jnp.concatenate([query_part, key_part], axis=0)
    if earlier_ref is None:
        gain_out_ref[...] = gains
    else:
        tail = pair_rows(gains + earlier_ref[...])
        for group in range(GROUPS):
            gain_out_ref[group] = tail


def attend(head, fields, d_out, gains, earlier=None):
    extra = () if earlier is None else (earlier,)
    gain_shape = jax.ShapeDtypeStruct((2, HEAD), F32)
    if extra:
        gain_shape = jax.ShapeDtypeStruct((GROUPS, 16, HEAD), BF)
    return pl.pallas_call(
        lambda *refs: attend_kernel(head, *refs),
        out_shape=(
            jax.ShapeDtypeStruct((SEQ, HEAD), BF),
            jax.ShapeDtypeStruct((GROUPS, 3 * ROWS, HEAD), BF),
            gain_shape,
        ),
        in_specs=[whole()] * (3 + len(extra)),
        out_specs=(whole(),) * 3,
        scratch_shapes=[pltpu.VMEM((SEQ, HEAD), F32)] * 3,
        compiler_params=pltpu.CompilerParams(vmem_limit_bytes=40 << 20),
    )(fields, d_out, gains, *extra)


def weigh_kernel(order_ref, *refs):
    blocks, head_refs = refs[:8], refs[8:10]
    out_ref, rows, sems, terms = refs[-4:]
    gather_blocks(order_ref, blocks, rows, sems)
    here = order_ref[8]
    out_t = jnp.concatenate([ref[...].T for ref in head_refs], axis=0)
    for j in range(PARTS):
        term = jnp.dot(out_t, rows[j].reshape(SEQ, 256), preferred_element_type=F32)
        for head in range(2):
            terms[head, j * 256 : (j + 1) * 256] = (
                term[head * HEAD : (head + 1) * HEAD].T.astype(BF)
            )
    for head in range(2):
        for i in range(4):
            for j in range(8):
                at = (j * 4 + i) * BLOCK
                out_ref[i ^ here, j, head * BLOCK : (head + 1) * BLOCK] = terms[
                    head, at : at + BLOCK
                ]


def pair_rows(rows):
    high = rows.astype(BF)
    low = (rows - high.astype(F32)).astype(BF)
    return jnp.concatenate([high, low, jnp.zeros((12, rows.shape[1]), BF)], axis=0)


def weigh(order, blocks, outs):
    return pl.pallas_call(
        weigh_kernel,
        out_shape=jax.ShapeDtypeStruct((4, 8, 2 * BLOCK + 16, HEAD), BF),
        in_specs=[pl.BlockSpec(memory_space=pltpu.SMEM)] + [anywhere()] * 8 + [whole()] * 2,
        out_specs=whole(),
        scratch_shapes=block_scratch() + [pltpu.VMEM((2, PARTS * 256, HEAD), BF)],
        compiler_params=pltpu.CompilerParams(vmem_limit_bytes=40 << 20),
    )(order, *blocks, *outs)


def tail_kernel(terms_ref, tails_ref, out_ref, tail, sem):
    total = sum(tails_ref[group].astype(F32) for group in range(GROUPS))
    rows = pair_rows(total[0:2] + total[2:4])
    for i in range(4):
        for j in range(8):
            tail[i, j] = rows
    copy = pltpu.make_async_copy(tail, out_ref.at[:, :, 2 * BLOCK : 2 * BLOCK + 16], sem)
    copy.start()
    copy.wait()


def add_tail(terms, tails):
    return pl.pallas_call(
        tail_kernel,
        out_shape=jax.ShapeDtypeStruct(terms.shape, terms.dtype),
        in_specs=[anywhere(), whole()],
        out_specs=anywhere(),
        scratch_shapes=[pltpu.VMEM((4, 8, 16, HEAD), BF), pltpu.SemaphoreType.DMA],
        input_output_aliases={0: 0},
    )(terms, tails)


def first_sum_kernel(*refs):
    terms, out_ref = refs[:4], refs[4]
    at = 2 * BLOCK
    for j in range(8):
        total = sum(ref[j].astype(F32) for ref in terms)
        out_ref[j, 0:at] = total[0:at].astype(BF)
        out_ref[j, at : at + 16] = pair_rows(total[at : at + 2] + total[at + 2 : at + 4])


def first_sum(terms):
    return pl.pallas_call(
        first_sum_kernel,
        out_shape=jax.ShapeDtypeStruct((8, 2 * BLOCK + 16, HEAD), BF),
        in_specs=[whole()] * 4,
        out_specs=whole(),
    )(*terms)


def second_sum_kernel(zhi_ref, in_ref, straight_ref, across_ref):
    total = sum(in_ref[j].astype(F32) for j in range(8))
    half = BLOCK // 2
    at = 2 * BLOCK
    gain = total[at : at + 2] + total[at + 2 : at + 4]
    row = jnp.concatenate([gain[0:1], gain[1:2]], axis=1)
    low_here = zhi_ref[0] == 0
    for ref in (straight_ref, across_ref):
        ref[half : half + 8] = jnp.broadcast_to(row, (8, 2 * HEAD))
    for head in range(2):
        lanes = slice(head * HEAD, (head + 1) * HEAD)
        low = total[head * BLOCK : head * BLOCK + half]
        high = total[head * BLOCK + half : (head + 1) * BLOCK]
        straight_ref[0:half, lanes] = jnp.where(low_here, low, high)
        across_ref[0:half, lanes] = jnp.where(low_here, high, low)


def second_sum(zhi, field):
    shape = jax.ShapeDtypeStruct((BLOCK // 2 + 8, 2 * HEAD), F32)
    return pl.pallas_call(
        second_sum_kernel,
        out_shape=(shape, shape),
        in_specs=[pl.BlockSpec(memory_space=pltpu.SMEM), whole()],
        out_specs=(whole(), whole()),
    )(zhi, field)


def spread(columns):
    x = lax.axis_index("x")
    columns = lax.all_to_all(
        jnp.broadcast_to(columns[None], (8,) + columns.shape), "zlo", 0, 0
    )
    for at, bit in ((1, 2), (2, 1)):
        other = moved(columns, x_step(bit))
        columns = jnp.where(
            (x & bit) == 0,
            jnp.stack([columns, other], axis=at),
            jnp.stack([other, columns], axis=at),
        )
    return columns


def local(query_in, key_in, value_in, velocity_grad, velocity_gap, query_gain, key_gain, out_proj):
    core, zhi, y = lax.axis_index("core"), lax.axis_index("zhi"), lax.axis_index("y")
    first, second = prepare(query_in[0], key_in[0], value_in[0])
    own = out_proj.T
    formed = form(
        jnp.stack([core]).astype(jnp.int32),
        velocity_grad[0],
        velocity_gap[0],
        own,
        after(moved(own, core_swap), first, second),
    )

    formed = moved(formed, clip_swap)
    d_velocity = formed[: PARTS * ROWS].reshape(PARTS, ROWS, 256)
    first = moved(after(first, formed), clip_swap)
    blocks = [d_velocity] + [moved(d_velocity, y_step(step)) for step in (1, 3, 2)]
    weight = spread(formed[PARTS * ROWS :]).reshape(-1, 2 * HEAD)
    blocks = blocks + [moved(block, core_swap) for block in blocks]
    from_y = [y, (y + 3) % 4, (y + 1) % 4, (y + 2) % 4]
    order = [core * 4 + at for at in from_y] + [(1 - core) * 4 + at for at in from_y]
    order = jnp.stack(order + [lax.axis_index("x")]).astype(jnp.int32)
    gains = jnp.stack([query_gain, key_gain])
    second = moved(after(second, first), clip_swap)

    first_in = lax.all_to_all(first, ("core", "y"), 0, 0)
    d_out = project(order, blocks, after(weight, first_in))
    first_out, first_grad, first_gain = attend(0, first_in, d_out, gains)
    first_back = lax.all_to_all(first_grad, ("core", "y"), 0, 0)
    second_in = lax.all_to_all(after(second, first_back), ("core", "y"), 0, 0)
    first_back = moved(first_back, clip_swap)
    second_out, second_grad, tails = attend(1, second_in, d_out, gains, first_gain)
    tails = lax.all_to_all(tails, ("core", "y"), 0, 0)
    terms = add_tail(weigh(order, blocks, (first_out, second_out)), tails)
    second_grad = after(second_grad, first_back, terms)
    second_back = lax.all_to_all(second_grad, ("core", "y"), 0, 0)
    second_back = moved(second_back, clip_swap)
    terms = first_sum([terms[0]] + [moved(terms[i], x_step(i)) for i in (1, 2, 3)])
    terms = lax.all_to_all(after(terms, second_back), "zlo", 0, 0)
    straight, across = second_sum(jnp.stack([zhi]).astype(jnp.int32), terms)
    total = moved(straight, clip_swap) + moved(across, clip_cross)
    grad_out_proj = total[: BLOCK // 2].T
    gain_grads = total[BLOCK // 2].reshape(2, HEAD)

    grad_query, grad_key, grad_value = finish(first_back, second_back)
    return (grad_query[None], grad_key[None], grad_value[None], gain_grads, grad_out_proj)


def solution(mesh):
    fine = Mesh(mesh.devices.reshape(SIZES), AXES)
    blk, uly = ("zlo", "x", "core"), ("zhi", "y")
    rows = P(blk, uly, None)
    return jax.shard_map(
        local,
        mesh=fine,
        in_specs=(rows, rows, rows, rows, rows, P(), P(), P(uly, blk)),
        out_specs=(rows, rows, rows, P(), P(uly, blk)),
        check_vma=False,
    )
```

time: 396 us -> 335 us (0.85)
  waiting for transfers between devices: 118 us -> 77.3 us
  starting transfers between devices: 186 us -> 150 us
  blocking collectives: 27.3 us -> 50.1 us
  between operations: 14.4 us -> 1.11 us
    all_to_all x6 -> x3, waiting for transfers between devices: 66 us -> 17 us  [the longest x1 17 us: local(): terms = lax.all_to_all(after(terms, second_back), 'zlo', 0, 0)]
    all_to_all x6 -> x3, starting transfers between devices: 89.7 us -> 53.1 us  [the longest x1 31.6 us: local(): terms = lax.all_to_all(after(terms, second_back), 'zlo', 0, 0)]
    all_to_all x1 -> x3, blocking collectives: 27.3 us -> 50.1 us  [the longest x1 17.2 us: local(): second_back = lax.all_to_all(second_grad, ('core', 'y'), 0, 0)]
    ppermute x16 -> x20, waiting for transfers between devices: 48.5 us -> 60.3 us  [moved(): return lax.ppermute(field, AXES, pairs)]
    pallas_call x3 -> x5, Pallas kernels: 8.86 us -> 13 us  [the longest x1 4.93 us: weigh(): pl.pallas_call(weigh_kernel, out_shape=jax.ShapeDtypeStruct((4, 8, 2 * BL...]
    ppermute x16 -> x20, starting transfers between devices: 91.6 us -> 93.4 us  [moved(): return lax.ppermute(field, AXES, pairs)]
    unnamed x38 -> x34, local copies, waits for them, and re-layouts: 8.11 us -> 8.02 us
  transfers between devices with their start and end apart: 24 -> 24, of which waited for: 11 -> 7; matrix products, arithmetic and copies ran while one was open for 1% -> 2% of each run, Pallas kernels for 9% -> 10%
where the time goes in v2:
time: 335 us; the launch traced here: 333 us
  starting transfers between devices  150 us (45%)
  waiting for transfers between devices  77.3 us (23%)
  blocking collectives  50.1 us (15%)
  Pallas kernels  36.7 us (11%)
  local copies, waits for them, and re-layouts  12.2 us (4%)
  other arithmetic  5.17 us (2%)
    ppermute x20, starting transfers between devices, moved(): return lax.ppermute(field, AXES, pairs)  93.4 us
    ppermute x20, waiting for transfers between devices, moved(): return lax.ppermute(field, AXES, pairs)  60.3 us
    all_to_all x1, starting transfers between devices, local(): terms = lax.all_to_all(after(terms, second_back), 'zlo', 0, 0)  31.6 us
    all_to_all x1, starting transfers between devices, spread(): lax.all_to_all(jnp.broadcast_to(columns[None], (8,) + columns.shape), 'zl...  17.9 us
    all_to_all x1, blocking collectives, local(): second_back = lax.all_to_all(second_grad, ('core', 'y'), 0, 0)  17.2 us
    all_to_all x1, waiting for transfers between devices, local(): terms = lax.all_to_all(after(terms, second_back), 'zlo', 0, 0)  17 us
    all_to_all x1, blocking collectives, local(): first_back = lax.all_to_all(first_grad, ('core', 'y'), 0, 0)  16.9 us
    all_to_all x1, blocking collectives, local(): second_in = lax.all_to_all(after(second, first_back), ('core', 'y'), 0, 0)  16 us
  transfers between devices with their start and end apart: 24, of which 7 were waited for; matrix products, arithmetic and copies ran while one was open for 2% of the time, Pallas kernels for 10%

profile of v2, /device:TPU:1, one launch (start us, length us, event | category | flops | bytes accessed | tf_op | source)
XLA Modules:
  0.0 332.5 jit_solution(1177971282587863777)
XLA Ops:
  0.6 8.8 %collective-permute-start = (bf16[48,256]{1,0:T(8,128)(2,1)}, bf16[48,256]{1,0:T(8,128)(2,1)S(1)}, u32[]{:S(2)}, u32[]{:S(2)}) collective-permute-start(bf16[48,256]{1,0:T(8,128)(2,1)} %bitcast.56), channel_id=1, source_target_pairs={{0,8},{1,9},{2,10},{3,11},{4,12},{5,13},{6,14},{7,15},{8,0},{9,1},... | collective-permute-start | bytes 73736 | tf_op jit(solution)/shard_map/ppermute | solution.py:32
  9.4 2.8 shard_map.119
  12.8 2.5 shard_map.121
  15.3 10.0 %collective-permute-start.1 = (bf16[1632,256]{1,0:T(8,128)(2,1)}, bf16[1632,256]{1,0:T(8,128)(2,1)S(1)}, u32[]{:S(2)}, u32[]{:S(2)}) collective-permute-start(bf16[1632,256]{1,0:T(8,128)(2,1)} %shard_map.121), channel_id=1, source_target_pairs={{0,0},{1,1},{2,2},{3,3},{4,8},{5,9},{6,10},{7,11},{8,4},{9,5},{10,... | collective-permute-start | bytes 2506760 | tf_op jit(solution)/shard_map/ppermute | solution.py:32
  25.3 33.9 %collective-permute-done.1.refs_1_ = bf16[1632,256]{1,0:T(8,128)(2,1)S(1)} collective-permute-done((bf16[1632,256]{1,0:T(8,128)(2,1)}, bf16[1632,256]{1,0:T(8,128)(2,1)S(1)}, u32[]{:S(2)}, u32[]{:S(2)}) %collective-permute-start.1) | collective-permute-done | bytes 835616 | tf_op jit(solution)/shard_map/ppermute | solution.py:32
  60.0 17.9 %all-to-all-start.1 = ((bf16[8,96,256]{2,1,0:T(8,128)(2,1)}), bf16[8,96,256]{2,1,0:T(8,128)(2,1)S(1)}, u32[]{:S(2)}, u32[]{:S(2)}) async-start(bf16[8,96,256]{2,1,0:T(8,128)(2,1)} %broadcast_in_dim.15), calls=%async_computation.1 | async-start | bytes 786432 | tf_op jit(solution)/shard_map/all_to_all | solution.py:368
  77.9 8.0 %collective-permute-start.2 = (bf16[8,3,128,128]{3,2,1,0:T(8,128)(2,1)}, bf16[8,3,128,128]{3,2,1,0:T(8,128)(2,1)}, u32[]{:S(2)}, u32[]{:S(2)}) collective-permute-start(bf16[8,3,128,128]{3,2,1,0:T(8,128)(2,1)} %shard_map.122), channel_id=1, source_target_pairs={{0,0},{1,1},{2,2},{3,3},{4,8},{5,9},{6,10},{7,11},{8,4},{9,5},{10,... | collective-permute-start | bytes 2359304 | tf_op jit(solution)/shard_map/ppermute | solution.py:32
  87.1 3.2 collective-permute-start.3
  90.4 3.4 %collective-permute-start.4 = (bf16[12,128,256]{2,1,0:T(8,128)(2,1)S(1)}, bf16[12,128,256]{2,1,0:T(8,128)(2,1)S(1)}, u32[]{:S(2)}, u32[]{:S(2)}) collective-permute-start(bf16[12,128,256]{2,1,0:T(8,128)(2,1)S(1)} %bitcast.42), channel_id=1, source_target_pairs={{0,3},{1,0},{2,1},{3,2},{4,7},{5,4},{6,5},{7,6},{8,11},{9,8},{10,9... | collective-permute-start | bytes 2359304 | tf_op jit(solution)/shard_map/ppermute | solution.py:32
  93.7 3.5 %collective-permute-start.5 = (bf16[12,128,256]{2,1,0:T(8,128)(2,1)S(1)}, bf16[12,128,256]{2,1,0:T(8,128)(2,1)}, u32[]{:S(2)}, u32[]{:S(2)}) collective-permute-start(bf16[12,128,256]{2,1,0:T(8,128)(2,1)S(1)} %bitcast.43), channel_id=1, source_target_pairs={{0,2},{1,3},{2,0},{3,1},{4,6},{5,7},{6,4},{7,5},{8,10},{9,11},{10,... | collective-permute-start | bytes 2359304 | tf_op jit(solution)/shard_map/ppermute | solution.py:32
  97.3 4.7 %collective-permute-start.10 = (bf16[8,96,256]{2,1,0:T(8,128)(2,1)S(1)}, bf16[8,96,256]{2,1,0:T(8,128)(2,1)S(1)}, u32[]{:S(2)}, u32[]{:S(2)}) collective-permute-start(bf16[8,96,256]{2,1,0:T(8,128)(2,1)S(1)} %all-to-all-done.1), channel_id=1, source_target_pairs={{0,32},{1,33},{2,34},{3,35},{4,36},{5,37},{6,38},{7,39},{8,40},{9,... | collective-permute-start | bytes 1179656 | tf_op jit(solution)/shard_map/ppermute | solution.py:32
  102.0 5.4 %collective-permute-done.10 = bf16[8,96,256]{2,1,0:T(8,128)(2,1)S(1)} collective-permute-done((bf16[8,96,256]{2,1,0:T(8,128)(2,1)S(1)}, bf16[8,96,256]{2,1,0:T(8,128)(2,1)S(1)}, u32[]{:S(2)}, u32[]{:S(2)}) %collective-permute-start.10) | collective-permute-done | bytes 393248 | tf_op jit(solution)/shard_map/ppermute | solution.py:32
  108.3 3.1 collective-permute-start.11
  111.4 1.9 collective-permute-start.6
  113.3 2.4 collective-permute-start.7
  115.8 1.9 collective-permute-start.8
  117.7 2.4 collective-permute-start.9
  120.3 3.5 %all-to-all-start = ((bf16[8,3,128,128]{3,2,1,0:T(8,128)(2,1)}), bf16[8,3,128,128]{3,2,1,0:T(8,128)(2,1)S(1)}, u32[]{:S(2)}, u32[]{:S(2)}) async-start(bf16[8,3,128,128]{3,2,1,0:T(8,128)(2,1)} %collective-permute-done.2.refs_1_), calls=%async_computation | async-start | bytes 1572864 | tf_op jit(solution)/shard_map/all_to_all | solution.py:405
  123.8 1.3 pad_maximum_fusion
  125.2 8.6 %collective-permute-start.13 = (bf16[8,3,128,128]{3,2,1,0:T(8,128)(2,1)}, bf16[8,3,128,128]{3,2,1,0:T(8,128)(2,1)}, u32[]{:S(2)}, u32[]{:S(2)}) collective-permute-start(bf16[8,3,128,128]{3,2,1,0:T(8,128)(2,1)} %shard_map.126), channel_id=1, source_target_pairs={{0,0},{1,1},{2,2},{3,3},{4,8},{5,9},{6,10},{7,11},{8,4},{9,5},{10,... | collective-permute-start | bytes 2359304 | tf_op jit(solution)/shard_map/ppermute | solution.py:32
  133.8 2.8 maximum_select_fusion
  137.5 1.4 copy-done.2
  138.9 4.6 %shard_map.124.refs_1_ = bf16[2,1024,128]{2,1,0:T(8,128)(2,1)S(1)} custom-call(s32[9]{0:T(128)S(1)} %stack.89.order_ref, bf16[12,128,256]{2,1,0:T(8,128)(2,1)S(1)} %bitcast.45, bf16[12,128,256]{2,1,0:T(8,128)(2,1)S(1)} %collective-permute-done.3.refs_1_, bf16[12,128,256]{2,1,0:T(8,128)(2,1)S(1)} %collective-permute-done.4.refs_2_, ...), custom_call_target="tpu_custom_call" | custom-call | tf_op jit(solution)/shard_map/pallas_call | solution.py:170
  143.6 6.4 %shard_map.125 = (bf16[1024,128]{1,0:T(8,128)(2,1)S(1)}, bf16[8,384,128]{2,1,0:T(8,128)(2,1)S(1)}, f32[2,128]{1,0:T(2,128)S(1)}) custom-call(bf16[8,3,128,128]{3,2,1,0:T(8,128)(2,1)S(1)} %copy-done.4, bf16[2,1024,128]{2,1,0:T(8,128)(2,1)S(1)} %shard_map.124.refs_1_, f32[2,128]{1,0:T(2,128)S(1)} %pad_maximum_fusion.2.refs_2_), custom_call_target="tpu_custom_call" | custom-call | tf_op jit(solution)/shard_map/pallas_call | solution.py:247
  150.0 16.9 %all_to_all.35.refs_1_ = bf16[8,384,128]{2,1,0:T(8,128)(2,1)} all-to-all(bf16[8,384,128]{2,1,0:T(8,128)(2,1)S(1)} %get-tuple-element.20), channel_id=1, replica_groups=mesh['zlo'=8,'x'=4,'core'=2,'zhi'=2,'y'=4] {'core','y'}, dimensions={0} | all-to-all | bytes 1572864 | tf_op jit(solution)/shard_map/all_to_all | solution.py:408
  166.9 7.4 %collective-permute-start.12 = (bf16[8,384,128]{2,1,0:T(8,128)(2,1)}, bf16[8,384,128]{2,1,0:T(8,128)(2,1)}, u32[]{:S(2)}, u32[]{:S(2)}) collective-permute-start(bf16[8,384,128]{2,1,0:T(8,128)(2,1)} %all_to_all.35.refs_1_), channel_id=1, source_target_pairs={{0,0},{1,1},{2,2},{3,3},{4,8},{5,9},{6,10},{7,11},{8,4},{9,5},{10,... | collective-permute-start | bytes 2359304 | tf_op jit(solution)/shard_map/ppermute | solution.py:32
  174.3 16.0 %all_to_all.36.refs_0_ = bf16[8,3,128,128]{3,2,1,0:T(8,128)(2,1)S(1)} all-to-all(bf16[8,3,128,128]{3,2,1,0:T(8,128)(2,1)} %shard_map.127), channel_id=1, replica_groups=mesh['zlo'=8,'x'=4,'core'=2,'zhi'=2,'y'=4] {'core','y'}, dimensions={0} | all-to-all | bytes 1572864 | tf_op jit(solution)/shard_map/all_to_all | solution.py:409
  190.3 7.0 %shard_map.128 = (bf16[1024,128]{1,0:T(8,128)(2,1)S(1)}, bf16[8,384,128]{2,1,0:T(8,128)(2,1)S(1)}, bf16[8,16,128]{2,1,0:T(8,128)(2,1)}) custom-call(bf16[8,3,128,128]{3,2,1,0:T(8,128)(2,1)S(1)} %all_to_all.36.refs_0_, bf16[2,1024,128]{2,1,0:T(8,128)(2,1)S(1)} %shard_map.124.refs_1_, f32[2,128]{1,0:T(2,128)S(1)} %pad_maximum_fusion.2.refs_2_, ...), custom_call_target="tpu_custom_call" | custom-call | tf_op jit(solution)/shard_map/pallas_call | solution.py:247
  198.1 3.6 %all-to-all-start.4 = ((bf16[8,16,128]{2,1,0:T(8,128)(2,1)}), bf16[8,16,128]{2,1,0:T(8,128)(2,1)S(1)}, u32[]{:S(2)}, u32[]{:S(2)}) async-start(bf16[8,16,128]{2,1,0:T(8,128)(2,1)} %get-tuple-element.25), calls=%async_computation.4 | async-start | bytes 65536 | tf_op jit(solution)/shard_map/all_to_all | solution.py:412
  201.7 4.9 %shard_map.129.terms_ref = bf16[4,8,208,128]{3,2,1,0:T(8,128)(2,1)S(1)} custom-call(s32[9]{0:T(128)S(1)} %stack.89.order_ref, bf16[12,128,256]{2,1,0:T(8,128)(2,1)S(1)} %bitcast.46, bf16[12,128,256]{2,1,0:T(8,128)(2,1)S(1)} %collective-permute-done.3.refs_1_, bf16[12,128,256]{2,1,0:T(8,128)(2,1)S(1)} %collective-permute-done.4.refs_2_, ...), custom_call_target="tpu_custom_call" | custom-call | tf_op jit(solution)/shard_map/pallas_call | solution.py:289
  206.7 1.2 copy-done
  208.5 1.5 shard_map.130.refs_2_
  210.0 17.2 %all_to_all.37 = bf16[8,384,128]{2,1,0:T(8,128)(2,1)} all-to-all(bf16[8,384,128]{2,1,0:T(8,128)(2,1)} %shard_map.131), channel_id=1, replica_groups=mesh['zlo'=8,'x'=4,'core'=2,'zhi'=2,'y'=4] {'core','y'}, dimensions={0} | all-to-all | bytes 1572864 | tf_op jit(solution)/shard_map/all_to_all | solution.py:415
  227.2 6.9 %collective-permute-start.14 = (bf16[8,384,128]{2,1,0:T(8,128)(2,1)}, bf16[8,384,128]{2,1,0:T(8,128)(2,1)S(1)}, u32[]{:S(2)}, u32[]{:S(2)}) collective-permute-start(bf16[8,384,128]{2,1,0:T(8,128)(2,1)} %all_to_all.37), channel_id=1, source_target_pairs={{0,0},{1,1},{2,2},{3,3},{4,8},{5,9},{6,10},{7,11},{8,4},{9,5},{10,... | collective-permute-start | bytes 2359304 | tf_op jit(solution)/shard_map/ppermute | solution.py:32
  235.0 2.2 collective-permute-start.15
  237.2 4.6 %collective-permute-start.16 = (bf16[8,208,128]{2,1,0:T(8,128)(2,1)S(1)}, bf16[8,208,128]{2,1,0:T(8,128)(2,1)S(1)}, u32[]{:S(2)}, u32[]{:S(2)}) collective-permute-start(bf16[8,208,128]{2,1,0:T(8,128)(2,1)S(1)} %get-tuple-element.32), channel_id=1, source_target_pairs={{0,32},{1,33},{2,34},{3,35},{4,36},{5,37},{6,38},{7,39},{8,40},{9,... | collective-permute-start | bytes 1277960 | tf_op jit(solution)/shard_map/ppermute | solution.py:32
  241.8 2.8 collective-permute-start.17
  244.6 4.2 %collective-permute-done.15.refs_1_ = bf16[8,208,128]{2,1,0:T(8,128)(2,1)S(1)} collective-permute-done((bf16[8,208,128]{2,1,0:T(8,128)(2,1)S(1)}, bf16[8,208,128]{2,1,0:T(8,128)(2,1)S(1)}, u32[]{:S(2)}, u32[]{:S(2)}) %collective-permute-start.15) | collective-permute-done | bytes 426016 | tf_op jit(solution)/shard_map/ppermute | solution.py:32
  248.8 6.1 %collective-permute-done.16.refs_2_ = bf16[8,208,128]{2,1,0:T(8,128)(2,1)S(1)} collective-permute-done((bf16[8,208,128]{2,1,0:T(8,128)(2,1)S(1)}, bf16[8,208,128]{2,1,0:T(8,128)(2,1)S(1)}, u32[]{:S(2)}, u32[]{:S(2)}) %collective-permute-start.16) | collective-permute-done | bytes 426016 | tf_op jit(solution)/shard_map/ppermute | solution.py:32
  254.9 5.8 %collective-permute-done.17.refs_3_ = bf16[8,208,128]{2,1,0:T(8,128)(2,1)S(1)} collective-permute-done((bf16[8,208,128]{2,1,0:T(8,128)(2,1)S(1)}, bf16[8,208,128]{2,1,0:T(8,128)(2,1)S(1)}, u32[]{:S(2)}, u32[]{:S(2)}) %collective-permute-start.17) | collective-permute-done | bytes 426016 | tf_op jit(solution)/shard_map/ppermute | solution.py:32
  261.5 2.4 shard_map.133.refs_0_
  264.7 31.6 %all-to-all-start.6 = ((bf16[8,208,128]{2,1,0:T(8,128)(2,1)}), bf16[8,208,128]{2,1,0:T(8,128)(2,1)S(1)}, u32[]{:S(2)}, u32[]{:S(2)}) async-start(bf16[8,208,128]{2,1,0:T(8,128)(2,1)} %shard_map.134), calls=%async_computation.6 | async-start | bytes 851968 | tf_op jit(solution)/shard_map/all_to_all | solution.py:418
  296.4 17.0 %all-to-all-done.6.in_ref = bf16[8,208,128]{2,1,0:T(8,128)(2,1)S(1)} async-done(((bf16[8,208,128]{2,1,0:T(8,128)(2,1)}), bf16[8,208,128]{2,1,0:T(8,128)(2,1)S(1)}, u32[]{:S(2)}, u32[]{:S(2)}) %all-to-all-start.6) | async-done | bytes 426016 | tf_op jit(solution)/shard_map/all_to_all | solution.py:418
  314.1 1.7 shard_map.135
  315.8 5.8 %collective-permute-start.18 = (f32[56,256]{1,0:T(8,128)}, f32[56,256]{1,0:T(8,128)S(1)}, u32[]{:S(2)}, u32[]{:S(2)}) collective-permute-start(f32[56,256]{1,0:T(8,128)} %get-tuple-element.29), channel_id=1, source_target_pairs={{0,0},{1,1},{2,2},{3,3},{4,8},{5,9},{6,10},{7,11},{8,4},{9,5},{10,... | collective-permute-start | bytes 172040 | tf_op jit(solution)/shard_map/ppermute | solution.py:32
  321.6 1.9 collective-permute-start.19
  323.5 2.9 shard_map.132
  326.4 4.9 %collective-permute-done.18 = f32[56,256]{1,0:T(8,128)S(1)} collective-permute-done((f32[56,256]{1,0:T(8,128)}, f32[56,256]{1,0:T(8,128)S(1)}, u32[]{:S(2)}, u32[]{:S(2)}) %collective-permute-start.18) | collective-permute-done | bytes 57376 | tf_op jit(solution)/shard_map/ppermute | solution.py:32
  (67 shorter events, 10.7 us)
Async XLA Ops:
  0.6 11.6 %collective-permute-start = (bf16[48,256]{1,0:T(8,128)(2,1)}, bf16[48,256]{1,0:T(8,128)(2,1)S(1)}, u32[]{:S(2)}, u32[]{:S(2)}) collective-permute-start(bf16[48,256]{1,0:T(8,128)(2,1)} %bitcast.56), channel_id=1, source_target_pairs={{0,8},{1,9},{2,10},{3,11},{4,12},{5,13},{6,14},{7,15},{8,0},{9,1},... | collective-permute-start | bytes 73736 | tf_op jit(solution)/shard_map/ppermute | solution.py:32
  12.2 0.6 copy-start.14
  15.3 43.9 %collective-permute-start.1 = (bf16[1632,256]{1,0:T(8,128)(2,1)}, bf16[1632,256]{1,0:T(8,128)(2,1)S(1)}, u32[]{:S(2)}, u32[]{:S(2)}) collective-permute-start(bf16[1632,256]{1,0:T(8,128)(2,1)} %shard_map.121), channel_id=1, source_target_pairs={{0,0},{1,1},{2,2},{3,3},{4,8},{5,9},{6,10},{7,11},{8,4},{9,5},{10,... | collective-permute-start | bytes 2506760 | tf_op jit(solution)/shard_map/ppermute | solution.py:32
  59.2 18.7 %copy-start.6 = (bf16[1632,256]{1,0:T(8,128)(2,1)}, bf16[1632,256]{1,0:T(8,128)(2,1)S(1)}, u32[]{:S(2)}) copy-start(bf16[1632,256]{1,0:T(8,128)(2,1)S(1)} %collective-permute-done.1.refs_1_) | copy-start | bytes 2506756
  60.0 37.2 %all-to-all-start.1 = ((bf16[8,96,256]{2,1,0:T(8,128)(2,1)}), bf16[8,96,256]{2,1,0:T(8,128)(2,1)S(1)}, u32[]{:S(2)}, u32[]{:S(2)}) async-start(bf16[8,96,256]{2,1,0:T(8,128)(2,1)} %broadcast_in_dim.15), calls=%async_computation.1 | async-start | bytes 786432 | tf_op jit(solution)/shard_map/all_to_all | solution.py:368
  77.9 33.5 %collective-permute-start.2 = (bf16[8,3,128,128]{3,2,1,0:T(8,128)(2,1)}, bf16[8,3,128,128]{3,2,1,0:T(8,128)(2,1)}, u32[]{:S(2)}, u32[]{:S(2)}) collective-permute-start(bf16[8,3,128,128]{3,2,1,0:T(8,128)(2,1)} %shard_map.122), channel_id=1, source_target_pairs={{0,0},{1,1},{2,2},{3,3},{4,8},{5,9},{6,10},{7,11},{8,4},{9,5},{10,... | collective-permute-start | bytes 2359304 | tf_op jit(solution)/shard_map/ppermute | solution.py:32
  87.1 26.2 %collective-permute-start.3 = (bf16[12,128,256]{2,1,0:T(8,128)(2,1)S(1)}, bf16[12,128,256]{2,1,0:T(8,128)(2,1)S(1)}, u32[]{:S(2)}, u32[]{:S(2)}) collective-permute-start(bf16[12,128,256]{2,1,0:T(8,128)(2,1)S(1)} %bitcast.41), channel_id=1, source_target_pairs={{0,1},{1,2},{2,3},{3,0},{4,5},{5,6},{6,7},{7,4},{8,9},{9,10},{10,1... | collective-permute-start | bytes 2359304 | tf_op jit(solution)/shard_map/ppermute | solution.py:32
  90.4 25.4 %collective-permute-start.4 = (bf16[12,128,256]{2,1,0:T(8,128)(2,1)S(1)}, bf16[12,128,256]{2,1,0:T(8,128)(2,1)S(1)}, u32[]{:S(2)}, u32[]{:S(2)}) collective-permute-start(bf16[12,128,256]{2,1,0:T(8,128)(2,1)S(1)} %bitcast.42), channel_id=1, source_target_pairs={{0,3},{1,0},{2,1},{3,2},{4,7},{5,4},{6,5},{7,6},{8,11},{9,8},{10,9... | collective-permute-start | bytes 2359304 | tf_op jit(solution)/shard_map/ppermute | solution.py:32
  93.7 24.0 %collective-permute-start.5 = (bf16[12,128,256]{2,1,0:T(8,128)(2,1)S(1)}, bf16[12,128,256]{2,1,0:T(8,128)(2,1)}, u32[]{:S(2)}, u32[]{:S(2)}) collective-permute-start(bf16[12,128,256]{2,1,0:T(8,128)(2,1)S(1)} %bitcast.43), channel_id=1, source_target_pairs={{0,2},{1,3},{2,0},{3,1},{4,6},{5,7},{6,4},{7,5},{8,10},{9,11},{10,... | collective-permute-start | bytes 2359304 | tf_op jit(solution)/shard_map/ppermute | solution.py:32
  97.3 10.0 %collective-permute-start.10 = (bf16[8,96,256]{2,1,0:T(8,128)(2,1)S(1)}, bf16[8,96,256]{2,1,0:T(8,128)(2,1)S(1)}, u32[]{:S(2)}, u32[]{:S(2)}) collective-permute-start(bf16[8,96,256]{2,1,0:T(8,128)(2,1)S(1)} %all-to-all-done.1), channel_id=1, source_target_pairs={{0,32},{1,33},{2,34},{3,35},{4,36},{5,37},{6,38},{7,39},{8,40},{9,... | collective-permute-start | bytes 1179656 | tf_op jit(solution)/shard_map/ppermute | solution.py:32
  107.3 12.9 %copy-start.9 = (bf16[8,96,256]{2,1,0:T(8,128)(2,1)}, bf16[8,96,256]{2,1,0:T(8,128)(2,1)S(1)}, u32[]{:S(2)}) copy-start(bf16[8,96,256]{2,1,0:T(8,128)(2,1)S(1)} %collective-permute-done.10) | copy-start | bytes 1179652
  107.3 16.5 %copy-start.15 = (f32[128]{0:T(128)S(1)}, f32[128]{0:T(128)}, u32[]{:S(2)}) copy-start(f32[128]{0:T(128)} %param.14) | copy-start | bytes 1540
  107.3 16.5 %copy-start.16 = (f32[128]{0:T(128)S(1)}, f32[128]{0:T(128)}, u32[]{:S(2)}) copy-start(f32[128]{0:T(128)} %param.13) | copy-start | bytes 1540
  108.3 16.9 %collective-permute-start.11 = (bf16[8,2,96,256]{3,2,1,0:T(8,128)(2,1)}, bf16[8,2,96,256]{3,2,1,0:T(8,128)(2,1)}, u32[]{:S(2)}, u32[]{:S(2)}) collective-permute-start(bf16[8,2,96,256]{3,2,1,0:T(8,128)(2,1)} %maximum_select_fusion.1), channel_id=1, source_target_pairs={{0,16},{1,17},{2,18},{3,19},{4,20},{5,21},{6,22},{7,23},{8,24},{9,... | collective-permute-start | bytes 2359304 | tf_op jit(solution)/shard_map/ppermute | solution.py:32
  111.4 26.1 %collective-permute-start.6 = (bf16[12,128,256]{2,1,0:T(8,128)(2,1)S(1)}, bf16[12,128,256]{2,1,0:T(8,128)(2,1)}, u32[]{:S(2)}, u32[]{:S(2)}) collective-permute-start(bf16[12,128,256]{2,1,0:T(8,128)(2,1)S(1)} %bitcast.44), channel_id=1, source_target_pairs={{0,8},{1,9},{2,10},{3,11},{4,12},{5,13},{6,14},{7,15},{8,0},{9,1},... | collective-permute-start | bytes 2359304 | tf_op jit(solution)/shard_map/ppermute | solution.py:32
  113.3 24.1 %collective-permute-start.7 = (bf16[12,128,256]{2,1,0:T(8,128)(2,1)S(1)}, bf16[12,128,256]{2,1,0:T(8,128)(2,1)}, u32[]{:S(2)}, u32[]{:S(2)}) collective-permute-start(bf16[12,128,256]{2,1,0:T(8,128)(2,1)S(1)} %collective-permute-done.3.refs_1_), channel_id=1, source_target_pairs={{0,8},{1,9},{2,10},{3,11},{4,12},{5,13},{6,14},{7,15},{8,0},{9,1},... | collective-permute-start | bytes 2359304 | tf_op jit(solution)/shard_map/ppermute | solution.py:32
  115.8 21.7 %collective-permute-start.8 = (bf16[12,128,256]{2,1,0:T(8,128)(2,1)S(1)}, bf16[12,128,256]{2,1,0:T(8,128)(2,1)}, u32[]{:S(2)}, u32[]{:S(2)}) collective-permute-start(bf16[12,128,256]{2,1,0:T(8,128)(2,1)S(1)} %collective-permute-done.4.refs_2_), channel_id=1, source_target_pairs={{0,8},{1,9},{2,10},{3,11},{4,12},{5,13},{6,14},{7,15},{8,0},{9,1},... | collective-permute-start | bytes 2359304 | tf_op jit(solution)/shard_map/ppermute | solution.py:32
  117.7 19.8 %collective-permute-start.9 = (bf16[12,128,256]{2,1,0:T(8,128)(2,1)}, bf16[12,128,256]{2,1,0:T(8,128)(2,1)}, u32[]{:S(2)}, u32[]{:S(2)}) collective-permute-start(bf16[12,128,256]{2,1,0:T(8,128)(2,1)} %collective-permute-done.5.refs_3_), channel_id=1, source_target_pairs={{0,8},{1,9},{2,10},{3,11},{4,12},{5,13},{6,14},{7,15},{8,0},{9,1},... | collective-permute-start | bytes 2359304 | tf_op jit(solution)/shard_map/ppermute | solution.py:32
  120.3 16.3 %all-to-all-start = ((bf16[8,3,128,128]{3,2,1,0:T(8,128)(2,1)}), bf16[8,3,128,128]{3,2,1,0:T(8,128)(2,1)S(1)}, u32[]{:S(2)}, u32[]{:S(2)}) async-start(bf16[8,3,128,128]{3,2,1,0:T(8,128)(2,1)} %collective-permute-done.2.refs_1_), calls=%async_computation | async-start | bytes 1572864 | tf_op jit(solution)/shard_map/all_to_all | solution.py:405
  125.2 49.1 %collective-permute-start.13 = (bf16[8,3,128,128]{3,2,1,0:T(8,128)(2,1)}, bf16[8,3,128,128]{3,2,1,0:T(8,128)(2,1)}, u32[]{:S(2)}, u32[]{:S(2)}) collective-permute-start(bf16[8,3,128,128]{3,2,1,0:T(8,128)(2,1)} %shard_map.126), channel_id=1, source_target_pairs={{0,0},{1,1},{2,2},{3,3},{4,8},{5,9},{6,10},{7,11},{8,4},{9,5},{10,... | collective-permute-start | bytes 2359304 | tf_op jit(solution)/shard_map/ppermute | solution.py:32
  136.6 0.9 copy-start.3
  137.5 1.4 copy-start.2
  138.9 4.7 %copy-start.4 = (bf16[8,3,128,128]{3,2,1,0:T(8,128)(2,1)S(1)}, bf16[8,3,128,128]{3,2,1,0:T(8,128)(2,1)}, u32[]{:S(2)}) copy-start(bf16[8,3,128,128]{3,2,1,0:T(8,128)(2,1)} %copy-done.3) | copy-start | bytes 2359300
  166.9 43.1 %collective-permute-start.12 = (bf16[8,384,128]{2,1,0:T(8,128)(2,1)}, bf16[8,384,128]{2,1,0:T(8,128)(2,1)}, u32[]{:S(2)}, u32[]{:S(2)}) collective-permute-start(bf16[8,384,128]{2,1,0:T(8,128)(2,1)} %all_to_all.35.refs_1_), channel_id=1, source_target_pairs={{0,0},{1,1},{2,2},{3,3},{4,8},{5,9},{6,10},{7,11},{8,4},{9,5},{10,... | collective-permute-start | bytes 2359304 | tf_op jit(solution)/shard_map/ppermute | solution.py:32
  197.2 0.9 copy-start.5
  198.1 9.8 %all-to-all-start.4 = ((bf16[8,16,128]{2,1,0:T(8,128)(2,1)}), bf16[8,16,128]{2,1,0:T(8,128)(2,1)S(1)}, u32[]{:S(2)}, u32[]{:S(2)}) async-start(bf16[8,16,128]{2,1,0:T(8,128)(2,1)} %get-tuple-element.25), calls=%async_computation.4 | async-start | bytes 65536 | tf_op jit(solution)/shard_map/all_to_all | solution.py:412
  206.7 1.2 copy-start
  207.9 0.6 copy-start.13
  210.0 24.1 %copy-start.1 = (bf16[4,8,208,128]{3,2,1,0:T(8,128)(2,1)S(1)}, bf16[4,8,208,128]{3,2,1,0:T(8,128)(2,1)}, u32[]{:S(2)}) copy-start(bf16[4,8,208,128]{3,2,1,0:T(8,128)(2,1)} %shard_map.130.refs_2_) | copy-start | bytes 5111812
  227.2 36.6 %collective-permute-start.14 = (bf16[8,384,128]{2,1,0:T(8,128)(2,1)}, bf16[8,384,128]{2,1,0:T(8,128)(2,1)S(1)}, u32[]{:S(2)}, u32[]{:S(2)}) collective-permute-start(bf16[8,384,128]{2,1,0:T(8,128)(2,1)} %all_to_all.37), channel_id=1, source_target_pairs={{0,0},{1,1},{2,2},{3,3},{4,8},{5,9},{6,10},{7,11},{8,4},{9,5},{10,... | collective-permute-start | bytes 2359304 | tf_op jit(solution)/shard_map/ppermute | solution.py:32
  235.0 13.8 %collective-permute-start.15 = (bf16[8,208,128]{2,1,0:T(8,128)(2,1)S(1)}, bf16[8,208,128]{2,1,0:T(8,128)(2,1)S(1)}, u32[]{:S(2)}, u32[]{:S(2)}) collective-permute-start(bf16[8,208,128]{2,1,0:T(8,128)(2,1)S(1)} %get-tuple-element.33), channel_id=1, source_target_pairs={{0,16},{1,17},{2,18},{3,19},{4,20},{5,21},{6,22},{7,23},{8,24},{9,... | collective-permute-start | bytes 1277960 | tf_op jit(solution)/shard_map/ppermute | solution.py:32
  237.2 17.7 %collective-permute-start.16 = (bf16[8,208,128]{2,1,0:T(8,128)(2,1)S(1)}, bf16[8,208,128]{2,1,0:T(8,128)(2,1)S(1)}, u32[]{:S(2)}, u32[]{:S(2)}) collective-permute-start(bf16[8,208,128]{2,1,0:T(8,128)(2,1)S(1)} %get-tuple-element.32), channel_id=1, source_target_pairs={{0,32},{1,33},{2,34},{3,35},{4,36},{5,37},{6,38},{7,39},{8,40},{9,... | collective-permute-start | bytes 1277960 | tf_op jit(solution)/shard_map/ppermute | solution.py:32
  241.8 18.9 %collective-permute-start.17 = (bf16[8,208,128]{2,1,0:T(8,128)(2,1)S(1)}, bf16[8,208,128]{2,1,0:T(8,128)(2,1)S(1)}, u32[]{:S(2)}, u32[]{:S(2)}) collective-permute-start(bf16[8,208,128]{2,1,0:T(8,128)(2,1)S(1)} %get-tuple-element.31), channel_id=1, source_target_pairs={{0,48},{1,49},{2,50},{3,51},{4,52},{5,53},{6,54},{7,55},{8,56},{9,... | collective-permute-start | bytes 1277960 | tf_op jit(solution)/shard_map/ppermute | solution.py:32
  248.8 11.9 %copy-start.10 = (bf16[8,208,128]{2,1,0:T(8,128)(2,1)}, bf16[8,208,128]{2,1,0:T(8,128)(2,1)S(1)}, u32[]{:S(2)}) copy-start(bf16[8,208,128]{2,1,0:T(8,128)(2,1)S(1)} %collective-permute-done.15.refs_1_) | copy-start | bytes 1277956
  254.9 5.8 %copy-start.11 = (bf16[8,208,128]{2,1,0:T(8,128)(2,1)}, bf16[8,208,128]{2,1,0:T(8,128)(2,1)S(1)}, u32[]{:S(2)}) copy-start(bf16[8,208,128]{2,1,0:T(8,128)(2,1)S(1)} %collective-permute-done.16.refs_2_) | copy-start | bytes 1277956
  260.7 0.8 copy-start.12
  263.8 0.9 copy-start.7
  264.7 48.6 %all-to-all-start.6 = ((bf16[8,208,128]{2,1,0:T(8,128)(2,1)}), bf16[8,208,128]{2,1,0:T(8,128)(2,1)S(1)}, u32[]{:S(2)}, u32[]{:S(2)}) async-start(bf16[8,208,128]{2,1,0:T(8,128)(2,1)} %shard_map.134), calls=%async_computation.6 | async-start | bytes 851968 | tf_op jit(solution)/shard_map/all_to_all | solution.py:418
  313.3 0.8 copy-start.8
  315.8 15.5 %collective-permute-start.18 = (f32[56,256]{1,0:T(8,128)}, f32[56,256]{1,0:T(8,128)S(1)}, u32[]{:S(2)}, u32[]{:S(2)}) collective-permute-start(f32[56,256]{1,0:T(8,128)} %get-tuple-element.29), channel_id=1, source_target_pairs={{0,0},{1,1},{2,2},{3,3},{4,8},{5,9},{6,10},{7,11},{8,4},{9,5},{10,... | collective-permute-start | bytes 172040 | tf_op jit(solution)/shard_map/ppermute | solution.py:32
  321.6 9.7 %collective-permute-start.19 = (f32[56,256]{1,0:T(8,128)}, f32[56,256]{1,0:T(8,128)S(1)}, u32[]{:S(2)}, u32[]{:S(2)}) collective-permute-start(f32[56,256]{1,0:T(8,128)} %get-tuple-element.30), channel_id=1, source_target_pairs={{0,8},{1,9},{2,10},{3,11},{4,0},{5,1},{6,2},{7,3},{8,12},{9,13},{1... | collective-permute-start | bytes 172040 | tf_op jit(solution)/shard_map/ppermute | solution.py:32

commit v3 on v2

--- a/solution.py
+++ b/solution.py
@@ -32,12 +32,18 @@
     return lax.ppermute(field, AXES, pairs)
 
 
+def moved_where(field, where, chosen):
+    number = lambda place: int(np.ravel_multi_index(place, SIZES))
+    pairs = [(number(place), number(where(*place))) for place in PLACES if chosen(*place)]
+    return lax.ppermute(field, AXES, pairs)
+
+
 def clip_swap(l, x, c, h, y):
     return (l, x, h, c, y)
 
 
-def clip_cross(l, x, c, h, y):
-    return (l, x, 1 - h, c, y)
+def z_swap(l, x, c, h, y):
+    return (l, x, c, 1 - h, y)
 
 
 def core_swap(l, x, c, h, y):
@@ -336,31 +342,26 @@
     )(*terms)
 
 
-def second_sum_kernel(zhi_ref, in_ref, straight_ref, across_ref):
+def second_sum_kernel(in_ref, out_ref):
     total = sum(in_ref[j].astype(F32) for j in range(8))
     half = BLOCK // 2
     at = 2 * BLOCK
     gain = total[at : at + 2] + total[at + 2 : at + 4]
     row = jnp.concatenate([gain[0:1], gain[1:2]], axis=1)
-    low_here = zhi_ref[0] == 0
-    for ref in (straight_ref, across_ref):
-        ref[half : half + 8] = jnp.broadcast_to(row, (8, 2 * HEAD))
-    for head in range(2):
-        lanes = slice(head * HEAD, (head + 1) * HEAD)
-        low = total[head * BLOCK : head * BLOCK + half]
-        high = total[head * BLOCK + half : (head + 1) * BLOCK]
-        straight_ref[0:half, lanes] = jnp.where(low_here, low, high)
-        across_ref[0:half, lanes] = jnp.where(low_here, high, low)
-
-
-def second_sum(zhi, field):
-    shape = jax.ShapeDtypeStruct((BLOCK // 2 + 8, 2 * HEAD), F32)
+    for part in range(2):
+        for head in range(2):
+            rows = head * BLOCK + part * half
+            out_ref[part, 0:half, head * HEAD : (head + 1) * HEAD] = total[rows : rows + half]
+        out_ref[part, half : half + 8] = jnp.broadcast_to(row, (8, 2 * HEAD))
+
+
+def second_sum(field):
     return pl.pallas_call(
         second_sum_kernel,
-        out_shape=(shape, shape),
-        in_specs=[pl.BlockSpec(memory_space=pltpu.SMEM), whole()],
-        out_specs=(whole(), whole()),
-    )(zhi, field)
+        out_shape=jax.ShapeDtypeStruct((2, BLOCK // 2 + 8, 2 * HEAD), F32),
+        in_specs=[whole()],
+        out_specs=whole(),
+    )(field)
 
 
 def spread(columns):
@@ -380,21 +381,21 @@
 
 def local(query_in, key_in, value_in, velocity_grad, velocity_gap, query_gain, key_gain, out_proj):
     core, zhi, y = lax.axis_index("core"), lax.axis_index("zhi"), lax.axis_index("y")
-    first, second = prepare(query_in[0], key_in[0], value_in[0])
+    first_raw, second = prepare(query_in[0], key_in[0], value_in[0])
     own = out_proj.T
     formed = form(
         jnp.stack([core]).astype(jnp.int32),
         velocity_grad[0],
         velocity_gap[0],
         own,
-        after(moved(own, core_swap), first, second),
+        moved(own, core_swap),
     )
 
     formed = moved(formed, clip_swap)
     d_velocity = formed[: PARTS * ROWS].reshape(PARTS, ROWS, 256)
-    first = moved(after(first, formed), clip_swap)
+    first = moved(after(first_raw, formed), clip_swap)
     blocks = [d_velocity] + [moved(d_velocity, y_step(step)) for step in (1, 3, 2)]
-    weight = spread(formed[PARTS * ROWS :]).reshape(-1, 2 * HEAD)
+    weight = spread(after(formed[PARTS * ROWS :], first_raw)).reshape(-1, 2 * HEAD)
     blocks = blocks + [moved(block, core_swap) for block in blocks]
     from_y = [y, (y + 3) % 4, (y + 1) % 4, (y + 2) % 4]
     order = [core * 4 + at for at in from_y] + [(1 - core) * 4 + at for at in from_y]
@@ -411,13 +412,16 @@
     second_out, second_grad, tails = attend(1, second_in, d_out, gains, first_gain)
     tails = lax.all_to_all(tails, ("core", "y"), 0, 0)
     terms = add_tail(weigh(order, blocks, (first_out, second_out)), tails)
-    second_grad = after(second_grad, first_back, terms)
+    terms = after(terms, first_back)
     second_back = lax.all_to_all(second_grad, ("core", "y"), 0, 0)
-    second_back = moved(second_back, clip_swap)
+    second_back = moved(after(second_back, terms), clip_swap)
     terms = first_sum([terms[0]] + [moved(terms[i], x_step(i)) for i in (1, 2, 3)])
     terms = lax.all_to_all(after(terms, second_back), "zlo", 0, 0)
-    straight, across = second_sum(jnp.stack([zhi]).astype(jnp.int32), terms)
-    total = moved(straight, clip_swap) + moved(across, clip_cross)
+    total = second_sum(terms)
+    total = total + moved_where(total, z_swap, lambda l, x, c, h, y: c != h)
+    mine = jnp.where(core == 0, total[0], total[1])
+    other = moved(jnp.where(core == 0, total[1], total[0]), core_swap)
+    total = jnp.where(core == zhi, mine, other)
     grad_out_proj = total[: BLOCK // 2].T
     gain_grads = total[BLOCK // 2].reshape(2, HEAD)
 

time: 335 us -> 330 us (0.985)
  starting transfers between devices: 150 us -> 135 us
  blocking collectives: 50.1 us -> 55.4 us
    all_to_all x2 -> x3, starting transfers between devices: 35.3 us -> 13.8 us  [the longest x1 4.81 us: local(): first_back = lax.all_to_all(first_grad, ('core', 'y'), 0, 0)]
    ppermute x20 -> x19, starting transfers between devices: 93.4 us -> 100 us  [moved(): return lax.ppermute(field, AXES, pairs)]
    ppermute x20 -> x19, waiting for transfers between devices: 60.3 us -> 53.9 us  [moved(): return lax.ppermute(field, AXES, pairs)]
    all_to_all x3 -> x2, blocking collectives: 50.1 us -> 55.4 us  [the longest x1 47.1 us: local(): terms = lax.all_to_all(after(terms, second_back), 'zlo', 0, 0)]
    all_to_all x2 -> x3, waiting for transfers between devices: 17 us -> 21.4 us  [the longest x1 12.3 us: local(): first_back = lax.all_to_all(first_grad, ('core', 'y'), 0, 0)]
    unnamed x34 -> x32, local copies, waits for them, and re-layouts: 8.02 us -> 7.47 us
  transfers between devices with their start and end apart: 24 -> 25, of which waited for: 7 -> 10; matrix products, arithmetic and copies ran while one was open for 2% -> 3% of each run, Pallas kernels for 10% -> 10%
where the time goes in v3:
time: 330 us; the launch traced here: 327 us
  starting transfers between devices  135 us (41%)
  waiting for transfers between devices  77.4 us (23%)
  blocking collectives  55.4 us (17%)
  Pallas kernels  37.3 us (11%)
  local copies, waits for them, and re-layouts  13 us (4%)
  other arithmetic  7.27 us (2%)
    ppermute x19, starting transfers between devices, moved(): return lax.ppermute(field, AXES, pairs)  100 us
    ppermute x19, waiting for transfers between devices, moved(): return lax.ppermute(field, AXES, pairs)  53.9 us
    all_to_all x1, blocking collectives, local(): terms = lax.all_to_all(after(terms, second_back), 'zlo', 0, 0)  47.1 us
    all_to_all x1, starting transfers between devices, spread(): lax.all_to_all(jnp.broadcast_to(columns[None], (8,) + columns.shape), 'zl...  15.9 us
    pallas_call x2, Pallas kernels, attend(): pl.pallas_call(lambda *refs: attend_kernel(head, *refs), out_shape=(jax.S...  13.9 us
    all_to_all x1, waiting for transfers between devices, local(): first_back = lax.all_to_all(first_grad, ('core', 'y'), 0, 0)  12.3 us
    all_to_all x1, blocking collectives, local(): tails = lax.all_to_all(tails, ('core', 'y'), 0, 0)  8.32 us
    unnamed x32, local copies, waits for them, and re-layouts  7.47 us
  transfers between devices with their start and end apart: 25, of which 10 were waited for; matrix products, arithmetic and copies ran while one was open for 3% of the time, Pallas kernels for 10%

profile of v3, /device:TPU:1, one launch (start us, length us, event | category | flops | bytes accessed | tf_op | source)
XLA Modules:
  0.0 326.5 jit_solution(4179454858945679241)
XLA Ops:
  0.6 8.8 %collective-permute-start = (bf16[48,256]{1,0:T(8,128)(2,1)}, bf16[48,256]{1,0:T(8,128)(2,1)S(1)}, u32[]{:S(2)}, u32[]{:S(2)}) collective-permute-start(bf16[48,256]{1,0:T(8,128)(2,1)} %bitcast.57), channel_id=1, source_target_pairs={{0,8},{1,9},{2,10},{3,11},{4,12},{5,13},{6,14},{7,15},{8,0},{9,1},... | collective-permute-start | bytes 73736 | tf_op jit(solution)/shard_map/ppermute | solution.py:32
  11.1 2.5 shard_map.120
  13.6 10.3 %collective-permute-start.1 = (bf16[1632,256]{1,0:T(8,128)(2,1)}, bf16[1632,256]{1,0:T(8,128)(2,1)S(1)}, u32[]{:S(2)}, u32[]{:S(2)}) collective-permute-start(bf16[1632,256]{1,0:T(8,128)(2,1)} %shard_map.120), channel_id=1, source_target_pairs={{0,0},{1,1},{2,2},{3,3},{4,8},{5,9},{6,10},{7,11},{8,4},{9,5},{10,... | collective-permute-start | bytes 2506760 | tf_op jit(solution)/shard_map/ppermute | solution.py:32
  23.9 2.8 shard_map.119
  26.7 32.7 %collective-permute-done.1.refs_1_ = bf16[1632,256]{1,0:T(8,128)(2,1)S(1)} collective-permute-done((bf16[1632,256]{1,0:T(8,128)(2,1)}, bf16[1632,256]{1,0:T(8,128)(2,1)S(1)}, u32[]{:S(2)}, u32[]{:S(2)}) %collective-permute-start.1) | collective-permute-done | bytes 835616 | tf_op jit(solution)/shard_map/ppermute | solution.py:32
  60.1 1.6 broadcast_in_dim.15
  61.6 15.9 %all-to-all-start.1 = ((bf16[8,96,256]{2,1,0:T(8,128)(2,1)}), bf16[8,96,256]{2,1,0:T(8,128)(2,1)S(1)}, u32[]{:S(2)}, u32[]{:S(2)}) async-start(bf16[8,96,256]{2,1,0:T(8,128)(2,1)} %broadcast_in_dim.15), calls=%async_computation.1 | async-start | bytes 786432 | tf_op jit(solution)/shard_map/all_to_all | solution.py:369
  77.5 8.5 %collective-permute-start.2 = (bf16[8,3,128,128]{3,2,1,0:T(8,128)(2,1)}, bf16[8,3,128,128]{3,2,1,0:T(8,128)(2,1)S(1)}, u32[]{:S(2)}, u32[]{:S(2)}) collective-permute-start(bf16[8,3,128,128]{3,2,1,0:T(8,128)(2,1)} %shard_map.121), channel_id=1, source_target_pairs={{0,0},{1,1},{2,2},{3,3},{4,8},{5,9},{6,10},{7,11},{8,4},{9,5},{10,... | collective-permute-start | bytes 2359304 | tf_op jit(solution)/shard_map/ppermute | solution.py:32
  87.2 3.2 collective-permute-start.3
  90.4 3.4 %collective-permute-start.4 = (bf16[12,128,256]{2,1,0:T(8,128)(2,1)S(1)}, bf16[12,128,256]{2,1,0:T(8,128)(2,1)S(1)}, u32[]{:S(2)}, u32[]{:S(2)}) collective-permute-start(bf16[12,128,256]{2,1,0:T(8,128)(2,1)S(1)} %bitcast.45), channel_id=1, source_target_pairs={{0,3},{1,0},{2,1},{3,2},{4,7},{5,4},{6,5},{7,6},{8,11},{9,8},{10,9... | collective-permute-start | bytes 2359304 | tf_op jit(solution)/shard_map/ppermute | solution.py:32
  93.7 3.5 %collective-permute-start.5 = (bf16[12,128,256]{2,1,0:T(8,128)(2,1)S(1)}, bf16[12,128,256]{2,1,0:T(8,128)(2,1)}, u32[]{:S(2)}, u32[]{:S(2)}) collective-permute-start(bf16[12,128,256]{2,1,0:T(8,128)(2,1)S(1)} %bitcast.46), channel_id=1, source_target_pairs={{0,2},{1,3},{2,0},{3,1},{4,6},{5,7},{6,4},{7,5},{8,10},{9,11},{10,... | collective-permute-start | bytes 2359304 | tf_op jit(solution)/shard_map/ppermute | solution.py:32
  97.3 4.7 %collective-permute-start.10 = (bf16[8,96,256]{2,1,0:T(8,128)(2,1)S(1)}, bf16[8,96,256]{2,1,0:T(8,128)(2,1)}, u32[]{:S(2)}, u32[]{:S(2)}) collective-permute-start(bf16[8,96,256]{2,1,0:T(8,128)(2,1)S(1)} %all-to-all-done.1), channel_id=1, source_target_pairs={{0,32},{1,33},{2,34},{3,35},{4,36},{5,37},{6,38},{7,39},{8,40},{9,... | collective-permute-start | bytes 1179656 | tf_op jit(solution)/shard_map/ppermute | solution.py:32
  102.0 5.5 %collective-permute-done.10 = bf16[8,96,256]{2,1,0:T(8,128)(2,1)} collective-permute-done((bf16[8,96,256]{2,1,0:T(8,128)(2,1)S(1)}, bf16[8,96,256]{2,1,0:T(8,128)(2,1)}, u32[]{:S(2)}, u32[]{:S(2)}) %collective-permute-start.10) | collective-permute-done | bytes 393248 | tf_op jit(solution)/shard_map/ppermute | solution.py:32
  107.4 2.1 maximum_select_fusion.1
  109.5 3.1 collective-permute-start.11
  112.7 1.9 collective-permute-start.6
  114.6 2.4 collective-permute-start.7
  117.1 1.9 collective-permute-start.8
  119.0 2.4 collective-permute-start.9
  121.5 3.5 %all-to-all-start = ((bf16[8,3,128,128]{3,2,1,0:T(8,128)(2,1)}), bf16[8,3,128,128]{3,2,1,0:T(8,128)(2,1)S(1)}, u32[]{:S(2)}, u32[]{:S(2)}) async-start(bf16[8,3,128,128]{3,2,1,0:T(8,128)(2,1)} %copy-done.9), calls=%async_computation | async-start | bytes 1572864 | tf_op jit(solution)/shard_map/all_to_all | solution.py:406
  126.5 8.1 %collective-permute-start.13 = (bf16[8,3,128,128]{3,2,1,0:T(8,128)(2,1)}, bf16[8,3,128,128]{3,2,1,0:T(8,128)(2,1)}, u32[]{:S(2)}, u32[]{:S(2)}) collective-permute-start(bf16[8,3,128,128]{3,2,1,0:T(8,128)(2,1)} %shard_map.126), channel_id=1, source_target_pairs={{0,0},{1,1},{2,2},{3,3},{4,8},{5,9},{6,10},{7,11},{8,4},{9,5},{10,... | collective-permute-start | bytes 2359304 | tf_op jit(solution)/shard_map/ppermute | solution.py:32
  134.6 2.9 maximum_select_fusion
  139.8 4.6 %shard_map.124.refs_1_ = bf16[2,1024,128]{2,1,0:T(8,128)(2,1)S(1)} custom-call(s32[9]{0:T(128)S(1)} %stack.86.order_ref, bf16[12,128,256]{2,1,0:T(8,128)(2,1)S(1)} %bitcast.48, bf16[12,128,256]{2,1,0:T(8,128)(2,1)S(1)} %collective-permute-done.3.refs_1_, bf16[12,128,256]{2,1,0:T(8,128)(2,1)S(1)} %collective-permute-done.4.refs_2_, ...), custom_call_target="tpu_custom_call" | custom-call | tf_op jit(solution)/shard_map/pallas_call | solution.py:176
  144.5 6.4 %shard_map.125 = (bf16[1024,128]{1,0:T(8,128)(2,1)S(1)}, bf16[8,384,128]{2,1,0:T(8,128)(2,1)S(1)}, f32[2,128]{1,0:T(2,128)S(1)}) custom-call(bf16[8,3,128,128]{3,2,1,0:T(8,128)(2,1)S(1)} %copy-done.4, bf16[2,1024,128]{2,1,0:T(8,128)(2,1)S(1)} %shard_map.124.refs_1_, f32[2,128]{1,0:T(2,128)S(1)} %pad_maximum_fusion.2.refs_2_), custom_call_target="tpu_custom_call" | custom-call | tf_op jit(solution)/shard_map/pallas_call | solution.py:253
  151.8 4.8 %all-to-all-start.2 = ((bf16[8,384,128]{2,1,0:T(8,128)(2,1)}), bf16[8,384,128]{2,1,0:T(8,128)(2,1)}, u32[]{:S(2)}, u32[]{:S(2)}) async-start(bf16[8,384,128]{2,1,0:T(8,128)(2,1)} %copy-done.6), calls=%async_computation.2 | async-start | bytes 1572864 | tf_op jit(solution)/shard_map/all_to_all | solution.py:409
  156.6 12.3 %all-to-all-done.2.refs_1_ = bf16[8,384,128]{2,1,0:T(8,128)(2,1)} async-done(((bf16[8,384,128]{2,1,0:T(8,128)(2,1)}), bf16[8,384,128]{2,1,0:T(8,128)(2,1)}, u32[]{:S(2)}, u32[]{:S(2)}) %all-to-all-start.2) | async-done | bytes 786464 | tf_op jit(solution)/shard_map/all_to_all | solution.py:409
  168.8 4.5 %all-to-all-start.3 = ((bf16[8,3,128,128]{3,2,1,0:T(8,128)(2,1)}), bf16[8,3,128,128]{3,2,1,0:T(8,128)(2,1)}, u32[]{:S(2)}, u32[]{:S(2)}) async-start(bf16[8,3,128,128]{3,2,1,0:T(8,128)(2,1)} %shard_map.127), calls=%async_computation.3 | async-start | bytes 1572864 | tf_op jit(solution)/shard_map/all_to_all | solution.py:410
  173.3 7.8 %collective-permute-start.12 = (bf16[8,384,128]{2,1,0:T(8,128)(2,1)}, bf16[8,384,128]{2,1,0:T(8,128)(2,1)}, u32[]{:S(2)}, u32[]{:S(2)}) collective-permute-start(bf16[8,384,128]{2,1,0:T(8,128)(2,1)} %all-to-all-done.2.refs_1_), channel_id=1, source_target_pairs={{0,0},{1,1},{2,2},{3,3},{4,8},{5,9},{6,10},{7,11},{8,4},{9,5},{10,... | collective-permute-start | bytes 2359304 | tf_op jit(solution)/shard_map/ppermute | solution.py:32
  181.1 4.5 %all-to-all-done.3.refs_0_ = bf16[8,3,128,128]{3,2,1,0:T(8,128)(2,1)} async-done(((bf16[8,3,128,128]{3,2,1,0:T(8,128)(2,1)}), bf16[8,3,128,128]{3,2,1,0:T(8,128)(2,1)}, u32[]{:S(2)}, u32[]{:S(2)}) %all-to-all-start.3) | async-done | bytes 786464 | tf_op jit(solution)/shard_map/all_to_all | solution.py:410
  185.6 7.5 %shard_map.128 = (bf16[1024,128]{1,0:T(8,128)(2,1)S(1)}, bf16[8,384,128]{2,1,0:T(8,128)(2,1)S(1)}, bf16[8,16,128]{2,1,0:T(8,128)(2,1)S(1)}) custom-call(bf16[8,3,128,128]{3,2,1,0:T(8,128)(2,1)} %all-to-all-done.3.refs_0_, bf16[2,1024,128]{2,1,0:T(8,128)(2,1)S(1)} %shard_map.124.refs_1_, f32[2,128]{1,0:T(2,128)S(1)} %pad_maximum_fusion.2.refs_2_, ...), custom_call_target="tpu_custom_call" | custom-call | tf_op jit(solution)/shard_map/pallas_call | solution.py:253
  194.0 8.3 %all_to_all.35.tails_ref = bf16[8,16,128]{2,1,0:T(8,128)(2,1)} all-to-all(bf16[8,16,128]{2,1,0:T(8,128)(2,1)S(1)} %get-tuple-element.23), channel_id=1, replica_groups=mesh['zlo'=8,'x'=4,'core'=2,'zhi'=2,'y'=4] {'core','y'}, dimensions={0} | all-to-all | bytes 65536 | tf_op jit(solution)/shard_map/all_to_all | solution.py:413
  202.3 4.5 %all-to-all-start.4 = ((bf16[8,384,128]{2,1,0:T(8,128)(2,1)}), bf16[8,384,128]{2,1,0:T(8,128)(2,1)}, u32[]{:S(2)}, u32[]{:S(2)}) async-start(bf16[8,384,128]{2,1,0:T(8,128)(2,1)} %copy-done.5), calls=%async_computation.4 | async-start | bytes 1572864 | tf_op jit(solution)/shard_map/all_to_all | solution.py:416
  206.8 4.9 %shard_map.129.terms_ref = bf16[4,8,208,128]{3,2,1,0:T(8,128)(2,1)S(1)} custom-call(s32[9]{0:T(128)S(1)} %stack.86.order_ref, bf16[12,128,256]{2,1,0:T(8,128)(2,1)S(1)} %bitcast.49, bf16[12,128,256]{2,1,0:T(8,128)(2,1)S(1)} %collective-permute-done.3.refs_1_, bf16[12,128,256]{2,1,0:T(8,128)(2,1)S(1)} %collective-permute-done.4.refs_2_, ...), custom_call_target="tpu_custom_call" | custom-call | tf_op jit(solution)/shard_map/pallas_call | solution.py:295
  214.5 4.7 %all-to-all-done.4.refs_0_ = bf16[8,384,128]{2,1,0:T(8,128)(2,1)} async-done(((bf16[8,384,128]{2,1,0:T(8,128)(2,1)}), bf16[8,384,128]{2,1,0:T(8,128)(2,1)}, u32[]{:S(2)}, u32[]{:S(2)}) %all-to-all-start.4) | async-done | bytes 786464 | tf_op jit(solution)/shard_map/all_to_all | solution.py:416
  219.1 7.9 %collective-permute-start.14 = (bf16[8,384,128]{2,1,0:T(8,128)(2,1)}, bf16[8,384,128]{2,1,0:T(8,128)(2,1)S(1)}, u32[]{:S(2)}, u32[]{:S(2)}) collective-permute-start(bf16[8,384,128]{2,1,0:T(8,128)(2,1)} %shard_map.132), channel_id=1, source_target_pairs={{0,0},{1,1},{2,2},{3,3},{4,8},{5,9},{6,10},{7,11},{8,4},{9,5},{10,... | collective-permute-start | bytes 2359304 | tf_op jit(solution)/shard_map/ppermute | solution.py:32
  227.9 2.1 collective-permute-start.15
  230.0 4.7 %collective-permute-start.16 = (bf16[8,208,128]{2,1,0:T(8,128)(2,1)S(1)}, bf16[8,208,128]{2,1,0:T(8,128)(2,1)S(1)}, u32[]{:S(2)}, u32[]{:S(2)}) collective-permute-start(bf16[8,208,128]{2,1,0:T(8,128)(2,1)S(1)} %get-tuple-element.28), channel_id=1, source_target_pairs={{0,32},{1,33},{2,34},{3,35},{4,36},{5,37},{6,38},{7,39},{8,40},{9,... | collective-permute-start | bytes 1277960 | tf_op jit(solution)/shard_map/ppermute | solution.py:32
  234.7 2.8 collective-permute-start.17
  237.5 3.4 %collective-permute-done.15.refs_1_ = bf16[8,208,128]{2,1,0:T(8,128)(2,1)S(1)} collective-permute-done((bf16[8,208,128]{2,1,0:T(8,128)(2,1)S(1)}, bf16[8,208,128]{2,1,0:T(8,128)(2,1)S(1)}, u32[]{:S(2)}, u32[]{:S(2)}) %collective-permute-start.15) | collective-permute-done | bytes 426016 | tf_op jit(solution)/shard_map/ppermute | solution.py:32
  240.9 5.9 %collective-permute-done.16.refs_2_ = bf16[8,208,128]{2,1,0:T(8,128)(2,1)S(1)} collective-permute-done((bf16[8,208,128]{2,1,0:T(8,128)(2,1)S(1)}, bf16[8,208,128]{2,1,0:T(8,128)(2,1)S(1)}, u32[]{:S(2)}, u32[]{:S(2)}) %collective-permute-start.16) | collective-permute-done | bytes 426016 | tf_op jit(solution)/shard_map/ppermute | solution.py:32
  246.8 5.3 %collective-permute-done.17.refs_3_ = bf16[8,208,128]{2,1,0:T(8,128)(2,1)S(1)} collective-permute-done((bf16[8,208,128]{2,1,0:T(8,128)(2,1)S(1)}, bf16[8,208,128]{2,1,0:T(8,128)(2,1)S(1)}, u32[]{:S(2)}, u32[]{:S(2)}) %collective-permute-start.17) | collective-permute-done | bytes 426016 | tf_op jit(solution)/shard_map/ppermute | solution.py:32
  252.9 2.4 shard_map.134.refs_0_
  256.2 47.1 %all_to_all.36.in_ref = bf16[8,208,128]{2,1,0:T(8,128)(2,1)} all-to-all(bf16[8,208,128]{2,1,0:T(8,128)(2,1)} %shard_map.135), channel_id=1, replica_groups=mesh['zlo'=8,'x'=4,'core'=2,'zhi'=2,'y'=4] {'zlo'}, dimensions={0} | all-to-all | bytes 851968 | tf_op jit(solution)/shard_map/all_to_all | solution.py:419
  303.3 1.7 shard_map.136
  305.0 1.8 collective-permute-start.18
  306.8 2.1 collective-permute-done.18
  309.8 12.6 %collective-permute-start.19 = (f32[56,256]{1,0:T(8,128)S(1)}, f32[56,256]{1,0:T(8,128)S(1)}, u32[]{:S(2)}, u32[]{:S(2)}) collective-permute-start(f32[56,256]{1,0:T(8,128)S(1)} %select_bitcast_fusion), channel_id=1, source_target_pairs={{0,8},{1,9},{2,10},{3,11},{4,12},{5,13},{6,14},{7,15},{8,0},{9,1},... | collective-permute-start | bytes 172040 | tf_op jit(solution)/shard_map/ppermute | solution.py:32
  322.4 2.9 shard_map.133
  (69 shorter events, 16.3 us)
Async XLA Ops:
  0.6 9.8 %collective-permute-start = (bf16[48,256]{1,0:T(8,128)(2,1)}, bf16[48,256]{1,0:T(8,128)(2,1)S(1)}, u32[]{:S(2)}, u32[]{:S(2)}) collective-permute-start(bf16[48,256]{1,0:T(8,128)(2,1)} %bitcast.57), channel_id=1, source_target_pairs={{0,8},{1,9},{2,10},{3,11},{4,12},{5,13},{6,14},{7,15},{8,0},{9,1},... | collective-permute-start | bytes 73736 | tf_op jit(solution)/shard_map/ppermute | solution.py:32
  10.5 0.6 copy-start.13
  13.6 45.8 %collective-permute-start.1 = (bf16[1632,256]{1,0:T(8,128)(2,1)}, bf16[1632,256]{1,0:T(8,128)(2,1)S(1)}, u32[]{:S(2)}, u32[]{:S(2)}) collective-permute-start(bf16[1632,256]{1,0:T(8,128)(2,1)} %shard_map.120), channel_id=1, source_target_pairs={{0,0},{1,1},{2,2},{3,3},{4,8},{5,9},{6,10},{7,11},{8,4},{9,5},{10,... | collective-permute-start | bytes 2506760 | tf_op jit(solution)/shard_map/ppermute | solution.py:32
  59.4 18.1 %copy-start.7 = (bf16[1632,256]{1,0:T(8,128)(2,1)}, bf16[1632,256]{1,0:T(8,128)(2,1)S(1)}, u32[]{:S(2)}) copy-start(bf16[1632,256]{1,0:T(8,128)(2,1)S(1)} %collective-permute-done.1.refs_1_) | copy-start | bytes 2506756
  61.6 35.7 %all-to-all-start.1 = ((bf16[8,96,256]{2,1,0:T(8,128)(2,1)}), bf16[8,96,256]{2,1,0:T(8,128)(2,1)S(1)}, u32[]{:S(2)}, u32[]{:S(2)}) async-start(bf16[8,96,256]{2,1,0:T(8,128)(2,1)} %broadcast_in_dim.15), calls=%async_computation.1 | async-start | bytes 786432 | tf_op jit(solution)/shard_map/all_to_all | solution.py:369
  77.5 35.2 %collective-permute-start.2 = (bf16[8,3,128,128]{3,2,1,0:T(8,128)(2,1)}, bf16[8,3,128,128]{3,2,1,0:T(8,128)(2,1)S(1)}, u32[]{:S(2)}, u32[]{:S(2)}) collective-permute-start(bf16[8,3,128,128]{3,2,1,0:T(8,128)(2,1)} %shard_map.121), channel_id=1, source_target_pairs={{0,0},{1,1},{2,2},{3,3},{4,8},{5,9},{6,10},{7,11},{8,4},{9,5},{10,... | collective-permute-start | bytes 2359304 | tf_op jit(solution)/shard_map/ppermute | solution.py:32
  87.2 27.5 %collective-permute-start.3 = (bf16[12,128,256]{2,1,0:T(8,128)(2,1)S(1)}, bf16[12,128,256]{2,1,0:T(8,128)(2,1)S(1)}, u32[]{:S(2)}, u32[]{:S(2)}) collective-permute-start(bf16[12,128,256]{2,1,0:T(8,128)(2,1)S(1)} %bitcast.44), channel_id=1, source_target_pairs={{0,1},{1,2},{2,3},{3,0},{4,5},{5,6},{6,7},{7,4},{8,9},{9,10},{10,1... | collective-permute-start | bytes 2359304 | tf_op jit(solution)/shard_map/ppermute | solution.py:32
  90.4 26.7 %collective-permute-start.4 = (bf16[12,128,256]{2,1,0:T(8,128)(2,1)S(1)}, bf16[12,128,256]{2,1,0:T(8,128)(2,1)S(1)}, u32[]{:S(2)}, u32[]{:S(2)}) collective-permute-start(bf16[12,128,256]{2,1,0:T(8,128)(2,1)S(1)} %bitcast.45), channel_id=1, source_target_pairs={{0,3},{1,0},{2,1},{3,2},{4,7},{5,4},{6,5},{7,6},{8,11},{9,8},{10,9... | collective-permute-start | bytes 2359304 | tf_op jit(solution)/shard_map/ppermute | solution.py:32
  93.7 25.3 %collective-permute-start.5 = (bf16[12,128,256]{2,1,0:T(8,128)(2,1)S(1)}, bf16[12,128,256]{2,1,0:T(8,128)(2,1)}, u32[]{:S(2)}, u32[]{:S(2)}) collective-permute-start(bf16[12,128,256]{2,1,0:T(8,128)(2,1)S(1)} %bitcast.46), channel_id=1, source_target_pairs={{0,2},{1,3},{2,0},{3,1},{4,6},{5,7},{6,4},{7,5},{8,10},{9,11},{10,... | collective-permute-start | bytes 2359304 | tf_op jit(solution)/shard_map/ppermute | solution.py:32
  97.3 10.1 %collective-permute-start.10 = (bf16[8,96,256]{2,1,0:T(8,128)(2,1)S(1)}, bf16[8,96,256]{2,1,0:T(8,128)(2,1)}, u32[]{:S(2)}, u32[]{:S(2)}) collective-permute-start(bf16[8,96,256]{2,1,0:T(8,128)(2,1)S(1)} %all-to-all-done.1), channel_id=1, source_target_pairs={{0,32},{1,33},{2,34},{3,35},{4,36},{5,37},{6,38},{7,39},{8,40},{9,... | collective-permute-start | bytes 1179656 | tf_op jit(solution)/shard_map/ppermute | solution.py:32
  107.4 17.6 %copy-start.14 = (f32[128]{0:T(128)S(1)}, f32[128]{0:T(128)}, u32[]{:S(2)}) copy-start(f32[128]{0:T(128)} %param.14) | copy-start | bytes 1540
  107.4 17.6 %copy-start.15 = (f32[128]{0:T(128)S(1)}, f32[128]{0:T(128)}, u32[]{:S(2)}) copy-start(f32[128]{0:T(128)} %param.13) | copy-start | bytes 1540
  109.5 16.9 %collective-permute-start.11 = (bf16[8,2,96,256]{3,2,1,0:T(8,128)(2,1)}, bf16[8,2,96,256]{3,2,1,0:T(8,128)(2,1)}, u32[]{:S(2)}, u32[]{:S(2)}) collective-permute-start(bf16[8,2,96,256]{3,2,1,0:T(8,128)(2,1)} %maximum_select_fusion.1), channel_id=1, source_target_pairs={{0,16},{1,17},{2,18},{3,19},{4,20},{5,21},{6,22},{7,23},{8,24},{9,... | collective-permute-start | bytes 2359304 | tf_op jit(solution)/shard_map/ppermute | solution.py:32
  112.7 8.8 %copy-start.9 = (bf16[8,3,128,128]{3,2,1,0:T(8,128)(2,1)}, bf16[8,3,128,128]{3,2,1,0:T(8,128)(2,1)S(1)}, u32[]{:S(2)}) copy-start(bf16[8,3,128,128]{3,2,1,0:T(8,128)(2,1)S(1)} %collective-permute-done.2.refs_1_) | copy-start | bytes 2359300
  112.7 25.7 %collective-permute-start.6 = (bf16[12,128,256]{2,1,0:T(8,128)(2,1)S(1)}, bf16[12,128,256]{2,1,0:T(8,128)(2,1)}, u32[]{:S(2)}, u32[]{:S(2)}) collective-permute-start(bf16[12,128,256]{2,1,0:T(8,128)(2,1)S(1)} %bitcast.47), channel_id=1, source_target_pairs={{0,8},{1,9},{2,10},{3,11},{4,12},{5,13},{6,14},{7,15},{8,0},{9,1},... | collective-permute-start | bytes 2359304 | tf_op jit(solution)/shard_map/ppermute | solution.py:32
  114.6 23.8 %collective-permute-start.7 = (bf16[12,128,256]{2,1,0:T(8,128)(2,1)S(1)}, bf16[12,128,256]{2,1,0:T(8,128)(2,1)}, u32[]{:S(2)}, u32[]{:S(2)}) collective-permute-start(bf16[12,128,256]{2,1,0:T(8,128)(2,1)S(1)} %collective-permute-done.3.refs_1_), channel_id=1, source_target_pairs={{0,8},{1,9},{2,10},{3,11},{4,12},{5,13},{6,14},{7,15},{8,0},{9,1},... | collective-permute-start | bytes 2359304 | tf_op jit(solution)/shard_map/ppermute | solution.py:32
  117.1 21.3 %collective-permute-start.8 = (bf16[12,128,256]{2,1,0:T(8,128)(2,1)S(1)}, bf16[12,128,256]{2,1,0:T(8,128)(2,1)}, u32[]{:S(2)}, u32[]{:S(2)}) collective-permute-start(bf16[12,128,256]{2,1,0:T(8,128)(2,1)S(1)} %collective-permute-done.4.refs_2_), channel_id=1, source_target_pairs={{0,8},{1,9},{2,10},{3,11},{4,12},{5,13},{6,14},{7,15},{8,0},{9,1},... | collective-permute-start | bytes 2359304 | tf_op jit(solution)/shard_map/ppermute | solution.py:32
  119.0 19.4 %collective-permute-start.9 = (bf16[12,128,256]{2,1,0:T(8,128)(2,1)}, bf16[12,128,256]{2,1,0:T(8,128)(2,1)}, u32[]{:S(2)}, u32[]{:S(2)}) collective-permute-start(bf16[12,128,256]{2,1,0:T(8,128)(2,1)} %collective-permute-done.5.refs_3_), channel_id=1, source_target_pairs={{0,8},{1,9},{2,10},{3,11},{4,12},{5,13},{6,14},{7,15},{8,0},{9,1},... | collective-permute-start | bytes 2359304 | tf_op jit(solution)/shard_map/ppermute | solution.py:32
  121.5 15.9 %all-to-all-start = ((bf16[8,3,128,128]{3,2,1,0:T(8,128)(2,1)}), bf16[8,3,128,128]{3,2,1,0:T(8,128)(2,1)S(1)}, u32[]{:S(2)}, u32[]{:S(2)}) async-start(bf16[8,3,128,128]{3,2,1,0:T(8,128)(2,1)} %copy-done.9), calls=%async_computation | async-start | bytes 1572864 | tf_op jit(solution)/shard_map/all_to_all | solution.py:406
  126.5 30.1 %collective-permute-start.13 = (bf16[8,3,128,128]{3,2,1,0:T(8,128)(2,1)}, bf16[8,3,128,128]{3,2,1,0:T(8,128)(2,1)}, u32[]{:S(2)}, u32[]{:S(2)}) collective-permute-start(bf16[8,3,128,128]{3,2,1,0:T(8,128)(2,1)} %shard_map.126), channel_id=1, source_target_pairs={{0,0},{1,1},{2,2},{3,3},{4,8},{5,9},{6,10},{7,11},{8,4},{9,5},{10,... | collective-permute-start | bytes 2359304 | tf_op jit(solution)/shard_map/ppermute | solution.py:32
  137.5 0.9 copy-start.3
  138.4 1.4 copy-start.2
  139.8 4.7 %copy-start.4 = (bf16[8,3,128,128]{3,2,1,0:T(8,128)(2,1)S(1)}, bf16[8,3,128,128]{3,2,1,0:T(8,128)(2,1)}, u32[]{:S(2)}) copy-start(bf16[8,3,128,128]{3,2,1,0:T(8,128)(2,1)} %copy-done.3) | copy-start | bytes 2359300
  150.9 0.9 copy-start.6
  151.8 17.1 %all-to-all-start.2 = ((bf16[8,384,128]{2,1,0:T(8,128)(2,1)}), bf16[8,384,128]{2,1,0:T(8,128)(2,1)}, u32[]{:S(2)}, u32[]{:S(2)}) async-start(bf16[8,384,128]{2,1,0:T(8,128)(2,1)} %copy-done.6), calls=%async_computation.2 | async-start | bytes 1572864 | tf_op jit(solution)/shard_map/all_to_all | solution.py:409
  168.8 16.8 %all-to-all-start.3 = ((bf16[8,3,128,128]{3,2,1,0:T(8,128)(2,1)}), bf16[8,3,128,128]{3,2,1,0:T(8,128)(2,1)}, u32[]{:S(2)}, u32[]{:S(2)}) async-start(bf16[8,3,128,128]{3,2,1,0:T(8,128)(2,1)} %shard_map.127), calls=%async_computation.3 | async-start | bytes 1572864 | tf_op jit(solution)/shard_map/all_to_all | solution.py:410
  173.3 41.1 %collective-permute-start.12 = (bf16[8,384,128]{2,1,0:T(8,128)(2,1)}, bf16[8,384,128]{2,1,0:T(8,128)(2,1)}, u32[]{:S(2)}, u32[]{:S(2)}) collective-permute-start(bf16[8,384,128]{2,1,0:T(8,128)(2,1)} %all-to-all-done.2.refs_1_), channel_id=1, source_target_pairs={{0,0},{1,1},{2,2},{3,3},{4,8},{5,9},{6,10},{7,11},{8,4},{9,5},{10,... | collective-permute-start | bytes 2359304 | tf_op jit(solution)/shard_map/ppermute | solution.py:32
  193.1 0.9 copy-start.5
  202.3 16.8 %all-to-all-start.4 = ((bf16[8,384,128]{2,1,0:T(8,128)(2,1)}), bf16[8,384,128]{2,1,0:T(8,128)(2,1)}, u32[]{:S(2)}, u32[]{:S(2)}) async-start(bf16[8,384,128]{2,1,0:T(8,128)(2,1)} %copy-done.5), calls=%async_computation.4 | async-start | bytes 1572864 | tf_op jit(solution)/shard_map/all_to_all | solution.py:416
  211.8 1.2 copy-start
  214.5 12.5 %copy-start.1 = (bf16[4,8,208,128]{3,2,1,0:T(8,128)(2,1)S(1)}, bf16[4,8,208,128]{3,2,1,0:T(8,128)(2,1)}, u32[]{:S(2)}) copy-start(bf16[4,8,208,128]{3,2,1,0:T(8,128)(2,1)} %shard_map.131.refs_1_) | copy-start | bytes 5111812
  219.1 36.1 %collective-permute-start.14 = (bf16[8,384,128]{2,1,0:T(8,128)(2,1)}, bf16[8,384,128]{2,1,0:T(8,128)(2,1)S(1)}, u32[]{:S(2)}, u32[]{:S(2)}) collective-permute-start(bf16[8,384,128]{2,1,0:T(8,128)(2,1)} %shard_map.132), channel_id=1, source_target_pairs={{0,0},{1,1},{2,2},{3,3},{4,8},{5,9},{6,10},{7,11},{8,4},{9,5},{10,... | collective-permute-start | bytes 2359304 | tf_op jit(solution)/shard_map/ppermute | solution.py:32
  227.9 13.0 %collective-permute-start.15 = (bf16[8,208,128]{2,1,0:T(8,128)(2,1)S(1)}, bf16[8,208,128]{2,1,0:T(8,128)(2,1)S(1)}, u32[]{:S(2)}, u32[]{:S(2)}) collective-permute-start(bf16[8,208,128]{2,1,0:T(8,128)(2,1)S(1)} %get-tuple-element.29), channel_id=1, source_target_pairs={{0,16},{1,17},{2,18},{3,19},{4,20},{5,21},{6,22},{7,23},{8,24},{9,... | collective-permute-start | bytes 1277960 | tf_op jit(solution)/shard_map/ppermute | solution.py:32
  230.0 16.8 %collective-permute-start.16 = (bf16[8,208,128]{2,1,0:T(8,128)(2,1)S(1)}, bf16[8,208,128]{2,1,0:T(8,128)(2,1)S(1)}, u32[]{:S(2)}, u32[]{:S(2)}) collective-permute-start(bf16[8,208,128]{2,1,0:T(8,128)(2,1)S(1)} %get-tuple-element.28), channel_id=1, source_target_pairs={{0,32},{1,33},{2,34},{3,35},{4,36},{5,37},{6,38},{7,39},{8,40},{9,... | collective-permute-start | bytes 1277960 | tf_op jit(solution)/shard_map/ppermute | solution.py:32
  234.7 17.4 %collective-permute-start.17 = (bf16[8,208,128]{2,1,0:T(8,128)(2,1)S(1)}, bf16[8,208,128]{2,1,0:T(8,128)(2,1)S(1)}, u32[]{:S(2)}, u32[]{:S(2)}) collective-permute-start(bf16[8,208,128]{2,1,0:T(8,128)(2,1)S(1)} %get-tuple-element.27), channel_id=1, source_target_pairs={{0,48},{1,49},{2,50},{3,51},{4,52},{5,53},{6,54},{7,55},{8,56},{9,... | collective-permute-start | bytes 1277960 | tf_op jit(solution)/shard_map/ppermute | solution.py:32
  240.9 11.2 %copy-start.10 = (bf16[8,208,128]{2,1,0:T(8,128)(2,1)}, bf16[8,208,128]{2,1,0:T(8,128)(2,1)S(1)}, u32[]{:S(2)}) copy-start(bf16[8,208,128]{2,1,0:T(8,128)(2,1)S(1)} %collective-permute-done.15.refs_1_) | copy-start | bytes 1277956
  246.8 5.3 %copy-start.11 = (bf16[8,208,128]{2,1,0:T(8,128)(2,1)}, bf16[8,208,128]{2,1,0:T(8,128)(2,1)S(1)}, u32[]{:S(2)}) copy-start(bf16[8,208,128]{2,1,0:T(8,128)(2,1)S(1)} %collective-permute-done.16.refs_2_) | copy-start | bytes 1277956
  252.1 0.8 copy-start.12
  255.3 0.9 copy-start.8
  305.0 3.9 %collective-permute-start.18 = (f32[2,56,256]{2,1,0:T(8,128)}, f32[2,56,256]{2,1,0:T(8,128)S(1)}, u32[]{:S(2)}, u32[]{:S(2)}) collective-permute-start(f32[2,56,256]{2,1,0:T(8,128)} %shard_map.136), channel_id=1, source_target_pairs={{4,0},{5,1},{6,2},{7,3},{8,12},{9,13},{10,14},{11,15},{20,16},{21,... | collective-permute-start | bytes 344072 | tf_op jit(solution)/shard_map/ppermute | solution.py:38
  309.8 15.5 %collective-permute-start.19 = (f32[56,256]{1,0:T(8,128)S(1)}, f32[56,256]{1,0:T(8,128)S(1)}, u32[]{:S(2)}, u32[]{:S(2)}) collective-permute-start(f32[56,256]{1,0:T(8,128)S(1)} %select_bitcast_fusion), channel_id=1, source_target_pairs={{0,8},{1,9},{2,10},{3,11},{4,12},{5,13},{6,14},{7,15},{8,0},{9,1},... | collective-permute-start | bytes 172040 | tf_op jit(solution)/shard_map/ppermute | solution.py:32

commit v4 on v3

--- a/solution.py
+++ b/solution.py
@@ -117,27 +117,40 @@
     )(first, second)
 
 
-def form_kernel(core_ref, grad_ref, gap_ref, own_ref, other_ref, out_ref):
+def form_kernel(grad_ref, gap_ref, out_ref):
     for j in range(PARTS):
         at = slice(j * 256, (j + 1) * 256)
         out_ref[j * ROWS : (j + 1) * ROWS] = (
             grad_ref[:, at].astype(F32) + kl_weight * gap_ref[:, at].astype(F32)
         ).astype(BF)
+
+
+def append_kernel(core_ref, formed_ref, own_ref, other_ref, out_ref, sems):
     half = BLOCK // 2
     core = core_ref[0]
     own_at = pl.multiple_of(PARTS * ROWS + core * half, 16)
     other_at = pl.multiple_of(PARTS * ROWS + (1 - core) * half, 16)
-    out_ref[pl.ds(own_at, half)] = own_ref[...]
-    out_ref[pl.ds(other_at, half)] = other_ref[...]
+    own_copy = pltpu.make_async_copy(own_ref, out_ref.at[pl.ds(own_at, half)], sems.at[0])
+    other_copy = pltpu.make_async_copy(other_ref, out_ref.at[pl.ds(other_at, half)], sems.at[1])
+    own_copy.start()
+    other_copy.start()
+    own_copy.wait()
+    other_copy.wait()
 
 
 def form(core, grad, gap, own, other):
-    return pl.pallas_call(
-        form_kernel,
-        out_shape=jax.ShapeDtypeStruct((PARTS * ROWS + BLOCK, 256), BF),
-        in_specs=[pl.BlockSpec(memory_space=pltpu.SMEM)] + [whole()] * 4,
-        out_specs=whole(),
-    )(core, grad, gap, own, other)
+    shape = jax.ShapeDtypeStruct((PARTS * ROWS + BLOCK, 256), BF)
+    formed = pl.pallas_call(
+        form_kernel, out_shape=shape, in_specs=[whole()] * 2, out_specs=whole()
+    )(grad, gap)
+    return pl.pallas_call(
+        append_kernel,
+        out_shape=shape,
+        in_specs=[pl.BlockSpec(memory_space=pltpu.SMEM), anywhere(), whole(), whole()],
+        out_specs=anywhere(),
+        scratch_shapes=[pltpu.SemaphoreType.DMA((2,))],
+        input_output_aliases={1: 0},
+    )(core, formed, own, other)
 
 
 def gather_blocks(order_ref, blocks, rows, sems):

time: 330 us -> 330 us (level)
  transfers between devices with their start and end apart: 25 -> 25, of which waited for: 10 -> 9; matrix products, arithmetic and copies ran while one was open for 3% -> 3% of each run, Pallas kernels for 10% -> 11%
where the time goes in v4:
time: 330 us; the launch traced here: 327 us
  starting transfers between devices  133 us (40%)
  waiting for transfers between devices  77.3 us (23%)
  blocking collectives  56.2 us (17%)
  Pallas kernels  38.7 us (12%)
  local copies, waits for them, and re-layouts  13 us (4%)
  other arithmetic  7.27 us (2%)
    ppermute x19, starting transfers between devices, moved(): return lax.ppermute(field, AXES, pairs)  99.5 us
    ppermute x19, waiting for transfers between devices, moved(): return lax.ppermute(field, AXES, pairs)  53.8 us
    all_to_all x1, blocking collectives, local(): terms = lax.all_to_all(after(terms, second_back), 'zlo', 0, 0)  47.9 us
    all_to_all x1, starting transfers between devices, spread(): lax.all_to_all(jnp.broadcast_to(columns[None], (8,) + columns.shape), 'zl...  15.3 us
    pallas_call x2, Pallas kernels, attend(): pl.pallas_call(lambda *refs: attend_kernel(head, *refs), out_shape=(jax.S...  13.9 us
    all_to_all x1, waiting for transfers between devices, local(): first_back = lax.all_to_all(first_grad, ('core', 'y'), 0, 0)  12.3 us
    all_to_all x1, blocking collectives, local(): tails = lax.all_to_all(tails, ('core', 'y'), 0, 0)  8.32 us
    unnamed x32, local copies, waits for them, and re-layouts  7.47 us
  transfers between devices with their start and end apart: 25, of which 9 were waited for; matrix products, arithmetic and copies ran while one was open for 3% of the time, Pallas kernels for 11%

profile of v4, /device:TPU:1, one launch (start us, length us, event | category | flops | bytes accessed | tf_op | source)
XLA Modules:
  0.0 326.9 jit_solution(15713877020970063675)
XLA Ops:
  0.6 8.8 %collective-permute-start = (bf16[48,256]{1,0:T(8,128)(2,1)}, bf16[48,256]{1,0:T(8,128)(2,1)S(1)}, u32[]{:S(2)}, u32[]{:S(2)}) collective-permute-start(bf16[48,256]{1,0:T(8,128)(2,1)} %bitcast.57), channel_id=1, source_target_pairs={{0,8},{1,9},{2,10},{3,11},{4,12},{5,13},{6,14},{7,15},{8,0},{9,1},... | collective-permute-start | bytes 73736 | tf_op jit(solution)/shard_map/ppermute | solution.py:32
  9.4 2.5 shard_map.120.formed_ref
  13.9 10.0 %collective-permute-start.1 = (bf16[1632,256]{1,0:T(8,128)(2,1)}, bf16[1632,256]{1,0:T(8,128)(2,1)S(1)}, u32[]{:S(2)}, u32[]{:S(2)}) collective-permute-start(bf16[1632,256]{1,0:T(8,128)(2,1)} %shard_map.121), channel_id=1, source_target_pairs={{0,0},{1,1},{2,2},{3,3},{4,8},{5,9},{6,10},{7,11},{8,4},{9,5},{10,... | collective-permute-start | bytes 2506760 | tf_op jit(solution)/shard_map/ppermute | solution.py:32
  23.9 2.8 shard_map.119
  26.7 33.6 %collective-permute-done.1.refs_1_ = bf16[1632,256]{1,0:T(8,128)(2,1)S(1)} collective-permute-done((bf16[1632,256]{1,0:T(8,128)(2,1)}, bf16[1632,256]{1,0:T(8,128)(2,1)S(1)}, u32[]{:S(2)}, u32[]{:S(2)}) %collective-permute-start.1) | collective-permute-done | bytes 835616 | tf_op jit(solution)/shard_map/ppermute | solution.py:32
  61.0 1.6 broadcast_in_dim.15
  62.6 15.3 %all-to-all-start.1 = ((bf16[8,96,256]{2,1,0:T(8,128)(2,1)}), bf16[8,96,256]{2,1,0:T(8,128)(2,1)S(1)}, u32[]{:S(2)}, u32[]{:S(2)}) async-start(bf16[8,96,256]{2,1,0:T(8,128)(2,1)} %broadcast_in_dim.15), calls=%async_computation.1 | async-start | bytes 786432 | tf_op jit(solution)/shard_map/all_to_all | solution.py:382
  77.9 8.1 %collective-permute-start.2 = (bf16[8,3,128,128]{3,2,1,0:T(8,128)(2,1)}, bf16[8,3,128,128]{3,2,1,0:T(8,128)(2,1)S(1)}, u32[]{:S(2)}, u32[]{:S(2)}) collective-permute-start(bf16[8,3,128,128]{3,2,1,0:T(8,128)(2,1)} %shard_map.122), channel_id=1, source_target_pairs={{0,0},{1,1},{2,2},{3,3},{4,8},{5,9},{6,10},{7,11},{8,4},{9,5},{10,... | collective-permute-start | bytes 2359304 | tf_op jit(solution)/shard_map/ppermute | solution.py:32
  87.2 3.2 collective-permute-start.3
  90.4 3.4 %collective-permute-start.4 = (bf16[12,128,256]{2,1,0:T(8,128)(2,1)S(1)}, bf16[12,128,256]{2,1,0:T(8,128)(2,1)S(1)}, u32[]{:S(2)}, u32[]{:S(2)}) collective-permute-start(bf16[12,128,256]{2,1,0:T(8,128)(2,1)S(1)} %bitcast.45), channel_id=1, source_target_pairs={{0,3},{1,0},{2,1},{3,2},{4,7},{5,4},{6,5},{7,6},{8,11},{9,8},{10,9... | collective-permute-start | bytes 2359304 | tf_op jit(solution)/shard_map/ppermute | solution.py:32
  93.8 3.5 %collective-permute-start.5 = (bf16[12,128,256]{2,1,0:T(8,128)(2,1)S(1)}, bf16[12,128,256]{2,1,0:T(8,128)(2,1)}, u32[]{:S(2)}, u32[]{:S(2)}) collective-permute-start(bf16[12,128,256]{2,1,0:T(8,128)(2,1)S(1)} %bitcast.46), channel_id=1, source_target_pairs={{0,2},{1,3},{2,0},{3,1},{4,6},{5,7},{6,4},{7,5},{8,10},{9,11},{10,... | collective-permute-start | bytes 2359304 | tf_op jit(solution)/shard_map/ppermute | solution.py:32
  97.3 4.7 %collective-permute-start.10 = (bf16[8,96,256]{2,1,0:T(8,128)(2,1)S(1)}, bf16[8,96,256]{2,1,0:T(8,128)(2,1)}, u32[]{:S(2)}, u32[]{:S(2)}) collective-permute-start(bf16[8,96,256]{2,1,0:T(8,128)(2,1)S(1)} %all-to-all-done.1), channel_id=1, source_target_pairs={{0,32},{1,33},{2,34},{3,35},{4,36},{5,37},{6,38},{7,39},{8,40},{9,... | collective-permute-start | bytes 1179656 | tf_op jit(solution)/shard_map/ppermute | solution.py:32
  102.0 5.5 %collective-permute-done.10 = bf16[8,96,256]{2,1,0:T(8,128)(2,1)} collective-permute-done((bf16[8,96,256]{2,1,0:T(8,128)(2,1)S(1)}, bf16[8,96,256]{2,1,0:T(8,128)(2,1)}, u32[]{:S(2)}, u32[]{:S(2)}) %collective-permute-start.10) | collective-permute-done | bytes 393248 | tf_op jit(solution)/shard_map/ppermute | solution.py:32
  107.5 2.1 maximum_select_fusion.1
  109.6 3.1 collective-permute-start.11
  112.7 1.9 collective-permute-start.6
  114.7 2.4 collective-permute-start.7
  117.1 1.9 collective-permute-start.8
  119.0 2.4 collective-permute-start.9
  121.6 3.5 %all-to-all-start = ((bf16[8,3,128,128]{3,2,1,0:T(8,128)(2,1)}), bf16[8,3,128,128]{3,2,1,0:T(8,128)(2,1)S(1)}, u32[]{:S(2)}, u32[]{:S(2)}) async-start(bf16[8,3,128,128]{3,2,1,0:T(8,128)(2,1)} %copy-done.9), calls=%async_computation | async-start | bytes 1572864 | tf_op jit(solution)/shard_map/all_to_all | solution.py:419
  126.5 8.5 %collective-permute-start.13 = (bf16[8,3,128,128]{3,2,1,0:T(8,128)(2,1)}, bf16[8,3,128,128]{3,2,1,0:T(8,128)(2,1)}, u32[]{:S(2)}, u32[]{:S(2)}) collective-permute-start(bf16[8,3,128,128]{3,2,1,0:T(8,128)(2,1)} %shard_map.127), channel_id=1, source_target_pairs={{0,0},{1,1},{2,2},{3,3},{4,8},{5,9},{6,10},{7,11},{8,4},{9,5},{10,... | collective-permute-start | bytes 2359304 | tf_op jit(solution)/shard_map/ppermute | solution.py:32
  135.0 2.9 maximum_select_fusion
  140.2 4.6 %shard_map.125.refs_1_ = bf16[2,1024,128]{2,1,0:T(8,128)(2,1)S(1)} custom-call(s32[9]{0:T(128)S(1)} %stack.86.order_ref, bf16[12,128,256]{2,1,0:T(8,128)(2,1)S(1)} %bitcast.48, bf16[12,128,256]{2,1,0:T(8,128)(2,1)S(1)} %collective-permute-done.3.refs_1_, bf16[12,128,256]{2,1,0:T(8,128)(2,1)S(1)} %collective-permute-done.4.refs_2_, ...), custom_call_target="tpu_custom_call" | custom-call | tf_op jit(solution)/shard_map/pallas_call | solution.py:189
  144.8 6.4 %shard_map.126 = (bf16[1024,128]{1,0:T(8,128)(2,1)S(1)}, bf16[8,384,128]{2,1,0:T(8,128)(2,1)S(1)}, f32[2,128]{1,0:T(2,128)S(1)}) custom-call(bf16[8,3,128,128]{3,2,1,0:T(8,128)(2,1)S(1)} %copy-done.4, bf16[2,1024,128]{2,1,0:T(8,128)(2,1)S(1)} %shard_map.125.refs_1_, f32[2,128]{1,0:T(2,128)S(1)} %pad_maximum_fusion.2.refs_2_), custom_call_target="tpu_custom_call" | custom-call | tf_op jit(solution)/shard_map/pallas_call | solution.py:266
  152.1 4.8 %all-to-all-start.2 = ((bf16[8,384,128]{2,1,0:T(8,128)(2,1)}), bf16[8,384,128]{2,1,0:T(8,128)(2,1)}, u32[]{:S(2)}, u32[]{:S(2)}) async-start(bf16[8,384,128]{2,1,0:T(8,128)(2,1)} %copy-done.6), calls=%async_computation.2 | async-start | bytes 1572864 | tf_op jit(solution)/shard_map/all_to_all | solution.py:422
  156.9 12.3 %all-to-all-done.2.refs_1_ = bf16[8,384,128]{2,1,0:T(8,128)(2,1)} async-done(((bf16[8,384,128]{2,1,0:T(8,128)(2,1)}), bf16[8,384,128]{2,1,0:T(8,128)(2,1)}, u32[]{:S(2)}, u32[]{:S(2)}) %all-to-all-start.2) | async-done | bytes 786464 | tf_op jit(solution)/shard_map/all_to_all | solution.py:422
  169.2 4.5 %all-to-all-start.3 = ((bf16[8,3,128,128]{3,2,1,0:T(8,128)(2,1)}), bf16[8,3,128,128]{3,2,1,0:T(8,128)(2,1)}, u32[]{:S(2)}, u32[]{:S(2)}) async-start(bf16[8,3,128,128]{3,2,1,0:T(8,128)(2,1)} %shard_map.128), calls=%async_computation.3 | async-start | bytes 1572864 | tf_op jit(solution)/shard_map/all_to_all | solution.py:423
  173.7 7.8 %collective-permute-start.12 = (bf16[8,384,128]{2,1,0:T(8,128)(2,1)}, bf16[8,384,128]{2,1,0:T(8,128)(2,1)}, u32[]{:S(2)}, u32[]{:S(2)}) collective-permute-start(bf16[8,384,128]{2,1,0:T(8,128)(2,1)} %all-to-all-done.2.refs_1_), channel_id=1, source_target_pairs={{0,0},{1,1},{2,2},{3,3},{4,8},{5,9},{6,10},{7,11},{8,4},{9,5},{10,... | collective-permute-start | bytes 2359304 | tf_op jit(solution)/shard_map/ppermute | solution.py:32
  181.5 4.5 %all-to-all-done.3.refs_0_ = bf16[8,3,128,128]{3,2,1,0:T(8,128)(2,1)} async-done(((bf16[8,3,128,128]{3,2,1,0:T(8,128)(2,1)}), bf16[8,3,128,128]{3,2,1,0:T(8,128)(2,1)}, u32[]{:S(2)}, u32[]{:S(2)}) %all-to-all-start.3) | async-done | bytes 786464 | tf_op jit(solution)/shard_map/all_to_all | solution.py:423
  186.0 7.5 %shard_map.129 = (bf16[1024,128]{1,0:T(8,128)(2,1)S(1)}, bf16[8,384,128]{2,1,0:T(8,128)(2,1)S(1)}, bf16[8,16,128]{2,1,0:T(8,128)(2,1)S(1)}) custom-call(bf16[8,3,128,128]{3,2,1,0:T(8,128)(2,1)} %all-to-all-done.3.refs_0_, bf16[2,1024,128]{2,1,0:T(8,128)(2,1)S(1)} %shard_map.125.refs_1_, f32[2,128]{1,0:T(2,128)S(1)} %pad_maximum_fusion.2.refs_2_, ...), custom_call_target="tpu_custom_call" | custom-call | tf_op jit(solution)/shard_map/pallas_call | solution.py:266
  194.4 8.3 %all_to_all.35.tails_ref = bf16[8,16,128]{2,1,0:T(8,128)(2,1)} all-to-all(bf16[8,16,128]{2,1,0:T(8,128)(2,1)S(1)} %get-tuple-element.23), channel_id=1, replica_groups=mesh['zlo'=8,'x'=4,'core'=2,'zhi'=2,'y'=4] {'core','y'}, dimensions={0} | all-to-all | bytes 65536 | tf_op jit(solution)/shard_map/all_to_all | solution.py:426
  202.7 4.5 %all-to-all-start.4 = ((bf16[8,384,128]{2,1,0:T(8,128)(2,1)}), bf16[8,384,128]{2,1,0:T(8,128)(2,1)}, u32[]{:S(2)}, u32[]{:S(2)}) async-start(bf16[8,384,128]{2,1,0:T(8,128)(2,1)} %copy-done.5), calls=%async_computation.4 | async-start | bytes 1572864 | tf_op jit(solution)/shard_map/all_to_all | solution.py:429
  207.2 4.9 %shard_map.130.terms_ref = bf16[4,8,208,128]{3,2,1,0:T(8,128)(2,1)S(1)} custom-call(s32[9]{0:T(128)S(1)} %stack.86.order_ref, bf16[12,128,256]{2,1,0:T(8,128)(2,1)S(1)} %bitcast.49, bf16[12,128,256]{2,1,0:T(8,128)(2,1)S(1)} %collective-permute-done.3.refs_1_, bf16[12,128,256]{2,1,0:T(8,128)(2,1)S(1)} %collective-permute-done.4.refs_2_, ...), custom_call_target="tpu_custom_call" | custom-call | tf_op jit(solution)/shard_map/pallas_call | solution.py:308
  213.3 1.5 shard_map.131.refs_0_
  214.8 4.7 %all-to-all-done.4.refs_0_ = bf16[8,384,128]{2,1,0:T(8,128)(2,1)} async-done(((bf16[8,384,128]{2,1,0:T(8,128)(2,1)}), bf16[8,384,128]{2,1,0:T(8,128)(2,1)}, u32[]{:S(2)}, u32[]{:S(2)}) %all-to-all-start.4) | async-done | bytes 786464 | tf_op jit(solution)/shard_map/all_to_all | solution.py:429
  219.5 7.9 %collective-permute-start.14 = (bf16[8,384,128]{2,1,0:T(8,128)(2,1)}, bf16[8,384,128]{2,1,0:T(8,128)(2,1)S(1)}, u32[]{:S(2)}, u32[]{:S(2)}) collective-permute-start(bf16[8,384,128]{2,1,0:T(8,128)(2,1)} %shard_map.133), channel_id=1, source_target_pairs={{0,0},{1,1},{2,2},{3,3},{4,8},{5,9},{6,10},{7,11},{8,4},{9,5},{10,... | collective-permute-start | bytes 2359304 | tf_op jit(solution)/shard_map/ppermute | solution.py:32
  228.2 2.2 collective-permute-start.15
  230.4 4.7 %collective-permute-start.16 = (bf16[8,208,128]{2,1,0:T(8,128)(2,1)S(1)}, bf16[8,208,128]{2,1,0:T(8,128)(2,1)S(1)}, u32[]{:S(2)}, u32[]{:S(2)}) collective-permute-start(bf16[8,208,128]{2,1,0:T(8,128)(2,1)S(1)} %get-tuple-element.28), channel_id=1, source_target_pairs={{0,32},{1,33},{2,34},{3,35},{4,36},{5,37},{6,38},{7,39},{8,40},{9,... | collective-permute-start | bytes 1277960 | tf_op jit(solution)/shard_map/ppermute | solution.py:32
  235.1 2.8 collective-permute-start.17
  237.8 3.4 %collective-permute-done.15.refs_1_ = bf16[8,208,128]{2,1,0:T(8,128)(2,1)S(1)} collective-permute-done((bf16[8,208,128]{2,1,0:T(8,128)(2,1)S(1)}, bf16[8,208,128]{2,1,0:T(8,128)(2,1)S(1)}, u32[]{:S(2)}, u32[]{:S(2)}) %collective-permute-start.15) | collective-permute-done | bytes 426016 | tf_op jit(solution)/shard_map/ppermute | solution.py:32
  241.3 5.9 %collective-permute-done.16.refs_2_ = bf16[8,208,128]{2,1,0:T(8,128)(2,1)S(1)} collective-permute-done((bf16[8,208,128]{2,1,0:T(8,128)(2,1)S(1)}, bf16[8,208,128]{2,1,0:T(8,128)(2,1)S(1)}, u32[]{:S(2)}, u32[]{:S(2)}) %collective-permute-start.16) | collective-permute-done | bytes 426016 | tf_op jit(solution)/shard_map/ppermute | solution.py:32
  247.2 5.3 %collective-permute-done.17.refs_3_ = bf16[8,208,128]{2,1,0:T(8,128)(2,1)S(1)} collective-permute-done((bf16[8,208,128]{2,1,0:T(8,128)(2,1)S(1)}, bf16[8,208,128]{2,1,0:T(8,128)(2,1)S(1)}, u32[]{:S(2)}, u32[]{:S(2)}) %collective-permute-start.17) | collective-permute-done | bytes 426016 | tf_op jit(solution)/shard_map/ppermute | solution.py:32
  253.3 2.4 shard_map.135.refs_0_
  256.5 47.9 %all_to_all.36.in_ref = bf16[8,208,128]{2,1,0:T(8,128)(2,1)} all-to-all(bf16[8,208,128]{2,1,0:T(8,128)(2,1)} %shard_map.136), channel_id=1, replica_groups=mesh['zlo'=8,'x'=4,'core'=2,'zhi'=2,'y'=4] {'zlo'}, dimensions={0} | all-to-all | bytes 851968 | tf_op jit(solution)/shard_map/all_to_all | solution.py:432
  304.4 1.7 shard_map.137
  307.4 2.1 collective-permute-done.18
  310.4 12.4 %collective-permute-start.19 = (f32[56,256]{1,0:T(8,128)S(1)}, f32[56,256]{1,0:T(8,128)S(1)}, u32[]{:S(2)}, u32[]{:S(2)}) collective-permute-start(f32[56,256]{1,0:T(8,128)S(1)} %select_bitcast_fusion), channel_id=1, source_target_pairs={{0,8},{1,9},{2,10},{3,11},{4,12},{5,13},{6,14},{7,15},{8,0},{9,1},... | collective-permute-start | bytes 172040 | tf_op jit(solution)/shard_map/ppermute | solution.py:32
  322.8 2.9 shard_map.134
  (70 shorter events, 16.5 us)
Async XLA Ops:
  0.6 11.3 %collective-permute-start = (bf16[48,256]{1,0:T(8,128)(2,1)}, bf16[48,256]{1,0:T(8,128)(2,1)S(1)}, u32[]{:S(2)}, u32[]{:S(2)}) collective-permute-start(bf16[48,256]{1,0:T(8,128)(2,1)} %bitcast.57), channel_id=1, source_target_pairs={{0,8},{1,9},{2,10},{3,11},{4,12},{5,13},{6,14},{7,15},{8,0},{9,1},... | collective-permute-start | bytes 73736 | tf_op jit(solution)/shard_map/ppermute | solution.py:32
  11.9 0.6 copy-start.13
  13.9 46.4 %collective-permute-start.1 = (bf16[1632,256]{1,0:T(8,128)(2,1)}, bf16[1632,256]{1,0:T(8,128)(2,1)S(1)}, u32[]{:S(2)}, u32[]{:S(2)}) collective-permute-start(bf16[1632,256]{1,0:T(8,128)(2,1)} %shard_map.121), channel_id=1, source_target_pairs={{0,0},{1,1},{2,2},{3,3},{4,8},{5,9},{6,10},{7,11},{8,4},{9,5},{10,... | collective-permute-start | bytes 2506760 | tf_op jit(solution)/shard_map/ppermute | solution.py:32
  60.3 17.5 %copy-start.7 = (bf16[1632,256]{1,0:T(8,128)(2,1)}, bf16[1632,256]{1,0:T(8,128)(2,1)S(1)}, u32[]{:S(2)}) copy-start(bf16[1632,256]{1,0:T(8,128)(2,1)S(1)} %collective-permute-done.1.refs_1_) | copy-start | bytes 2506756
  62.6 34.8 %all-to-all-start.1 = ((bf16[8,96,256]{2,1,0:T(8,128)(2,1)}), bf16[8,96,256]{2,1,0:T(8,128)(2,1)S(1)}, u32[]{:S(2)}, u32[]{:S(2)}) async-start(bf16[8,96,256]{2,1,0:T(8,128)(2,1)} %broadcast_in_dim.15), calls=%async_computation.1 | async-start | bytes 786432 | tf_op jit(solution)/shard_map/all_to_all | solution.py:382
  77.9 34.8 %collective-permute-start.2 = (bf16[8,3,128,128]{3,2,1,0:T(8,128)(2,1)}, bf16[8,3,128,128]{3,2,1,0:T(8,128)(2,1)S(1)}, u32[]{:S(2)}, u32[]{:S(2)}) collective-permute-start(bf16[8,3,128,128]{3,2,1,0:T(8,128)(2,1)} %shard_map.122), channel_id=1, source_target_pairs={{0,0},{1,1},{2,2},{3,3},{4,8},{5,9},{6,10},{7,11},{8,4},{9,5},{10,... | collective-permute-start | bytes 2359304 | tf_op jit(solution)/shard_map/ppermute | solution.py:32
  87.2 27.5 %collective-permute-start.3 = (bf16[12,128,256]{2,1,0:T(8,128)(2,1)S(1)}, bf16[12,128,256]{2,1,0:T(8,128)(2,1)S(1)}, u32[]{:S(2)}, u32[]{:S(2)}) collective-permute-start(bf16[12,128,256]{2,1,0:T(8,128)(2,1)S(1)} %bitcast.44), channel_id=1, source_target_pairs={{0,1},{1,2},{2,3},{3,0},{4,5},{5,6},{6,7},{7,4},{8,9},{9,10},{10,1... | collective-permute-start | bytes 2359304 | tf_op jit(solution)/shard_map/ppermute | solution.py:32
  90.4 26.7 %collective-permute-start.4 = (bf16[12,128,256]{2,1,0:T(8,128)(2,1)S(1)}, bf16[12,128,256]{2,1,0:T(8,128)(2,1)S(1)}, u32[]{:S(2)}, u32[]{:S(2)}) collective-permute-start(bf16[12,128,256]{2,1,0:T(8,128)(2,1)S(1)} %bitcast.45), channel_id=1, source_target_pairs={{0,3},{1,0},{2,1},{3,2},{4,7},{5,4},{6,5},{7,6},{8,11},{9,8},{10,9... | collective-permute-start | bytes 2359304 | tf_op jit(solution)/shard_map/ppermute | solution.py:32
  93.8 25.3 %collective-permute-start.5 = (bf16[12,128,256]{2,1,0:T(8,128)(2,1)S(1)}, bf16[12,128,256]{2,1,0:T(8,128)(2,1)}, u32[]{:S(2)}, u32[]{:S(2)}) collective-permute-start(bf16[12,128,256]{2,1,0:T(8,128)(2,1)S(1)} %bitcast.46), channel_id=1, source_target_pairs={{0,2},{1,3},{2,0},{3,1},{4,6},{5,7},{6,4},{7,5},{8,10},{9,11},{10,... | collective-permute-start | bytes 2359304 | tf_op jit(solution)/shard_map/ppermute | solution.py:32
  97.3 10.1 %collective-permute-start.10 = (bf16[8,96,256]{2,1,0:T(8,128)(2,1)S(1)}, bf16[8,96,256]{2,1,0:T(8,128)(2,1)}, u32[]{:S(2)}, u32[]{:S(2)}) collective-permute-start(bf16[8,96,256]{2,1,0:T(8,128)(2,1)S(1)} %all-to-all-done.1), channel_id=1, source_target_pairs={{0,32},{1,33},{2,34},{3,35},{4,36},{5,37},{6,38},{7,39},{8,40},{9,... | collective-permute-start | bytes 1179656 | tf_op jit(solution)/shard_map/ppermute | solution.py:32
  107.5 17.6 %copy-start.14 = (f32[128]{0:T(128)S(1)}, f32[128]{0:T(128)}, u32[]{:S(2)}) copy-start(f32[128]{0:T(128)} %param.14) | copy-start | bytes 1540
  107.5 17.6 %copy-start.15 = (f32[128]{0:T(128)S(1)}, f32[128]{0:T(128)}, u32[]{:S(2)}) copy-start(f32[128]{0:T(128)} %param.13) | copy-start | bytes 1540
  109.6 16.9 %collective-permute-start.11 = (bf16[8,2,96,256]{3,2,1,0:T(8,128)(2,1)}, bf16[8,2,96,256]{3,2,1,0:T(8,128)(2,1)}, u32[]{:S(2)}, u32[]{:S(2)}) collective-permute-start(bf16[8,2,96,256]{3,2,1,0:T(8,128)(2,1)} %maximum_select_fusion.1), channel_id=1, source_target_pairs={{0,16},{1,17},{2,18},{3,19},{4,20},{5,21},{6,22},{7,23},{8,24},{9,... | collective-permute-start | bytes 2359304 | tf_op jit(solution)/shard_map/ppermute | solution.py:32
  112.7 8.8 %copy-start.9 = (bf16[8,3,128,128]{3,2,1,0:T(8,128)(2,1)}, bf16[8,3,128,128]{3,2,1,0:T(8,128)(2,1)S(1)}, u32[]{:S(2)}) copy-start(bf16[8,3,128,128]{3,2,1,0:T(8,128)(2,1)S(1)} %collective-permute-done.2.refs_1_) | copy-start | bytes 2359300
  112.7 26.0 %collective-permute-start.6 = (bf16[12,128,256]{2,1,0:T(8,128)(2,1)S(1)}, bf16[12,128,256]{2,1,0:T(8,128)(2,1)}, u32[]{:S(2)}, u32[]{:S(2)}) collective-permute-start(bf16[12,128,256]{2,1,0:T(8,128)(2,1)S(1)} %bitcast.47), channel_id=1, source_target_pairs={{0,8},{1,9},{2,10},{3,11},{4,12},{5,13},{6,14},{7,15},{8,0},{9,1},... | collective-permute-start | bytes 2359304 | tf_op jit(solution)/shard_map/ppermute | solution.py:32
  114.7 24.1 %collective-permute-start.7 = (bf16[12,128,256]{2,1,0:T(8,128)(2,1)S(1)}, bf16[12,128,256]{2,1,0:T(8,128)(2,1)}, u32[]{:S(2)}, u32[]{:S(2)}) collective-permute-start(bf16[12,128,256]{2,1,0:T(8,128)(2,1)S(1)} %collective-permute-done.3.refs_1_), channel_id=1, source_target_pairs={{0,8},{1,9},{2,10},{3,11},{4,12},{5,13},{6,14},{7,15},{8,0},{9,1},... | collective-permute-start | bytes 2359304 | tf_op jit(solution)/shard_map/ppermute | solution.py:32
  117.1 21.7 %collective-permute-start.8 = (bf16[12,128,256]{2,1,0:T(8,128)(2,1)S(1)}, bf16[12,128,256]{2,1,0:T(8,128)(2,1)}, u32[]{:S(2)}, u32[]{:S(2)}) collective-permute-start(bf16[12,128,256]{2,1,0:T(8,128)(2,1)S(1)} %collective-permute-done.4.refs_2_), channel_id=1, source_target_pairs={{0,8},{1,9},{2,10},{3,11},{4,12},{5,13},{6,14},{7,15},{8,0},{9,1},... | collective-permute-start | bytes 2359304 | tf_op jit(solution)/shard_map/ppermute | solution.py:32
  119.0 19.7 %collective-permute-start.9 = (bf16[12,128,256]{2,1,0:T(8,128)(2,1)}, bf16[12,128,256]{2,1,0:T(8,128)(2,1)}, u32[]{:S(2)}, u32[]{:S(2)}) collective-permute-start(bf16[12,128,256]{2,1,0:T(8,128)(2,1)} %collective-permute-done.5.refs_3_), channel_id=1, source_target_pairs={{0,8},{1,9},{2,10},{3,11},{4,12},{5,13},{6,14},{7,15},{8,0},{9,1},... | collective-permute-start | bytes 2359304 | tf_op jit(solution)/shard_map/ppermute | solution.py:32
  121.6 16.3 %all-to-all-start = ((bf16[8,3,128,128]{3,2,1,0:T(8,128)(2,1)}), bf16[8,3,128,128]{3,2,1,0:T(8,128)(2,1)S(1)}, u32[]{:S(2)}, u32[]{:S(2)}) async-start(bf16[8,3,128,128]{3,2,1,0:T(8,128)(2,1)} %copy-done.9), calls=%async_computation | async-start | bytes 1572864 | tf_op jit(solution)/shard_map/all_to_all | solution.py:419
  126.5 30.4 %collective-permute-start.13 = (bf16[8,3,128,128]{3,2,1,0:T(8,128)(2,1)}, bf16[8,3,128,128]{3,2,1,0:T(8,128)(2,1)}, u32[]{:S(2)}, u32[]{:S(2)}) collective-permute-start(bf16[8,3,128,128]{3,2,1,0:T(8,128)(2,1)} %shard_map.127), channel_id=1, source_target_pairs={{0,0},{1,1},{2,2},{3,3},{4,8},{5,9},{6,10},{7,11},{8,4},{9,5},{10,... | collective-permute-start | bytes 2359304 | tf_op jit(solution)/shard_map/ppermute | solution.py:32
  137.8 0.9 copy-start.3
  138.8 1.4 copy-start.2
  140.2 4.7 %copy-start.4 = (bf16[8,3,128,128]{3,2,1,0:T(8,128)(2,1)S(1)}, bf16[8,3,128,128]{3,2,1,0:T(8,128)(2,1)}, u32[]{:S(2)}) copy-start(bf16[8,3,128,128]{3,2,1,0:T(8,128)(2,1)} %copy-done.3) | copy-start | bytes 2359300
  151.2 0.9 copy-start.6
  152.1 17.1 %all-to-all-start.2 = ((bf16[8,384,128]{2,1,0:T(8,128)(2,1)}), bf16[8,384,128]{2,1,0:T(8,128)(2,1)}, u32[]{:S(2)}, u32[]{:S(2)}) async-start(bf16[8,384,128]{2,1,0:T(8,128)(2,1)} %copy-done.6), calls=%async_computation.2 | async-start | bytes 1572864 | tf_op jit(solution)/shard_map/all_to_all | solution.py:422
  169.2 16.8 %all-to-all-start.3 = ((bf16[8,3,128,128]{3,2,1,0:T(8,128)(2,1)}), bf16[8,3,128,128]{3,2,1,0:T(8,128)(2,1)}, u32[]{:S(2)}, u32[]{:S(2)}) async-start(bf16[8,3,128,128]{3,2,1,0:T(8,128)(2,1)} %shard_map.128), calls=%async_computation.3 | async-start | bytes 1572864 | tf_op jit(solution)/shard_map/all_to_all | solution.py:423
  173.7 41.1 %collective-permute-start.12 = (bf16[8,384,128]{2,1,0:T(8,128)(2,1)}, bf16[8,384,128]{2,1,0:T(8,128)(2,1)}, u32[]{:S(2)}, u32[]{:S(2)}) collective-permute-start(bf16[8,384,128]{2,1,0:T(8,128)(2,1)} %all-to-all-done.2.refs_1_), channel_id=1, source_target_pairs={{0,0},{1,1},{2,2},{3,3},{4,8},{5,9},{6,10},{7,11},{8,4},{9,5},{10,... | collective-permute-start | bytes 2359304 | tf_op jit(solution)/shard_map/ppermute | solution.py:32
  193.5 0.9 copy-start.5
  202.7 16.8 %all-to-all-start.4 = ((bf16[8,384,128]{2,1,0:T(8,128)(2,1)}), bf16[8,384,128]{2,1,0:T(8,128)(2,1)}, u32[]{:S(2)}, u32[]{:S(2)}) async-start(bf16[8,384,128]{2,1,0:T(8,128)(2,1)} %copy-done.5), calls=%async_computation.4 | async-start | bytes 1572864 | tf_op jit(solution)/shard_map/all_to_all | solution.py:429
  212.2 1.2 copy-start
  214.8 12.5 %copy-start.1 = (bf16[4,8,208,128]{3,2,1,0:T(8,128)(2,1)S(1)}, bf16[4,8,208,128]{3,2,1,0:T(8,128)(2,1)}, u32[]{:S(2)}) copy-start(bf16[4,8,208,128]{3,2,1,0:T(8,128)(2,1)} %shard_map.132.refs_1_) | copy-start | bytes 5111812
  219.5 36.1 %collective-permute-start.14 = (bf16[8,384,128]{2,1,0:T(8,128)(2,1)}, bf16[8,384,128]{2,1,0:T(8,128)(2,1)S(1)}, u32[]{:S(2)}, u32[]{:S(2)}) collective-permute-start(bf16[8,384,128]{2,1,0:T(8,128)(2,1)} %shard_map.133), channel_id=1, source_target_pairs={{0,0},{1,1},{2,2},{3,3},{4,8},{5,9},{6,10},{7,11},{8,4},{9,5},{10,... | collective-permute-start | bytes 2359304 | tf_op jit(solution)/shard_map/ppermute | solution.py:32
  228.2 13.0 %collective-permute-start.15 = (bf16[8,208,128]{2,1,0:T(8,128)(2,1)S(1)}, bf16[8,208,128]{2,1,0:T(8,128)(2,1)S(1)}, u32[]{:S(2)}, u32[]{:S(2)}) collective-permute-start(bf16[8,208,128]{2,1,0:T(8,128)(2,1)S(1)} %get-tuple-element.29), channel_id=1, source_target_pairs={{0,16},{1,17},{2,18},{3,19},{4,20},{5,21},{6,22},{7,23},{8,24},{9,... | collective-permute-start | bytes 1277960 | tf_op jit(solution)/shard_map/ppermute | solution.py:32
  230.4 16.8 %collective-permute-start.16 = (bf16[8,208,128]{2,1,0:T(8,128)(2,1)S(1)}, bf16[8,208,128]{2,1,0:T(8,128)(2,1)S(1)}, u32[]{:S(2)}, u32[]{:S(2)}) collective-permute-start(bf16[8,208,128]{2,1,0:T(8,128)(2,1)S(1)} %get-tuple-element.28), channel_id=1, source_target_pairs={{0,32},{1,33},{2,34},{3,35},{4,36},{5,37},{6,38},{7,39},{8,40},{9,... | collective-permute-start | bytes 1277960 | tf_op jit(solution)/shard_map/ppermute | solution.py:32
  235.1 17.4 %collective-permute-start.17 = (bf16[8,208,128]{2,1,0:T(8,128)(2,1)S(1)}, bf16[8,208,128]{2,1,0:T(8,128)(2,1)S(1)}, u32[]{:S(2)}, u32[]{:S(2)}) collective-permute-start(bf16[8,208,128]{2,1,0:T(8,128)(2,1)S(1)} %get-tuple-element.27), channel_id=1, source_target_pairs={{0,48},{1,49},{2,50},{3,51},{4,52},{5,53},{6,54},{7,55},{8,56},{9,... | collective-permute-start | bytes 1277960 | tf_op jit(solution)/shard_map/ppermute | solution.py:32
  241.3 11.2 %copy-start.10 = (bf16[8,208,128]{2,1,0:T(8,128)(2,1)}, bf16[8,208,128]{2,1,0:T(8,128)(2,1)S(1)}, u32[]{:S(2)}) copy-start(bf16[8,208,128]{2,1,0:T(8,128)(2,1)S(1)} %collective-permute-done.15.refs_1_) | copy-start | bytes 1277956
  247.2 5.3 %copy-start.11 = (bf16[8,208,128]{2,1,0:T(8,128)(2,1)}, bf16[8,208,128]{2,1,0:T(8,128)(2,1)S(1)}, u32[]{:S(2)}) copy-start(bf16[8,208,128]{2,1,0:T(8,128)(2,1)S(1)} %collective-permute-done.16.refs_2_) | copy-start | bytes 1277956
  252.5 0.8 copy-start.12
  255.6 0.9 copy-start.8
  306.1 3.4 %collective-permute-start.18 = (f32[2,56,256]{2,1,0:T(8,128)}, f32[2,56,256]{2,1,0:T(8,128)S(1)}, u32[]{:S(2)}, u32[]{:S(2)}) collective-permute-start(f32[2,56,256]{2,1,0:T(8,128)} %shard_map.137), channel_id=1, source_target_pairs={{4,0},{5,1},{6,2},{7,3},{8,12},{9,13},{10,14},{11,15},{20,16},{21,... | collective-permute-start | bytes 344072 | tf_op jit(solution)/shard_map/ppermute | solution.py:38
  310.4 15.3 %collective-permute-start.19 = (f32[56,256]{1,0:T(8,128)S(1)}, f32[56,256]{1,0:T(8,128)S(1)}, u32[]{:S(2)}, u32[]{:S(2)}) collective-permute-start(f32[56,256]{1,0:T(8,128)S(1)} %select_bitcast_fusion), channel_id=1, source_target_pairs={{0,8},{1,9},{2,10},{3,11},{4,12},{5,13},{6,14},{7,15},{8,0},{9,1},... | collective-permute-start | bytes 172040 | tf_op jit(solution)/shard_map/ppermute | solution.py:32
